TPU v7x, 256 devices: a whole 4x4x8 slice. The times are simulated.
256 devices in a mesh: gx: 8 (over x, core), gy: 32 (over y, z).
Axes of the slice: x: 4, y: 4, z: 8, core: 2. Of those that a mesh axis runs over, the one named last changes fastest.
Arguments:
- air_now: float32 [128, 1024, 512], P('gx', 'gy'), may hold values from -6 to 6
- air_prev: float32 [128, 1024, 512], P('gx', 'gy'), may hold values from -6 to 6
- membrane_now: float32 [128, 1024], P('gx', 'gy'), may hold values from -5.3 to 5.3
- membrane_prev: float32 [128, 1024], P('gx', 'gy'), may hold values from -5.3 to 5.3
- inv_mass: float32 [128, 1024], P('gx', 'gy'), may hold values from 0.5 to 2
- air_row: int32 [1024], replicated, may hold values from 720 to 975, as said below
Outputs:
- air_next: float32 [128, 1024, 512], P('gx', 'gy')
- air_last: float32 [128, 1024, 512], P('gx', 'gy')
- membrane_next: float32 [128, 1024], P('gx', 'gy')
- membrane_last: float32 [128, 1024], P('gx', 'gy')
Inputs may be any that keep to these rules, and one draw needn't show every extreme that they name: `air_row`: nondecreasing over the membrane's columns and rising by 0 or 1 from one column to the next, so every air y row from 720 to 975 lies under some column.
All inputs are finite; a program needn't handle non-finite values.
Results may differ from a plain program's by a relative error of at most 0.0003.
Values sent between devices are 32-bit elements; how exact they have to be, the bound alone decides.
No kernel may reach another device: no remote copies, remote signals or barrier semaphores. Data moves between devices by JAX's collectives and lax.ppermute only.
A program may use at most 128 MiB of HBM per device.

v0:
```python
import jax
import jax.numpy as jnp
from jax import lax
from jax.sharding import PartitionSpec as P

STEPS = 4


courant_square = 0.32
membrane_speed = 0.08
berger_gain = 0.4
force_gain = 0.1
source_gain = 0.5


def extended(block, sides, width):
    for axis, dim in sides:
        count = lax.axis_size(axis)
        forward = [(i, i + 1) for i in range(count - 1)]
        backward = [(target, source) for source, target in forward]
        low = lax.ppermute(
            lax.slice_in_dim(block, block.shape[dim] - width, None, axis=dim), axis, forward
        )
        high = lax.ppermute(lax.slice_in_dim(block, 0, width, axis=dim), axis, backward)
        block = jnp.concatenate([low, block, high], axis=dim)
    return block


def exact_dot(left, right):
    return jnp.dot(left, right, precision=lax.Precision.HIGHEST, preferred_element_type=jnp.float32)


def air_update(padded_xy, older, source):
    middle = padded_xy.shape[2] // 2
    padded = jnp.pad(padded_xy, ((0, 0), (0, 0), (1, 1)))
    center = padded_xy[1:-1, 1:-1]
    beside = padded[2:, 1:-1, 1:-1] + padded[:-2, 1:-1, 1:-1]
    beside = beside + padded[1:-1, 2:, 1:-1] + padded[1:-1, :-2, 1:-1]
    beside = beside + padded[1:-1, 1:-1, 2:] + padded[1:-1, 1:-1, :-2]
    air_step = 2.0 * center - older + courant_square * (beside - 6.0 * center)
    air_step = air_step.at[:, :, middle].add(source_gain * source)
    air_step = air_step.at[:, :, middle - 1].add(-source_gain * source)
    return air_step


def per_device(air_now, air_prev, membrane_now, membrane_prev, inv_mass, air_row):
    brick_x, brick_y, layers = air_now.shape
    band_cols = membrane_now.shape[1]
    middle = layers // 2
    position = lax.axis_index("gy")
    own_rows = lax.dynamic_slice_in_dim(air_row, position * band_cols, band_cols)
    air_width = brick_y * lax.axis_size("gy")
    node_total = brick_x * lax.axis_size("gx") * band_cols * lax.axis_size("gy")
    pressure, pressure_old = (air_now, air_prev)
    shape_now, shape_old = (membrane_now, membrane_prev)
    for moment in range(STEPS):
        edged = extended(shape_now, (("gx", 0), ("gy", 1)), 1)
        curvature = (
            edged[2:, 1:-1]
            + edged[:-2, 1:-1]
            + edged[1:-1, 2:]
            + edged[1:-1, :-2]
            - 4.0 * shape_now
        )
        energy = -jnp.sum(shape_now * curvature)
        pressure_jump = pressure[:, :, middle - 1] - pressure[:, :, middle]
        portion = lax.all_gather(pressure_jump, "gy", axis=1, tiled=True)
        width = portion.shape[1]
        chooser = (own_rows[None, :] == jnp.arange(width, dtype=jnp.int32)[:, None]).astype(
            jnp.float32
        )
        forcing = exact_dot(portion, chooser)
        summed = lax.psum(energy, ("gx", "gy"))
        tension = 1.0 + berger_gain * summed / node_total
        acceleration = inv_mass * (membrane_speed * tension * curvature + force_gain * forcing)
        shape_next = 2.0 * shape_now - shape_old + acceleration
        chooser_full = (
            own_rows[:, None] == jnp.arange(air_width, dtype=jnp.int32)[None, :]
        ).astype(jnp.float32)
        source = lax.psum_scatter(
            exact_dot(acceleration, chooser_full), "gy", scatter_dimension=1, tiled=True
        )
        shape_next, source = (shape_next, source)
        padded_xy = extended(pressure, (("gx", 0), ("gy", 1)), 1)
        air_step = air_update(padded_xy, pressure_old, source)
        pressure_old, pressure = (pressure, air_step)
        shape_old, shape_now = (shape_now, shape_next)
    return (pressure, pressure_old, shape_now, shape_old)


def solution(mesh):
    in_specs = (
        P("gx", "gy", None),
        P("gx", "gy", None),
        P("gx", "gy"),
        P("gx", "gy"),
        P("gx", "gy"),
        P(),
    )
    out_specs = (P("gx", "gy", None), P("gx", "gy", None), P("gx", "gy"), P("gx", "gy"))
    return jax.shard_map(
        per_device, mesh=mesh, in_specs=in_specs, out_specs=out_specs, check_vma=False
    )
```

profile of v0, /device:TPU:1, one launch (start us, length us, event | category | flops | bytes accessed | tf_op | source)
XLA Modules:
  0.0 1294.6 jit_solution(14548207254331995663)
XLA Ops:
  8.3 4.5 collective-permute-start.1
  17.3 3.6 collective-permute-start.5
  21.0 4.6 copy.87
  25.8 3.7 copy.88
  30.0 41.5 %all-gather = f32[16,1024,1]{0,2,1:T(1,128)S(1)} all-gather(f32[16,32,1]{0,2,1:T(1,128)S(1)} %sub.75), channel_id=2, replica_groups=mesh['gx'=8,'gy'=32] {'gy'}, dimensions={1}, use_global_device_ids=true | all-gather | bytes 67584 | tf_op jit(solution)/shard_map/all_gather | solution.py:67
  72.9 4.0 collective-permute-start.7
  79.8 88.3 %psum.28 = f32[]{:T(128)} all-reduce(f32[]{:T(128)S(6)} %neg.12), channel_id=1, replica_groups=mesh['gx'=8,'gy'=32] {'gx','gy'}, use_global_device_ids=true, to_apply=%region_1.0 | all-reduce | flops 1 | bytes 8 | tf_op jit(solution)/shard_map/psum | solution.py:73
  177.9 4.3 collective-permute-start.15
  185.5 4.0 collective-permute-start.3
  190.9 79.5 %psum.29 = f32[]{:T(128)} all-reduce(f32[]{:T(128)S(6)} %neg.13), channel_id=1, replica_groups=mesh['gx'=8,'gy'=32] {'gx','gy'}, use_global_device_ids=true, to_apply=%region_4.5 | all-reduce | flops 1 | bytes 8 | tf_op jit(solution)/shard_map/psum | solution.py:73
  271.1 4.6 copy.130
  275.7 3.7 copy.131
  280.7 4.6 copy.132
  285.3 3.7 copy.133
  289.3 4.4 copy.93
  293.6 15.5 %fusion.4 = f32[16,32,512]{1,0,2:T(8,128)} fusion(f32[18,34,512]{1,0,2:T(8,128)} %copy.93, f32[16,32,512]{1,0,2:T(8,128)} %copy.87, f32[16,32,512]{1,0,2:T(8,128)} %copy.133, f32[16,32,512]{1,0,2:T(8,128)} %copy.132, f32[16,32,512]{1,0,2:T(8,128)} %copy.130, f32[16,32,512]{1,0,2:T(8,128)} %copy.131, f32[16,32,512]{1,0,2:T(8,128)} %copy.88), kind=kLoop, calls=%fused_computation.12 | loop fusion | flops 2883584 | bytes 8593408 | tf_op jit(solution)/shard_map/add | solution.py:40
  309.1 90.2 %reduce-scatter.13.cloned.1.call-done = f32[32,16]{1,0:T(8,128)} async-done(((f32[1024,16]{1,0:T(8,128)}), f32[32,16]{1,0:T(8,128)}) %reduce-scatter.13.cloned.1.call-update) | async-done | bytes 2064
  408.9 35.7 %all-gather.1 = f32[16,1024,1]{0,2,1:T(1,128)S(1)} all-gather(f32[16,32,1]{0,2,1:T(1,128)S(1)} %copy.105), channel_id=3, replica_groups=mesh['gx'=8,'gy'=32] {'gy'}, dimensions={1}, use_global_device_ids=true | all-gather | bytes 67584 | tf_op jit(solution)/shard_map/all_gather | solution.py:67
  445.2 20.2 %collective-permute-start.20 = (f32[1,32]{1,0:T(1,128)S(1)}, f32[1,32]{1,0:T(1,128)S(1)}, u32[]{:S(2)}, u32[]{:S(2)}) collective-permute-start(f32[1,32]{1,0:T(1,128)S(1)} %get-tuple-element.164), channel_id=1, source_target_pairs={{32,0},{64,32},{96,64},{128,96},{160,128},{192,160},{224,192},{33,... | collective-permute-start | bytes 392 | tf_op jit(solution)/shard_map/ppermute | solution.py:24
  465.5 3.0 collective-permute-start.21
  471.9 3.6 collective-permute-start.9
  476.9 4.0 collective-permute-start.23
  482.5 4.6 collective-permute-start.11
  489.1 78.0 %psum.30 = f32[]{:T(128)} all-reduce(f32[]{:T(128)S(6)} %neg.14), channel_id=1, replica_groups=mesh['gx'=8,'gy'=32] {'gx','gy'}, use_global_device_ids=true, to_apply=%region_7.8 | all-reduce | flops 1 | bytes 8 | tf_op jit(solution)/shard_map/psum | solution.py:73
  569.5 3.7 copy.136
  573.3 3.7 copy.137
  578.0 4.4 copy.104
  582.4 16.6 %fusion.9 = f32[16,32,512]{1,0,2:T(8,128)} fusion(f32[18,34,512]{1,0,2:T(8,128)} %copy.104, f32[16,32,512]{1,0,2:T(8,128)} %copy.137, f32[16,32,512]{1,0,2:T(8,128)} %copy.136, f32[16,32,512]{1,0,2:T(8,128)} %copy-done, f32[1,32,512]{1,0,2:T(1,128)S(1)} %copy-done.9, f32[1,32,512]{1,0,2:T(1,128)S(1)} %collective-permute-done.8, f32[16,32,512]{1,0,2:T(8,128)} %copy.87), kind=kLoop, calls=%fused_computation.17 | loop fusion | flops 3407872 | bytes 6627328 | tf_op jit(solution)/shard_map/add | solution.py:40
  599.0 97.2 %reduce-scatter.15.cloned.1.call-done = f32[32,16]{1,0:T(8,128)} async-done(((f32[1024,16]{1,0:T(8,128)}), f32[32,16]{1,0:T(8,128)}) %reduce-scatter.15.cloned.1.call-update) | async-done | bytes 2064
  708.7 35.8 %all-gather.2 = f32[16,1024,1]{0,2,1:T(1,128)S(1)} all-gather(f32[16,32,1]{0,2,1:T(1,128)S(1)} %copy.112), channel_id=4, replica_groups=mesh['gx'=8,'gy'=32] {'gy'}, dimensions={1}, use_global_device_ids=true | all-gather | bytes 67584 | tf_op jit(solution)/shard_map/all_gather | solution.py:67
  745.1 20.2 %collective-permute-start.28 = (f32[1,32]{1,0:T(1,128)S(1)}, f32[1,32]{1,0:T(1,128)S(1)}, u32[]{:S(2)}, u32[]{:S(2)}) collective-permute-start(f32[1,32]{1,0:T(1,128)S(1)} %get-tuple-element.162), channel_id=1, source_target_pairs={{32,0},{64,32},{96,64},{128,96},{160,128},{192,160},{224,192},{33,... | collective-permute-start | bytes 392 | tf_op jit(solution)/shard_map/ppermute | solution.py:24
  775.5 4.0 collective-permute-start.31
  781.3 4.6 collective-permute-start.19
  787.9 79.0 %psum.31 = f32[]{:T(128)} all-reduce(f32[]{:T(128)S(6)} %neg.15), channel_id=1, replica_groups=mesh['gx'=8,'gy'=32] {'gx','gy'}, use_global_device_ids=true, to_apply=%region_10.11 | all-reduce | flops 1 | bytes 8 | tf_op jit(solution)/shard_map/psum | solution.py:73
  869.3 3.7 copy.138
  873.0 3.7 copy.139
  877.8 4.4 copy.111
  882.1 16.9 %fusion.14 = f32[16,32,512]{1,0,2:T(8,128)} fusion(f32[18,34,512]{1,0,2:T(8,128)} %copy.111, f32[16,32,512]{1,0,2:T(8,128)} %copy.139, f32[16,32,512]{1,0,2:T(8,128)} %copy.138, f32[16,32,512]{1,0,2:T(8,128)} %copy-done.1, f32[1,32,512]{1,0,2:T(1,128)S(1)} %collective-permute-done.17, f32[1,32,512]{1,0,2:T(1,128)S(1)} %copy-done.7, f32[16,32,512]{1,0,2:T(8,128)} %copy-done), kind=kLoop, calls=%fused_computation.22 | loop fusion | flops 3407872 | bytes 6627328 | tf_op jit(solution)/shard_map/add | solution.py:40
  899.0 97.5 %reduce-scatter.17.cloned.1.call-done = f32[32,16]{1,0:T(8,128)} async-done(((f32[1024,16]{1,0:T(8,128)}), f32[32,16]{1,0:T(8,128)}) %reduce-scatter.17.cloned.1.call-update) | async-done | bytes 2064
  1003.3 35.8 %all-gather.3 = f32[16,1024,1]{0,2,1:T(1,128)S(1)} all-gather(f32[16,32,1]{0,2,1:T(1,128)S(1)} %copy.119), channel_id=5, replica_groups=mesh['gx'=8,'gy'=32] {'gy'}, dimensions={1}, use_global_device_ids=true | all-gather | bytes 67584 | tf_op jit(solution)/shard_map/all_gather | solution.py:67
  1039.1 21.3 %collective-permute-start.25 = (f32[1,32,512]{1,0,2:T(1,128)S(1)}, f32[1,32,512]{1,0,2:T(1,128)S(1)}, u32[]{:S(2)}, u32[]{:S(2)}) collective-permute-start(f32[1,32,512]{1,0,2:T(1,128)S(1)} %get-tuple-element.124), channel_id=1, source_target_pairs={{0,32},{32,64},{64,96},{96,128},{128,160},{160,192},{192,224},{1,3... | collective-permute-start | bytes 196616 | tf_op jit(solution)/shard_map/ppermute | solution.py:21
  1069.5 4.8 collective-permute-start.27
  1077.5 3.7 copy.140
  1081.3 3.7 copy.141
  1086.0 4.4 copy.118
  1090.4 16.6 %fusion.19 = f32[16,32,512]{1,0,2:T(8,128)} fusion(f32[18,34,512]{1,0,2:T(8,128)} %copy.118, f32[16,32,512]{1,0,2:T(8,128)} %copy.141, f32[16,32,512]{1,0,2:T(8,128)} %copy.140, f32[16,32,512]{1,0,2:T(8,128)} %copy-done.2, f32[1,32,512]{1,0,2:T(1,128)S(1)} %collective-permute-done.25, f32[1,32,512]{1,0,2:T(1,128)S(1)} %copy-done.11, f32[16,32,512]{1,0,2:T(8,128)} %copy-done.1), kind=kLoop, calls=%fused_computation.27 | loop fusion | flops 3407872 | bytes 6627328 | tf_op jit(solution)/shard_map/add | solution.py:40
  1107.0 173.9 %reduce-scatter.19.cloned.1.call-done = f32[32,16]{1,0:T(8,128)} async-done(((f32[1024,16]{1,0:T(8,128)}), f32[32,16]{1,0:T(8,128)}) %reduce-scatter.19.cloned.1.call-update) | async-done | bytes 2064
  1284.3 3.6 copy.120
  (197 shorter events, 97.5 us)
Async XLA Ops:
  7.2 392.2 %reduce-scatter.13.cloned.1.call-start = ((), (), s32[]{:S(2)}) async-start(), calls=%async_computation.4 | async-start | bytes 540672
  8.3 173.9 %collective-permute-start.1 = (f32[1,32,512]{2,1,0:T(8,128)S(1)}, f32[1,32,512]{2,1,0:T(8,128)S(1)}, u32[]{:S(2)}, u32[]{:S(2)}) collective-permute-start(f32[1,32,512]{2,1,0:T(8,128)S(1)} %get-tuple-element.152), channel_id=1, source_target_pairs={{0,32},{32,64},{64,96},{96,128},{128,160},{160,192},{192,224},{1,3... | collective-permute-start | bytes 196616 | tf_op jit(solution)/shard_map/ppermute | solution.py:21
  12.8 169.4 %collective-permute-start = (f32[1,32,512]{2,1,0:T(8,128)S(1)}, f32[1,32,512]{2,1,0:T(8,128)S(1)}, u32[]{:S(2)}, u32[]{:S(2)}) collective-permute-start(f32[1,32,512]{2,1,0:T(8,128)S(1)} %get-tuple-element.151), channel_id=1, source_target_pairs={{32,0},{64,32},{96,64},{128,96},{160,128},{192,160},{224,192},{33,... | collective-permute-start | bytes 196616 | tf_op jit(solution)/shard_map/ppermute | solution.py:24
  15.4 56.1 %collective-permute-start.4 = (f32[1,32]{1,0:T(1,128)S(1)}, f32[1,32]{1,0:T(1,128)S(1)}, u32[]{:S(2)}, u32[]{:S(2)}) collective-permute-start(f32[1,32]{1,0:T(1,128)S(1)} %get-tuple-element.168), channel_id=1, source_target_pairs={{32,0},{64,32},{96,64},{128,96},{160,128},{192,160},{224,192},{33,... | collective-permute-start | bytes 392 | tf_op jit(solution)/shard_map/ppermute | solution.py:24
  17.3 54.2 %collective-permute-start.5 = (f32[1,32]{1,0:T(1,128)S(1)}, f32[1,32]{1,0:T(1,128)S(1)}, u32[]{:S(2)}, u32[]{:S(2)}) collective-permute-start(f32[1,32]{1,0:T(1,128)S(1)} %get-tuple-element.167), channel_id=1, source_target_pairs={{0,32},{32,64},{64,96},{96,128},{128,160},{160,192},{192,224},{1,3... | collective-permute-start | bytes 392 | tf_op jit(solution)/shard_map/ppermute | solution.py:21
  25.6 45.9 %copy-start.19 = (f32[16,32]{1,0:T(8,128)S(1)}, f32[16,32]{1,0:T(8,128)}, u32[]{:S(2)}) copy-start(f32[16,32]{1,0:T(8,128)} %param.24) | copy-start | bytes 6148
  25.6 143.2 %copy-start.22 = (f32[16,32]{1,0:T(8,128)S(1)}, f32[16,32]{1,0:T(8,128)}, u32[]{:S(2)}) copy-start(f32[16,32]{1,0:T(8,128)} %param.26) | copy-start | bytes 6148
  25.6 143.2 %copy-start.30 = (f32[16,32]{1,0:T(8,128)S(1)}, f32[16,32]{1,0:T(8,128)}, u32[]{:S(2)}) copy-start(f32[16,32]{1,0:T(8,128)} %param.25) | copy-start | bytes 6148
  71.6 5.3 collective-permute-start.6
  72.9 4.8 collective-permute-start.7
  79.8 388.6 %copy-start.25 = (s32[32]{0:T(128)}, s32[32]{0:T(128)S(1)}, u32[]{:S(2)}) copy-start(s32[32]{0:T(128)S(1)} %dynamic_slice.3) | copy-start | bytes 388
  169.4 7.1 collective-permute-start.12
  172.0 4.5 collective-permute-start.13
  176.6 12.9 collective-permute-start.14
  177.9 11.6 collective-permute-start.15
  183.9 91.8 %copy-start.5 = (f32[16,32,512]{2,1,0:T(8,128)S(1)}, f32[16,32,512]{2,1,0:T(8,128)}, u32[]{:S(2)}) copy-start(f32[16,32,512]{2,1,0:T(8,128)} %get-tuple-element.148) | copy-start | bytes 3145732
  184.0 95.4 %collective-permute-start.2 = (f32[18,1,512]{2,1,0:T(1,128)S(1)}, f32[18,1,512]{2,1,0:T(1,128)S(1)}, u32[]{:S(2)}, u32[]{:S(2)}) collective-permute-start(f32[18,1,512]{2,1,0:T(1,128)S(1)} %get-tuple-element.145), channel_id=1, source_target_pairs={{1,0},{2,1},{3,2},{4,3},{5,4},{6,5},{7,6},{8,7},{9,8},{10,9},{11,1... | collective-permute-start | bytes 110600 | tf_op jit(solution)/shard_map/ppermute | solution.py:24
  185.5 93.9 %collective-permute-start.3 = (f32[18,1,512]{2,1,0:T(1,128)S(1)}, f32[18,1,512]{2,1,0:T(1,128)S(1)}, u32[]{:S(2)}, u32[]{:S(2)}) collective-permute-start(f32[18,1,512]{2,1,0:T(1,128)S(1)} %get-tuple-element.144), channel_id=1, source_target_pairs={{0,1},{1,2},{2,3},{3,4},{4,5},{5,6},{6,7},{7,8},{8,9},{9,10},{10,1... | collective-permute-start | bytes 110600 | tf_op jit(solution)/shard_map/ppermute | solution.py:21
  190.8 505.4 %reduce-scatter.15.cloned.1.call-start = ((), (), s32[]{:S(2)}) async-start(), calls=%async_computation.5 | async-start | bytes 540672
  445.2 30.3 %collective-permute-start.20 = (f32[1,32]{1,0:T(1,128)S(1)}, f32[1,32]{1,0:T(1,128)S(1)}, u32[]{:S(2)}, u32[]{:S(2)}) collective-permute-start(f32[1,32]{1,0:T(1,128)S(1)} %get-tuple-element.164), channel_id=1, source_target_pairs={{32,0},{64,32},{96,64},{128,96},{160,128},{192,160},{224,192},{33,... | collective-permute-start | bytes 392 | tf_op jit(solution)/shard_map/ppermute | solution.py:24
  465.5 10.1 collective-permute-start.21
  470.0 11.0 collective-permute-start.8
  471.9 9.2 collective-permute-start.9
  475.6 11.5 collective-permute-start.22
  476.9 10.2 collective-permute-start.23
  481.0 86.8 %copy-start.8 = (f32[1,32,512]{1,0,2:T(1,128)}, f32[1,32,512]{1,0,2:T(1,128)S(1)}, u32[]{:S(2)}) copy-start(f32[1,32,512]{1,0,2:T(1,128)S(1)} %collective-permute-done.9) | copy-start | bytes 196612
  481.2 86.6 %collective-permute-start.10 = (f32[18,1,512]{2,1,0:T(1,128)S(1)}, f32[18,1,512]{2,1,0:T(1,128)S(1)}, u32[]{:S(2)}, u32[]{:S(2)}) collective-permute-start(f32[18,1,512]{2,1,0:T(1,128)S(1)} %get-tuple-element.141), channel_id=1, source_target_pairs={{1,0},{2,1},{3,2},{4,3},{5,4},{6,5},{7,6},{8,7},{9,8},{10,9},{11,1... | collective-permute-start | bytes 110600 | tf_op jit(solution)/shard_map/ppermute | solution.py:24
  482.5 85.9 %collective-permute-start.11 = (f32[18,1,512]{2,1,0:T(1,128)S(1)}, f32[18,1,512]{2,1,0:T(1,128)}, u32[]{:S(2)}, u32[]{:S(2)}) collective-permute-start(f32[18,1,512]{2,1,0:T(1,128)S(1)} %get-tuple-element.140), channel_id=1, source_target_pairs={{0,1},{1,2},{2,3},{3,4},{4,5},{5,6},{6,7},{7,8},{8,9},{9,10},{10,1... | collective-permute-start | bytes 110600 | tf_op jit(solution)/shard_map/ppermute | solution.py:21
  489.1 507.5 %reduce-scatter.17.cloned.1.call-start = ((), (), s32[]{:S(2)}) async-start(), calls=%async_computation.6 | async-start | bytes 540672
  745.1 122.5 %copy-start.20 = (f32[16,32]{1,0:T(8,128)}, f32[16,32]{1,0:T(8,128)S(1)}, u32[]{:S(2)}) copy-start(f32[16,32]{1,0:T(8,128)S(1)} %get-tuple-element.173) | copy-start | bytes 6148
  745.1 29.0 %collective-permute-start.28 = (f32[1,32]{1,0:T(1,128)S(1)}, f32[1,32]{1,0:T(1,128)S(1)}, u32[]{:S(2)}, u32[]{:S(2)}) collective-permute-start(f32[1,32]{1,0:T(1,128)S(1)} %get-tuple-element.162), channel_id=1, source_target_pairs={{32,0},{64,32},{96,64},{128,96},{160,128},{192,160},{224,192},{33,... | collective-permute-start | bytes 392 | tf_op jit(solution)/shard_map/ppermute | solution.py:24
  765.3 8.8 collective-permute-start.29
  769.8 9.7 collective-permute-start.17
  772.2 7.7 collective-permute-start.16
  774.2 11.7 collective-permute-start.30
  775.5 10.4 collective-permute-start.31
  779.9 87.7 %copy-start.6 = (f32[1,32,512]{1,0,2:T(1,128)}, f32[1,32,512]{1,0,2:T(1,128)S(1)}, u32[]{:S(2)}) copy-start(f32[1,32,512]{1,0,2:T(1,128)S(1)} %collective-permute-done.16) | copy-start | bytes 196612
  780.0 87.5 %collective-permute-start.18 = (f32[18,1,512]{2,1,0:T(1,128)S(1)}, f32[18,1,512]{2,1,0:T(1,128)S(1)}, u32[]{:S(2)}, u32[]{:S(2)}) collective-permute-start(f32[18,1,512]{2,1,0:T(1,128)S(1)} %get-tuple-element.137), channel_id=1, source_target_pairs={{1,0},{2,1},{3,2},{4,3},{5,4},{6,5},{7,6},{8,7},{9,8},{10,9},{11,1... | collective-permute-start | bytes 110600 | tf_op jit(solution)/shard_map/ppermute | solution.py:24
  781.3 86.9 %collective-permute-start.19 = (f32[18,1,512]{2,1,0:T(1,128)S(1)}, f32[18,1,512]{2,1,0:T(1,128)}, u32[]{:S(2)}, u32[]{:S(2)}) collective-permute-start(f32[18,1,512]{2,1,0:T(1,128)S(1)} %get-tuple-element.136), channel_id=1, source_target_pairs={{0,1},{1,2},{2,3},{3,4},{4,5},{5,6},{6,7},{7,8},{8,9},{9,10},{10,1... | collective-permute-start | bytes 110600 | tf_op jit(solution)/shard_map/ppermute | solution.py:21
  787.9 493.0 %reduce-scatter.19.cloned.1.call-start = ((), (), s32[]{:S(2)}) async-start(), calls=%async_computation.7 | async-start | bytes 540672
  998.6 63.7 %copy-start.21 = (f32[16,32]{1,0:T(8,128)S(1)}, f32[16,32]{1,0:T(8,128)}, u32[]{:S(2)}) copy-start(f32[16,32]{1,0:T(8,128)} %copy-done.20) | copy-start | bytes 6148
  998.6 63.7 %copy-start.24 = (f32[16,32]{1,0:T(8,128)S(1)}, f32[16,32]{1,0:T(8,128)}, u32[]{:S(2)}) copy-start(f32[16,32]{1,0:T(8,128)} %param.26) | copy-start | bytes 6148
  998.6 63.7 %copy-start.27 = (s32[32]{0:T(128)S(1)}, s32[32]{0:T(128)}, u32[]{:S(2)}) copy-start(s32[32]{0:T(128)} %copy-done.25) | copy-start | bytes 388
  998.6 63.7 %copy-start.28 = (f32[16,32]{1,0:T(8,128)S(1)}, f32[16,32]{1,0:T(8,128)}, u32[]{:S(2)}) copy-start(f32[16,32]{1,0:T(8,128)} %get-tuple-element.117) | copy-start | bytes 6148
  1039.1 27.2 %collective-permute-start.25 = (f32[1,32,512]{1,0,2:T(1,128)S(1)}, f32[1,32,512]{1,0,2:T(1,128)S(1)}, u32[]{:S(2)}, u32[]{:S(2)}) collective-permute-start(f32[1,32,512]{1,0,2:T(1,128)S(1)} %get-tuple-element.124), channel_id=1, source_target_pairs={{0,32},{32,64},{64,96},{96,128},{128,160},{160,192},{192,224},{1,3... | collective-permute-start | bytes 196616 | tf_op jit(solution)/shard_map/ppermute | solution.py:21
  1060.4 7.7 collective-permute-start.24
  1068.2 7.6 collective-permute-start.26
  1069.5 6.9 collective-permute-start.27
  (19 other events, 227.7 us)
Sparse Core Ops, SparseCore 0:
  191.0 208.3 reduce-scatter.12
  489.2 206.9 reduce-scatter.14
  788.0 208.4 reduce-scatter.16
  1075.9 204.9 reduce-scatter.18
where the time goes:
time: 1310 us; the launch traced here: 1290 us
  blocking collectives  474 us (36%)
  waiting for transfers between devices  462 us (35%)
  starting transfers between devices  142 us (11%)
  local copies, waits for them, and re-layouts  101 us (8%)
  other arithmetic  88.1 us (7%)
  between operations  20 us (2%)
    unnamed x8, waiting for transfers between devices  459 us
    psum x4, blocking collectives, per_device(): summed = lax.psum(energy, ('gx', 'gy'))  325 us
    all_gather x4, blocking collectives, per_device(): portion = lax.all_gather(pressure_jump, 'gy', axis=1, tiled=True)  149 us
    ppermute x16, starting transfers between devices, extended(): lax.ppermute(lax.slice_in_dim(block, block.shape[dim] - width, None, axis...  78.7 us
    unnamed x85, local copies, waits for them, and re-layouts  67.7 us
    add x4, other arithmetic, air_update(): air_step = 2.0 * center - older + courant_square * (beside - 6.0 * center)  65.7 us
    ppermute x16, starting transfers between devices, extended(): lax.ppermute(lax.slice_in_dim(block, 0, width, axis=dim), axis, backward)  63 us
  transfers between devices with their start and end apart: 36, of which 7 were waited for; matrix products, arithmetic and copies ran while one was open for 12% of the time, Pallas kernels for 0%

commit v1 on v0

v1 whole, which is shorter than its diff:
```python
import functools

import jax
import jax.numpy as jnp
from jax import lax
from jax.experimental import pallas as pl
from jax.experimental.pallas import tpu as pltpu
from jax.sharding import PartitionSpec as P

COURANT = 0.32
SPEED = 0.08
BERGER = 0.4
FORCE = 0.1
SOURCE = 0.5

GX, GY = 8, 32
BX, BY, NZ = 16, 32, 512
MID = NZ // 2
COLS = GY * BY
NODES = GX * BX * COLS
HALO = 4
XE = BX + 2 * HALO
YE = BY + 16
WINDOW = 384
ROW0 = COLS - WINDOW
FIRST, LAST = 22, 30
PACK = 160
FOLD = 40

VMEM = pltpu.VMEM
WHOLE = pl.BlockSpec(memory_space=pltpu.VMEM)
ANY = pl.BlockSpec(memory_space=pl.ANY)
PARAMS = pltpu.CompilerParams(vmem_limit_bytes=40 * 1024 * 1024)


def f32(*shape):
    return jax.ShapeDtypeStruct(shape, jnp.float32)


def lanes(shape):
    return lax.broadcasted_iota(jnp.int32, shape, len(shape) - 1)


def sublanes(shape):
    return lax.broadcasted_iota(jnp.int32, shape, len(shape) - 2)


def pack_x_kernel(p, q, u, w, m, low, high, sems):
    copies = [
        pltpu.make_async_copy(p.at[0:4], low.at[0:4], sems.at[0]),
        pltpu.make_async_copy(q.at[0:3], low.at[4:7], sems.at[1]),
        pltpu.make_async_copy(p.at[12:16], high.at[0:4], sems.at[2]),
        pltpu.make_async_copy(q.at[13:16], high.at[4:7], sems.at[3]),
    ]
    for copy in copies:
        copy.start()
    for out, at in ((low, 0), (high, 12)):
        for i, field in enumerate((u, w, m)):
            out[7, 8 * i : 8 * i + 4, 0:BY] = field[at : at + 4, :]
    for copy in copies:
        copy.wait()


def pack_y_kernel(p, q, xlow, xhigh, low, high):
    tall = lax.axis_index("gx")
    lower = sublanes((8, NZ)) < 4

    def row(r, pt, qt, keep):
        a = jnp.where(lower, pt[0:8], pltpu.roll(qt[0:8], 4, 0))
        b = jnp.where(lower, pltpu.roll(qt[24:32], 4, 0), pt[24:32])
        if keep is not None:
            a = jnp.where(keep, a, 0.0)
            b = jnp.where(keep, b, 0.0)
        low[r] = a
        high[r] = b

    for r in range(BX):
        row(r + 4, p.at[r], q.at[r], None)
    keep_low = jnp.broadcast_to(tall, (8, NZ)) > 0
    keep_high = jnp.broadcast_to(tall, (8, NZ)) < GX - 1
    for i in range(4):
        row(i, xlow.at[i], xlow.at[4 + max(i - 1, 0)], keep_low)
        row(20 + i, xhigh.at[i], xhigh.at[4 + min(i, 2)], keep_high)


def air_kernel(p, q, xlow, xhigh, ylow, yhigh, u, w, m, out_next, out_last, block, a, b, jumps, rows, sems):
    tall = lax.axis_index("gx")
    wide = lax.axis_index("gy")
    copies = [
        pltpu.make_async_copy(p, a.at[4:20, 8:40], sems.at[0]),
        pltpu.make_async_copy(q, b.at[4:20, 8:40], sems.at[1]),
    ]
    for copy in copies:
        copy.start()
    first, last = tall == 0, tall == GX - 1
    bottom, top = wide == 0, wide == GY - 1

    def keep(shape, edge):
        return jnp.broadcast_to(edge.astype(jnp.int32), shape) == 0

    inner_low, inner_high = keep((BY, NZ), first), keep((BY, NZ), last)
    for i in range(4):
        a[i, 8:40] = jnp.where(inner_low, xlow[i], 0.0)
        a[20 + i, 8:40] = jnp.where(inner_high, xhigh[i], 0.0)
    b[0, 8:40] = jnp.zeros((BY, NZ), jnp.float32)
    b[23, 8:40] = jnp.zeros((BY, NZ), jnp.float32)
    for i in range(3):
        b[1 + i, 8:40] = jnp.where(inner_low, xlow[4 + i], 0.0)
        b[20 + i, 8:40] = jnp.where(inner_high, xhigh[4 + i], 0.0)
    tile_low, tile_high = keep((8, NZ), bottom), keep((8, NZ), top)
    for r in range(XE):
        lo = jnp.where(tile_low, ylow[r], 0.0)
        hi = jnp.where(tile_high, yhigh[r], 0.0)
        a[r, 0:8] = lo
        a[r, 40:48] = hi
        b[r, 0:8] = pltpu.roll(lo, 4, 0)
        b[r, 40:48] = pltpu.roll(hi, 4, 0)

    own = (u, w, m)
    narrow = keep((4, BY), first), keep((4, BY), last)
    for i in range(3):
        at = XE * i
        rows[at : at + 4, 0:BY] = jnp.where(narrow[0], xlow[7, 8 * i : 8 * i + 4, 0:BY], 0.0)
        rows[at + 4 : at + 20, 0:BY] = own[i][...]
        rows[at + 20 : at + 24, 0:BY] = jnp.where(narrow[1], xhigh[7, 8 * i : 8 * i + 4, 0:BY], 0.0)
    for copy in copies:
        copy.wait()

    lane = lanes((YE, NZ))
    at_low, at_high = lane == 0, lane == NZ - 1
    slot = lanes((BY, 128))
    start = jnp.where(first, 4, 0)
    stop = jnp.where(last, 20, 24)

    def stepped(now, old, r):
        c = now[r]
        z = jnp.where(at_low, 0.0, pltpu.roll(c, 1, 1)) + jnp.where(at_high, 0.0, pltpu.roll(c, NZ - 1, 1))
        y = pltpu.roll(c, 1, 0) + pltpu.roll(c, YE - 1, 0)
        x = now[r - 1] + now[r + 1]
        return (2.0 - 6.0 * COURANT) * c - old[r] + COURANT * (x + y + z)

    def jump(now, r, at, total):
        below = pltpu.roll(now[r, 8:40, MID - 128 : MID], at + 1, 1)
        above = pltpu.roll(now[r, 8:40, MID : MID + 128], at, 1)
        return jnp.where(slot == at, below - above, total)

    total = jnp.zeros((BY, 128), jnp.float32)
    for t in range(4):
        now, old = (a, b) if t % 2 == 0 else (b, a)
        shift = 24 * t if t < 3 else 68
        total = lax.fori_loop(t + 1, XE - 1 - t, lambda r, s: jump(now, r, r + shift, s), total)
        if t < 3:

            def advance(r, carry):
                new = stepped(now, old, r)
                old[r, 8:40] = new[8:40]
                old[r, 0:8] = jnp.where(tile_low, new[0:8], 0.0)
                old[r, 40:48] = jnp.where(tile_high, new[40:48], 0.0)
                return carry

            lax.fori_loop(jnp.maximum(t + 1, start), jnp.minimum(XE - 1 - t, stop), advance, 0)
        else:

            def finish(r, carry):
                out_next[r - 4] = stepped(now, old, r)[8:40]
                out_last[r - 4] = now[r, 8:40]
                return carry

            lax.fori_loop(4, 20, finish, 0)

    jumps[0:BY, :] = total
    jumps[BY:128, :] = jnp.zeros((128 - BY, 128), jnp.float32)
    rows[72:160, :] = jnp.transpose(jumps[...])[0:88]
    quarter = lanes((FOLD, 128)) // 32
    folded = rows[0:FOLD, :]
    for g in range(1, 4):
        folded = jnp.where(quarter == g, pltpu.roll(rows[FOLD * g : FOLD * (g + 1), :], 32 * g, 1), folded)
    folded = pltpu.roll(folded, 32 * lax.rem(wide, 4), 1)
    for i in range(GY):
        block[i] = folded


def split(x):
    high = x.astype(jnp.bfloat16)
    low = (x - high.astype(jnp.float32)).astype(jnp.bfloat16)
    return jnp.concatenate([high, low], axis=0)


def to_columns(x, chooser):
    n = x.shape[0]
    both = lax.dot_general(split(x), chooser, (((1,), (0,)), ((), ())), preferred_element_type=jnp.float32)
    return both[0:n] + both[n : 2 * n]


def to_rows(x, chooser):
    n = x.shape[0]
    both = lax.dot_general(split(x), chooser, (((1,), (1,)), ((), ())), preferred_element_type=jnp.float32)
    return both[0:n] + both[n : 2 * n]


def chooser_of(air_row):
    rows = lax.broadcasted_iota(jnp.int32, (WINDOW, COLS), 0) + ROW0
    return jnp.where(rows == air_row[...], 1.0, 0.0).astype(jnp.bfloat16)


def beside(field):
    n = field.shape[1]
    lane = lanes(field.shape)
    left = jnp.where(lane == 0, 0.0, pltpu.roll(field, 1, 1))
    right = jnp.where(lane == n - 1, 0.0, pltpu.roll(field, n - 1, 1))
    return left + right + pltpu.roll(field, 1, 0) + pltpu.roll(field, field.shape[0] - 1, 0)


def curve(field):
    return beside(field) - 4.0 * field


def inside(shape):
    tall = lax.axis_index("gx")
    row = sublanes(shape)
    low = jnp.where(tall == 0, 4, 0)
    high = jnp.where(tall == GX - 1, 20, 24)
    return (row >= low) & (row < high)


def membrane_kernel(blocks, air_row, sums, start, mono1, mono2, force2, force3, source0, source1, parts):
    quarter = lanes((FOLD, 128)) // 32
    for g in range(4):
        for t in range(8):
            if g == 3 and t < 5:
                continue
            merged = blocks[4 * t + (-g) % 4]
            for s in range(1, 4):
                merged = jnp.where(quarter == s, blocks[4 * t + (s - g) % 4], merged)
            parts[FOLD * g : FOLD * (g + 1), 128 * t : 128 * (t + 1)] = pltpu.roll(merged, (128 - 32 * g) % 128, 1)
    chooser = chooser_of(air_row)
    u0, w0, m0 = parts[0:24, :], parts[24:48, :], parts[48:72, :]
    start[0:24] = u0
    start[24:48] = m0
    free = to_columns(parts[72:160, ROW0:], chooser)
    force3[0:8] = jnp.zeros((8, COLS), jnp.float32)
    force3[8:24] = free[72:88]
    drive, stiff = FORCE * m0, SPEED * m0
    within = inside((XE, WINDOW))
    row = sublanes((XE, COLS))
    mine = (row >= HALO) & (row < HALO + BX)
    totals = []

    def gram(fields, curves):
        for i in range(len(fields)):
            for j in range(i, len(fields)):
                product = fields[i] * curves[j]
                part = product[:, 0:128]
                for k in range(1, COLS // 128):
                    part = part + product[:, 128 * k : 128 * (k + 1)]
                totals.append(jnp.sum(part, axis=0, keepdims=True))

    def masked(curves):
        return [jnp.where(mine, -c, 0.0) for c in curves]

    c0 = curve(u0)
    gram([u0], masked([c0]))
    a0 = [drive * free[0:24], stiff * c0]
    u1 = [2.0 * u0 - w0 + a0[0], a0[1]]
    mono1[0:24] = u1[0]
    mono1[24:48] = u1[1]
    c1 = [curve(x) for x in u1]
    gram(u1, masked(c1))
    s0 = to_rows(jnp.concatenate(a0, axis=0), chooser)
    source0[...] = s0
    f1 = to_columns(-s0, chooser)
    a1 = [drive * (free[24:48] + f1[0:24]), drive * f1[24:48], stiff * c1[0], stiff * c1[1]]
    u2 = [2.0 * u1[0] - u0 + a1[0], 2.0 * u1[1] + a1[1], a1[2], a1[3]]
    for i in range(4):
        mono2[24 * i : 24 * (i + 1)] = u2[i]
    c2 = [curve(x) for x in u2]
    gram(u2, masked(c2))
    s1 = to_rows(jnp.concatenate(a1, axis=0), chooser)
    source1[...] = s1
    jump2 = []
    for i in range(4):
        half = SOURCE * s1[24 * i : 24 * (i + 1)]
        if i < 2:
            g1 = SOURCE * s0[24 * i : 24 * (i + 1)]
            half = half + (2.0 - 7.0 * COURANT) * g1 + COURANT * jnp.where(within, beside(g1), 0.0)
        jump2.append(-2.0 * half)
    f2 = to_columns(jnp.concatenate(jump2, axis=0), chooser)
    f2 = [f2[24 * i : 24 * (i + 1)] for i in range(4)]
    f2[0] = f2[0] + free[48:72]
    for i in range(4):
        force2[24 * i : 24 * (i + 1)] = f2[i]
    u3 = [2.0 * u2[i] + drive * f2[i] for i in range(4)] + [stiff * c for c in c2]
    u3[0] = u3[0] - u1[0]
    u3[1] = u3[1] - u1[1]
    gram(u3, masked([curve(x) for x in u3]))

    count = len(totals)
    stack = jnp.concatenate(totals + [jnp.zeros((56 - count, 128), jnp.float32)], axis=0)
    column = jnp.sum(stack, axis=1, keepdims=True)
    diagonal = jnp.where(sublanes((56, 128)) == lanes((56, 128)), column, 0.0)
    sums[...] = jnp.sum(diagonal, axis=0, keepdims=True)


def quadratic(sums, at, monos):
    total = 0.0
    for i in range(len(monos)):
        for j in range(i, len(monos)):
            term = monos[i] * (sums[0, at] * monos[j])
            total = total + (term if i == j else 2.0 * term)
            at += 1
    return total


def finish_kernel(
    sums, air_row, start, mono1, mono2, force2, force3, source0, source1, next_in, last_in,
    out_next, out_last, out_u, out_w, plane_next, plane_last, fields, wide_rows, turned, sems,
):
    wide = lax.axis_index("gy")
    reached = (wide >= FIRST) & (wide <= LAST)
    loads = [
        pltpu.make_async_copy(next_in.at[:, :, MID - 128 : MID + 128], plane_next, sems.at[0]),
        pltpu.make_async_copy(last_in.at[:, :, MID - 128 : MID + 128], plane_last, sems.at[1]),
    ]

    @pl.when(reached)
    def _():
        for copy in loads:
            copy.start()

    def tension(energy):
        return 1.0 + BERGER * energy / NODES

    t0 = tension(sums[0, 0])
    t1 = tension(quadratic(sums, 1, [1.0, t0]))
    four = [1.0, t0, t1, t0 * t1]
    t2 = tension(quadratic(sums, 4, four))
    t3 = tension(quadratic(sums, 14, four + [t2 * x for x in four]))

    def mixed(ref, factors):
        total = ref[0:24]
        for i in range(1, len(factors)):
            total = total + factors[i] * ref[24 * i : 24 * (i + 1)]
        return total

    chooser = chooser_of(air_row)
    m0 = start[24:48]
    drive, stiff = FORCE * m0, SPEED * m0
    u1 = mixed(mono1, four[:2])
    u2 = mixed(mono2, four)
    a2 = stiff * (t2 * curve(u2)) + drive * mixed(force2, four)
    u3 = 2.0 * u2 - u1 + a2
    s0 = mixed(source0, four[:2])
    s1 = mixed(source1, four)
    s2 = to_rows(a2, chooser)
    within = inside((XE, WINDOW))

    def spread(x):
        return jnp.where(within, beside(x), 0.0)

    g1 = SOURCE * s0
    g2 = [SOURCE * s1 + (2.0 - 7.0 * COURANT) * g1 + COURANT * spread(g1), COURANT * g1]
    g3 = [
        SOURCE * s2 + (2.0 - 7.0 * COURANT) * g2[0] - g1 + COURANT * (spread(g2[0]) + g2[1]),
        (2.0 - 6.0 * COURANT) * g2[1] + COURANT * (spread(g2[1]) + g2[0]),
        COURANT * g2[1],
    ]
    f3 = to_columns(-2.0 * g3[0], chooser)
    shifted = pltpu.roll(force3[...], XE - 4, 0)
    a3 = stiff * (t3 * curve(u3)) + drive * (f3 + shifted)
    u4 = 2.0 * u3 - u2 + a3

    tile = pl.ds(pl.multiple_of(128 * (wide // 4), 128), 128)
    back = lax.rem(128 - 32 * lax.rem(wide, 4), 128)
    fields[0:24] = u4
    fields[24:48] = u3
    out_u[...] = pltpu.roll(fields[4:20, tile], back, 1)[:, 0:BY]
    out_w[...] = pltpu.roll(fields[28:44, tile], back, 1)[:, 0:BY]

    @pl.when(reached)
    def _():
        s3 = to_rows(a3, chooser)
        g4 = [
            SOURCE * s3 + (2.0 - 7.0 * COURANT) * g3[0] - g2[0] + COURANT * (spread(g3[0]) + g3[1]),
            (2.0 - 6.0 * COURANT) * g3[1] - g2[1] + COURANT * (spread(g3[1]) + g3[0] + g3[2]),
            (2.0 - 6.0 * COURANT) * g3[2] + COURANT * (spread(g3[2]) + g3[1]),
            COURANT * g3[2],
        ]
        tile = pl.ds(pl.multiple_of(128 * (wide // 4 - ROW0 // 128), 128), 128)
        for copy in loads:
            copy.wait()
        for gains, plane in ((g4, plane_next), (g3 + [None], plane_last)):
            for k in range(4):
                if gains[k] is None:
                    turned[pl.ds(k, BX, stride=8), :] = jnp.zeros((BX, 128), jnp.float32)
                    turned[pl.ds(7 - k, BX, stride=8), :] = jnp.zeros((BX, 128), jnp.float32)
                    continue
                wide_rows[...] = gains[k]
                part = pltpu.roll(wide_rows[4:20, tile], back, 1)
                turned[pl.ds(k, BX, stride=8), :] = part
                turned[pl.ds(7 - k, BX, stride=8), :] = -part
            across = jnp.transpose(turned[...])[0:BY]
            lane = lanes((BY, 128))
            for x in range(BX):
                above = jnp.where(lane < 4, pltpu.roll(across, (128 - 8 * x) % 128, 1), 0.0)
                below = jnp.where(lane >= 124, pltpu.roll(across, (120 - 8 * x) % 128, 1), 0.0)
                plane[x, :, 0:128] = plane[x, :, 0:128] + below
                plane[x, :, 128:256] = plane[x, :, 128:256] + above
        stores = [
            pltpu.make_async_copy(plane_next, out_next.at[:, :, MID - 128 : MID + 128], sems.at[2]),
            pltpu.make_async_copy(plane_last, out_last.at[:, :, MID - 128 : MID + 128], sems.at[3]),
        ]
        for copy in stores:
            copy.start()
        for copy in stores:
            copy.wait()


def ring(count, by):
    return [(i, (i + by) % count) for i in range(count)]


def per_device(air_now, air_prev, membrane_now, membrane_prev, inv_mass, air_row):
    sem = pltpu.SemaphoreType.DMA((4,))
    halo_x = f32(8, BY, NZ)
    halo_y = f32(XE, 8, NZ)
    to_low, to_high = pl.pallas_call(
        pack_x_kernel,
        out_shape=(halo_x, halo_x),
        in_specs=[ANY, ANY, WHOLE, WHOLE, WHOLE],
        out_specs=(WHOLE, WHOLE),
        scratch_shapes=[sem],
        compiler_params=PARAMS,
        name="pack_x",
    )(air_now, air_prev, membrane_now, membrane_prev, inv_mass)
    xlow = lax.ppermute(to_high, "gx", ring(GX, 1))
    xhigh = lax.ppermute(to_low, "gx", ring(GX, -1))
    to_low, to_high = pl.pallas_call(
        pack_y_kernel,
        out_shape=(halo_y, halo_y),
        in_specs=[WHOLE] * 4,
        out_specs=(WHOLE, WHOLE),
        compiler_params=PARAMS,
        name="pack_y",
    )(air_now, air_prev, xlow, xhigh)
    ylow = lax.ppermute(to_high, "gy", ring(GY, 1))
    yhigh = lax.ppermute(to_low, "gy", ring(GY, -1))
    air = f32(BX, BY, NZ)
    next_free, last_free, block = pl.pallas_call(
        air_kernel,
        out_shape=(air, air, f32(GY, FOLD, 128)),
        in_specs=[ANY, ANY] + [WHOLE] * 7,
        out_specs=(WHOLE, WHOLE, WHOLE),
        scratch_shapes=[
            VMEM((XE, YE, NZ), jnp.float32),
            VMEM((XE, YE, NZ), jnp.float32),
            VMEM((128, 128), jnp.float32),
            VMEM((PACK, 128), jnp.float32),
            sem,
        ],
        compiler_params=PARAMS,
        name="air_free",
    )(air_now, air_prev, xlow, xhigh, ylow, yhigh, membrane_now, membrane_prev, inv_mass)
    blocks = lax.all_to_all(block, "gy", 0, 0)
    listed = air_row.reshape(1, COLS)
    sums, *saved = pl.pallas_call(
        membrane_kernel,
        out_shape=(
            f32(1, 128), f32(48, COLS), f32(48, COLS), f32(96, COLS), f32(96, COLS), f32(24, COLS),
            f32(48, WINDOW), f32(96, WINDOW),
        ),
        in_specs=[WHOLE] * 2,
        out_specs=(WHOLE,) * 8,
        scratch_shapes=[VMEM((PACK, COLS), jnp.float32)],
        compiler_params=PARAMS,
        name="membrane",
    )(blocks, listed)
    sums = lax.psum(sums, "gx")
    return pl.pallas_call(
        finish_kernel,
        out_shape=(air, air, f32(BX, BY), f32(BX, BY)),
        in_specs=[pl.BlockSpec(memory_space=pltpu.SMEM)] + [WHOLE] * 8 + [ANY, ANY],
        out_specs=(ANY, ANY, WHOLE, WHOLE),
        scratch_shapes=[
            VMEM((BX, BY, 256), jnp.float32),
            VMEM((BX, BY, 256), jnp.float32),
            VMEM((48, COLS), jnp.float32),
            VMEM((XE, WINDOW), jnp.float32),
            VMEM((128, 128), jnp.float32),
            sem,
        ],
        input_output_aliases={9: 0, 10: 1},
        compiler_params=PARAMS,
        name="finish",
    )(sums, listed, *saved, next_free, last_free)


def solution(mesh):
    in_specs = (
        P("gx", "gy", None),
        P("gx", "gy", None),
        P("gx", "gy"),
        P("gx", "gy"),
        P("gx", "gy"),
        P(),
    )
    out_specs = (P("gx", "gy", None), P("gx", "gy", None), P("gx", "gy"), P("gx", "gy"))
    return jax.shard_map(
        per_device, mesh=mesh, in_specs=in_specs, out_specs=out_specs, check_vma=False
    )
```

time: 1310 us -> 94.7 us (0.07); the launches traced: 1290 us -> 94.4 us
  waiting for transfers between devices: 462 us -> 17.5 us
  blocking collectives: 474 us -> 38.6 us
  starting transfers between devices: 142 us -> 11.2 us
  local copies, waits for them, and re-layouts: 101 us -> 4.54 us
  other arithmetic: 88.1 us -> 0 us
  Pallas kernels: 0 us -> 21.9 us
  between operations: 20 us -> 0.68 us
    unnamed x8 -> x0, waiting for transfers between devices: 459 us -> none
    psum x4 -> x1, blocking collectives: 325 us -> 15.8 us  [per_device(): sums = lax.psum(sums, 'gx')]
    all_gather x4 -> x0, blocking collectives: 149 us -> none  [per_device(): portion = lax.all_gather(pressure_jump, 'gy', axis=1, tiled=True)]
    ppermute x32 -> x4, starting transfers between devices: 142 us -> 11.2 us  [the longest x1 6.48 us: per_device(): yhigh = lax.ppermute(to_low, 'gy', ring(GY, -1))]
    add x4 -> x0, other arithmetic: 65.7 us -> none  [air_update(): air_step = 2.0 * center - older + courant_square * (beside - 6.0 * center)]
    unnamed x85 -> x12, local copies, waits for them, and re-layouts: 67.7 us -> 4.54 us
    all_to_all x0 -> x1, blocking collectives: none -> 22.8 us  [per_device(): blocks = lax.all_to_all(block, 'gy', 0, 0)]
    pallas_call x0 -> x5, Pallas kernels: none -> 21.9 us  [the longest x1 16.7 us: per_device(): pl.pallas_call(air_kernel, out_shape=(air, air, f32(GY, FOLD, 128)), in_s...]
  transfers between devices with their start and end apart: 36 -> 4, of which waited for: 7 -> 3; matrix products, arithmetic and copies ran while one was open for 12% -> 0% of each run, Pallas kernels for 0% -> 0%
where the time goes in v1:
time: 94.7 us; the launch traced here: 94.4 us
  blocking collectives  38.6 us (41%)
  Pallas kernels  21.9 us (23%)
  waiting for transfers between devices  17.5 us (18%)
  starting transfers between devices  11.2 us (12%)
  local copies, waits for them, and re-layouts  4.54 us (5%)
    all_to_all x1, blocking collectives, per_device(): blocks = lax.all_to_all(block, 'gy', 0, 0)  22.8 us
    pallas_call x1, Pallas kernels, per_device(): pl.pallas_call(air_kernel, out_shape=(air, air, f32(GY, FOLD, 128)), in_s...  16.7 us
    psum x1, blocking collectives, per_device(): sums = lax.psum(sums, 'gx')  15.8 us
    ppermute x1, waiting for transfers between devices, per_device(): ylow = lax.ppermute(to_high, 'gy', ring(GY, 1))  9.28 us
    ppermute x1, starting transfers between devices, per_device(): yhigh = lax.ppermute(to_low, 'gy', ring(GY, -1))  6.48 us
    ppermute x1, waiting for transfers between devices, per_device(): xlow = lax.ppermute(to_high, 'gx', ring(GX, 1))  5.46 us
    unnamed x12, local copies, waits for them, and re-layouts  4.54 us
    ppermute x1, waiting for transfers between devices, per_device(): xhigh = lax.ppermute(to_low, 'gx', ring(GX, -1))  2.77 us
  transfers between devices with their start and end apart: 4, of which 3 were waited for; matrix products, arithmetic and copies ran while one was open for 0% of the time, Pallas kernels for 0%

profile of v1, /device:TPU:1, one launch (start us, length us, event | category | flops | bytes accessed | tf_op | source)
XLA Modules:
  0.0 94.4 jit_solution(11850891200173541022)
XLA Ops:
  0.6 0.0 copy-start
  0.6 1.2 %copy-done = f32[16,32,512]{2,1,0:T(8,128)S(1)} copy-done((f32[16,32,512]{2,1,0:T(8,128)S(1)}, f32[16,32,512]{2,1,0:T(8,128)}, u32[]{:S(2)}) %copy-start) | copy-done | bytes 1048600
  1.9 0.0 copy-start.1
  1.9 1.2 %copy-done.1 = f32[16,32,512]{2,1,0:T(8,128)S(1)} copy-done((f32[16,32,512]{2,1,0:T(8,128)S(1)}, f32[16,32,512]{2,1,0:T(8,128)}, u32[]{:S(2)}) %copy-start.1) | copy-done | bytes 1048600
  3.1 0.0 copy-start.2
  3.1 0.7 copy-done.2
  3.8 0.0 copy-start.3
  3.8 0.7 copy-done.3
  4.5 0.0 copy-start.4
  4.5 0.7 copy-done.4
  5.2 0.6 pack_x.1
  5.8 2.6 %collective-permute-start = (f32[8,32,512]{2,1,0:T(8,128)S(1)}, f32[8,32,512]{2,1,0:T(8,128)S(1)}, u32[]{:S(2)}, u32[]{:S(2)}) collective-permute-start(f32[8,32,512]{2,1,0:T(8,128)S(1)} %get-tuple-element.19), channel_id=1, source_target_pairs={{0,32},{32,64},{64,96},{96,128},{128,160},{160,192},{192,224},{224... | collective-permute-start | bytes 1572872 | tf_op jit(solution)/shard_map/ppermute | solution.py:435
  8.4 0.7 collective-permute-start.1
  9.0 5.5 %collective-permute-done.xlow = f32[8,32,512]{2,1,0:T(8,128)S(1)} collective-permute-done((f32[8,32,512]{2,1,0:T(8,128)S(1)}, f32[8,32,512]{2,1,0:T(8,128)S(1)}, u32[]{:S(2)}, u32[]{:S(2)}) %collective-permute-start) | collective-permute-done | bytes 524320 | tf_op jit(solution)/shard_map/ppermute | solution.py:435
  14.5 2.8 %collective-permute-done.1.xhigh = f32[8,32,512]{2,1,0:T(8,128)S(1)} collective-permute-done((f32[8,32,512]{2,1,0:T(8,128)S(1)}, f32[8,32,512]{2,1,0:T(8,128)S(1)}, u32[]{:S(2)}, u32[]{:S(2)}) %collective-permute-start.1) | collective-permute-done | bytes 524320 | tf_op jit(solution)/shard_map/ppermute | solution.py:436
  17.3 0.1 pack_y.1
  17.4 1.4 %collective-permute-start.2 = (f32[24,8,512]{2,1,0:T(8,128)S(1)}, f32[24,8,512]{2,1,0:T(8,128)S(1)}, u32[]{:S(2)}, u32[]{:S(2)}) collective-permute-start(f32[24,8,512]{2,1,0:T(8,128)S(1)} %get-tuple-element.21), channel_id=1, source_target_pairs={{0,1},{1,2},{2,3},{3,4},{4,5},{5,6},{6,7},{7,8},{8,9},{9,10},{10,1... | collective-permute-start | bytes 1179656 | tf_op jit(solution)/shard_map/ppermute | solution.py:445
  18.8 6.5 %collective-permute-start.3 = (f32[24,8,512]{2,1,0:T(8,128)S(1)}, f32[24,8,512]{2,1,0:T(8,128)S(1)}, u32[]{:S(2)}, u32[]{:S(2)}) collective-permute-start(f32[24,8,512]{2,1,0:T(8,128)S(1)} %get-tuple-element.22), channel_id=1, source_target_pairs={{0,31},{1,0},{2,1},{3,2},{4,3},{5,4},{6,5},{7,6},{8,7},{9,8},{10,9... | collective-permute-start | bytes 1179656 | tf_op jit(solution)/shard_map/ppermute | solution.py:446
  25.3 9.3 %collective-permute-done.2.ylow = f32[24,8,512]{2,1,0:T(8,128)S(1)} collective-permute-done((f32[24,8,512]{2,1,0:T(8,128)S(1)}, f32[24,8,512]{2,1,0:T(8,128)S(1)}, u32[]{:S(2)}, u32[]{:S(2)}) %collective-permute-start.2) | collective-permute-done | bytes 393248 | tf_op jit(solution)/shard_map/ppermute | solution.py:445
  34.5 0.0 collective-permute-done.3.yhigh
  34.6 16.7 %air_free.1 = (f32[16,32,512]{2,1,0:T(8,128)}, f32[16,32,512]{2,1,0:T(8,128)}, f32[32,40,128]{2,1,0:T(8,128)S(1)}) custom-call(f32[16,32,512]{2,1,0:T(8,128)S(1)} %copy-done, f32[16,32,512]{2,1,0:T(8,128)S(1)} %copy-done.1, f32[8,32,512]{2,1,0:T(8,128)S(1)} %collective-permute-done.xlow, f32[8,32,512]{2,1,0:T(8,128)S(1)} %collective-permute-done.1.xhigh, ...), custom_call_target="tpu_custom_call" | custom-call | tf_op jit(solution)/shard_map/air_free/pallas_call | solution.py:448
  51.2 0.0 copy-start.5
  51.2 22.8 %all_to_all.5.blocks = f32[32,40,128]{2,1,0:T(8,128)S(1)} all-to-all(f32[32,40,128]{2,1,0:T(8,128)S(1)} %get-tuple-element.23), channel_id=1, replica_groups=mesh['gx'=8,'gy'=32] {'gy'}, dimensions={0} | all-to-all | bytes 1310720 | tf_op jit(solution)/shard_map/all_to_all | solution.py:463
  74.0 0.0 copy-done.5
  74.0 2.5 %membrane.1 = (f32[1,128]{1,0:T(1,128)S(1)}, f32[48,1024]{1,0:T(8,128)S(1)}, f32[48,1024]{1,0:T(8,128)S(1)}, f32[96,1024]{1,0:T(8,128)S(1)}, f32[96,1024]{1,0:T(...) custom-call(f32[32,40,128]{2,1,0:T(8,128)S(1)} %all_to_all.5.blocks, ...), custom_call_target="tpu_custom_call" | custom-call | tf_op jit(solution)/shard_map/membrane/pallas_call | solution.py:465
  76.5 15.8 %psum.7.sums = f32[1,128]{1,0:T(1,128)S(1)} all-reduce(f32[1,128]{1,0:T(1,128)S(1)} %get-tuple-element.24), channel_id=1, replica_groups=mesh['gx'=8,'gy'=32] {'gx'}, use_global_device_ids=true, to_apply=%region_0.0 | all-reduce | flops 128 | bytes 1024 | tf_op jit(solution)/shard_map/psum | solution.py:477
  92.3 2.1 %finish.1 = (f32[16,32,512]{2,1,0:T(8,128)}, f32[16,32,512]{2,1,0:T(8,128)}, f32[16,32]{1,0:T(8,128)}, f32[16,32]{1,0:T(8,128)}) custom-call(f32[1,128]{1,0:T(1,128)S(1)} %psum.7.sums, s32[1,1024]{1,0:T(1,128)S(1)} %bitcast.2, f32[48,1024]{1,0:T(8,128)S(1)} %get-tuple-element.25.start, ...), custom_call_target="tpu_custom_call", output_to_operand_aliasing={{0}: (9, {}), {1}: (10, {})} | custom-call | tf_op jit(solution)/shard_map/finish/pallas_call | solution.py:478
Async XLA Ops:
  0.6 1.2 %copy-start = (f32[16,32,512]{2,1,0:T(8,128)S(1)}, f32[16,32,512]{2,1,0:T(8,128)}, u32[]{:S(2)}) copy-start(f32[16,32,512]{2,1,0:T(8,128)} %p.5) | copy-start | bytes 3145732
  1.9 1.2 %copy-start.1 = (f32[16,32,512]{2,1,0:T(8,128)S(1)}, f32[16,32,512]{2,1,0:T(8,128)}, u32[]{:S(2)}) copy-start(f32[16,32,512]{2,1,0:T(8,128)} %q.5) | copy-start | bytes 3145732
  3.1 0.7 copy-start.2
  3.8 0.7 copy-start.3
  4.5 0.7 copy-start.4
  5.8 8.7 %collective-permute-start = (f32[8,32,512]{2,1,0:T(8,128)S(1)}, f32[8,32,512]{2,1,0:T(8,128)S(1)}, u32[]{:S(2)}, u32[]{:S(2)}) collective-permute-start(f32[8,32,512]{2,1,0:T(8,128)S(1)} %get-tuple-element.19), channel_id=1, source_target_pairs={{0,32},{32,64},{64,96},{96,128},{128,160},{160,192},{192,224},{224... | collective-permute-start | bytes 1572872 | tf_op jit(solution)/shard_map/ppermute | solution.py:435
  8.4 8.9 %collective-permute-start.1 = (f32[8,32,512]{2,1,0:T(8,128)S(1)}, f32[8,32,512]{2,1,0:T(8,128)S(1)}, u32[]{:S(2)}, u32[]{:S(2)}) collective-permute-start(f32[8,32,512]{2,1,0:T(8,128)S(1)} %get-tuple-element.20), channel_id=1, source_target_pairs={{0,224},{32,0},{64,32},{96,64},{128,96},{160,128},{192,160},{224,1... | collective-permute-start | bytes 1572872 | tf_op jit(solution)/shard_map/ppermute | solution.py:436
  17.4 17.2 %collective-permute-start.2 = (f32[24,8,512]{2,1,0:T(8,128)S(1)}, f32[24,8,512]{2,1,0:T(8,128)S(1)}, u32[]{:S(2)}, u32[]{:S(2)}) collective-permute-start(f32[24,8,512]{2,1,0:T(8,128)S(1)} %get-tuple-element.21), channel_id=1, source_target_pairs={{0,1},{1,2},{2,3},{3,4},{4,5},{5,6},{6,7},{7,8},{8,9},{9,10},{10,1... | collective-permute-start | bytes 1179656 | tf_op jit(solution)/shard_map/ppermute | solution.py:445
  18.8 15.8 %collective-permute-start.3 = (f32[24,8,512]{2,1,0:T(8,128)S(1)}, f32[24,8,512]{2,1,0:T(8,128)S(1)}, u32[]{:S(2)}, u32[]{:S(2)}) collective-permute-start(f32[24,8,512]{2,1,0:T(8,128)S(1)} %get-tuple-element.22), channel_id=1, source_target_pairs={{0,31},{1,0},{2,1},{3,2},{4,3},{5,4},{6,5},{7,6},{8,7},{9,8},{10,9... | collective-permute-start | bytes 1179656 | tf_op jit(solution)/shard_map/ppermute | solution.py:446
  51.2 22.8 %copy-start.5 = (s32[1024]{0:T(1024)S(1)}, s32[1024]{0:T(1024)}, u32[]{:S(2)}) copy-start(s32[1024]{0:T(1024)} %param.11) | copy-start | bytes 12292

commit v2 on v1

v2 whole, which is shorter than its diff:
```python
import functools

import jax
import jax.numpy as jnp
from jax import lax
from jax.experimental import pallas as pl
from jax.experimental.pallas import tpu as pltpu
from jax.sharding import PartitionSpec as P

COURANT = 0.32
SPEED = 0.08
BERGER = 0.4
FORCE = 0.1
SOURCE = 0.5

GX, GY = 8, 32
BX, BY, NZ = 16, 32, 512
MID = NZ // 2
COLS = GY * BY
NODES = GX * BX * COLS
HALO = 4
XE = BX + 2 * HALO
YE = BY + 16
WINDOW = 384
ROW0 = COLS - WINDOW
FIRST, LAST = 22, 30
PACK = 160
FOLD = 40

VMEM = pltpu.VMEM
WHOLE = pl.BlockSpec(memory_space=pltpu.VMEM)
ANY = pl.BlockSpec(memory_space=pl.ANY)
HBM = pl.BlockSpec(memory_space=pltpu.HBM)


def granted(mib):
    return pltpu.CompilerParams(vmem_limit_bytes=mib * 1024 * 1024)


def f32(*shape):
    return jax.ShapeDtypeStruct(shape, jnp.float32)


def lanes(shape):
    return lax.broadcasted_iota(jnp.int32, shape, len(shape) - 1)


def sublanes(shape):
    return lax.broadcasted_iota(jnp.int32, shape, len(shape) - 2)


def fold(rows, wide):
    quarter = lanes((FOLD, 128)) // 32
    folded = rows[0:FOLD, :]
    for g in range(1, 4):
        folded = jnp.where(quarter == g, pltpu.roll(rows[FOLD * g : FOLD * (g + 1), :], 32 * g, 1), folded)
    return pltpu.roll(folded, 32 * lax.rem(wide, 4), 1)


def pack_kernel(
    p, q, u, w, m, xlow, xhigh, ylow, yhigh, block,
    edges, sides, tips, copied, planes, members, turned, rows, sems,
):
    wide = lax.axis_index("gy")

    def started(pairs, at):
        copies = [pltpu.make_async_copy(x, y, sems.at[at + i]) for i, (x, y) in enumerate(pairs)]
        for copy in copies:
            copy.start()
        return copies

    mids = started([(x.at[:, :, MID - 128 : MID + 128], planes.at[i]) for i, x in enumerate((p, q))], 0)
    own = started([(x, members.at[i]) for i, x in enumerate((u, w, m))], 2)
    ins = started([(x.at[:, at : at + 8], edges.at[i]) for i, (x, at) in enumerate(((p, 0), (q, 0), (p, 24), (q, 24)))], 5)
    ends = started(
        [
            (p.at[0:4], tips.at[0, 0:4]),
            (q.at[0:3], tips.at[0, 4:7]),
            (p.at[12:16], tips.at[1, 0:4]),
            (q.at[13:16], tips.at[1, 4:7]),
        ],
        9,
    )
    lane = lanes((BY, 128))
    for i in range(2):
        mids[i].wait()
        total = jnp.zeros((BY, 128), jnp.float32)
        for x in range(BX):
            above = pltpu.roll(planes[i, x, :, 128:256], 8 * x, 1)
            below = pltpu.roll(planes[i, x, :, 0:128], (8 * x + 8) % 128, 1)
            total = jnp.where((lane >= 8 * x) & (lane < 8 * x + 4), above, total)
            total = jnp.where((lane >= 8 * x + 4) & (lane < 8 * x + 8), below, total)
        turned[i, 0:BY, :] = total
        turned[i, BY:128, :] = jnp.zeros((128 - BY, 128), jnp.float32)
        turned[i] = jnp.transpose(turned[i])
        for k in range(4 - i):
            at = 48 + 64 * i + 16 * k
            rows[at : at + 16, :] = turned[i, pl.ds(7 - k, BX, stride=8), :] - turned[i, pl.ds(k, BX, stride=8), :]
    for i in range(3):
        own[i].wait()
        rows[16 * i : 16 * i + 16, 0:BY] = members[i]
    folded = fold(rows, wide)
    for i in range(GY):
        copied[i] = folded
    sent = started([(copied, block)], 13)
    lower = sublanes((8, NZ)) < 4
    for copy in ins:
        copy.wait()
    for r in range(BX):
        sides[0, r] = jnp.where(lower, edges[0, r], pltpu.roll(edges[1, r], 4, 0))
        sides[1, r] = jnp.where(lower, pltpu.roll(edges[3, r], 4, 0), edges[2, r])
    sent += started([(sides.at[0], ylow), (sides.at[1], yhigh)], 14)
    for copy in ends:
        copy.wait()
    sent += started([(tips.at[0], xlow), (tips.at[1], xhigh)], 16)
    for copy in sent:
        copy.wait()


def corner_kernel(xlow, xhigh, corner_low, corner_high):
    lower = sublanes((8, NZ)) < 4
    for i in range(4):
        for at, halo, j in ((i, xlow, 4 + max(i - 1, 0)), (4 + i, xhigh, 4 + min(i, 2))):
            corner_low[at] = jnp.where(lower, halo[i, 0:8], pltpu.roll(halo[j, 0:8], 4, 0))
            corner_high[at] = jnp.where(lower, pltpu.roll(halo[j, 24:32], 4, 0), halo[i, 24:32])


def unfold_kernel(blocks, members, jumps, to_low, to_high):
    quarter = lanes((FOLD, 128)) // 32
    for g in range(4):
        for t in range(8):
            if g >= 2 and t < 5:
                continue
            merged = blocks[4 * t + (-g) % 4]
            for s in range(1, 4):
                merged = jnp.where(quarter == s, blocks[4 * t + (s - g) % 4], merged)
            merged = pltpu.roll(merged, (128 - 32 * g) % 128, 1)
            column = slice(128 * t, 128 * (t + 1))
            narrow = slice(128 * (t - 5), 128 * (t - 4))
            if g == 0:
                members[0:40, column] = merged
            elif g == 1:
                members[40:48, column] = merged[0:8]
                if t >= 5:
                    jumps[0:32, narrow] = merged[8:40]
            else:
                jumps[40 * g - 48 : 40 * g - 8, narrow] = merged
    for out, at in ((to_low, 0), (to_high, 12)):
        for i in range(3):
            out[4 * i : 4 * i + 4, :] = members[16 * i + at : 16 * i + at + 4, :]
        for k in range(4):
            out[12 + 4 * k : 16 + 4 * k, 0:WINDOW] = jumps[16 * k + at : 16 * k + at + 4, :]
        for k in range(3):
            out[12 + 4 * k : 16 + 4 * k, 512 : 512 + WINDOW] = jumps[64 + 16 * k + at : 68 + 16 * k + at, :]


def edge_free(shape, edge):
    return jnp.broadcast_to(edge.astype(jnp.int32), shape) == 0


def air_kernel(p, q, xlow, xhigh, ylow, yhigh, clow, chigh, out_next, out_last, a, b, sems):
    tall = lax.axis_index("gx")
    wide = lax.axis_index("gy")
    first, last = tall == 0, tall == GX - 1
    bottom, top = wide == 0, wide == GY - 1
    layers = [slice(128 * k, 128 * (k + 1)) for k in range(4)]
    copies = []
    for k in range(4):
        copies.append(pltpu.make_async_copy(p.at[:, :, layers[k]], a.at[k, 4:20, 8:40], sems.at[k]))
        copies.append(pltpu.make_async_copy(q.at[:, :, layers[k]], b.at[k, 4:20, 8:40], sems.at[4 + k]))
    for copy in copies:
        copy.start()
    inner_low, inner_high = edge_free((BY, 128), first), edge_free((BY, 128), last)
    tile_low, tile_high = edge_free((8, 128), bottom), edge_free((8, 128), top)
    for k in range(4):
        for i in range(4):
            a[k, i, 8:40] = jnp.where(inner_low, xlow[i, :, layers[k]], 0.0)
            a[k, 20 + i, 8:40] = jnp.where(inner_high, xhigh[i, :, layers[k]], 0.0)
        for i in range(3):
            b[k, 1 + i, 8:40] = jnp.where(inner_low, xlow[4 + i, :, layers[k]], 0.0)
            b[k, 20 + i, 8:40] = jnp.where(inner_high, xhigh[4 + i, :, layers[k]], 0.0)
        for r in range(XE):
            if 4 <= r < 20:
                lo, hi = ylow[r - 4, :, layers[k]], yhigh[r - 4, :, layers[k]]
            else:
                i = r if r < 4 else r - 16
                free = (inner_low if r < 4 else inner_high)[0:8]
                lo = jnp.where(free, clow[i, :, layers[k]], 0.0)
                hi = jnp.where(free, chigh[i, :, layers[k]], 0.0)
            lo = jnp.where(tile_low, lo, 0.0)
            hi = jnp.where(tile_high, hi, 0.0)
            a[k, r, 0:8] = lo
            a[k, r, 40:48] = hi
            b[k, r, 0:8] = pltpu.roll(lo, 4, 0)
            b[k, r, 40:48] = pltpu.roll(hi, 4, 0)
    for copy in copies:
        copy.wait()

    lane = lanes((8, 128))

    def advance(now, old, r, tile):
        at = 8 * tile
        c = [now[k, r, at : at + 8] for k in range(4)]
        up = [pltpu.roll(x, 1, 1) for x in c]
        down = [pltpu.roll(x, 127, 1) for x in c]
        for k in range(4):
            left = jnp.where(lane == 0, up[k - 1] if k else 0.0, up[k])
            right = jnp.where(lane == 127, down[k + 1] if k < 3 else 0.0, down[k])
            if tile > 0:
                before = now[k, r, at - 1 : at + 7]
            else:
                before = pltpu.roll(c[k], 1, 0)
            if tile < 5:
                after = now[k, r, at + 1 : at + 9]
            else:
                after = pltpu.roll(c[k], 7, 0)
            ring = (left + right) + (before + after) + (now[k, r - 1, at : at + 8] + now[k, r + 1, at : at + 8])
            new = (2.0 - 6.0 * COURANT) * c[k] - old[k, r, at : at + 8] + COURANT * ring
            if tile == 0:
                new = jnp.where(tile_low, new, 0.0)
            if tile == 5:
                new = jnp.where(tile_high, new, 0.0)
            old[k, r, at : at + 8] = new

    def results(x, out, at):
        return [pltpu.make_async_copy(x.at[k, 4:20, 8:40], out.at[:, :, layers[k]], sems.at[at + k]) for k in range(4)]

    for t in range(4):
        now, old = (a, b) if t % 2 == 0 else (b, a)

        def row(r):
            for tile in range(6) if t < 3 else range(1, 5):
                advance(now, old, r, tile)

        if t < 3:

            @pl.when(jnp.logical_not(first))
            def _():
                for r in range(t + 1, 4):
                    row(r)

        def body(i, carry):
            for r in range(8):
                row(4 + 8 * i + r)
            return carry

        lax.fori_loop(0, 2, body, 0)
        if t < 3:

            @pl.when(jnp.logical_not(last))
            def _():
                for r in range(20, XE - 1 - t):
                    row(r)

        if t == 2:
            sent = results(b, out_last, 8)
            for copy in sent:
                copy.start()
    sent = sent + results(a, out_next, 12)
    for copy in sent[4:]:
        copy.start()
    for copy in sent:
        copy.wait()


def split(x):
    high = x.astype(jnp.bfloat16)
    low = (x - high.astype(jnp.float32)).astype(jnp.bfloat16)
    return jnp.concatenate([high, low], axis=0)


def to_columns(x, chooser):
    n = x.shape[0]
    both = lax.dot_general(split(x), chooser, (((1,), (0,)), ((), ())), preferred_element_type=jnp.float32)
    return both[0:n] + both[n : 2 * n]


def to_rows(x, chooser):
    n = x.shape[0]
    both = lax.dot_general(split(x), chooser, (((1,), (1,)), ((), ())), preferred_element_type=jnp.float32)
    return both[0:n] + both[n : 2 * n]


def chooser_of(air_row):
    rows = lax.broadcasted_iota(jnp.int32, (WINDOW, COLS), 0) + ROW0
    return jnp.where(rows == air_row[...], 1.0, 0.0).astype(jnp.bfloat16)


def beside(field):
    n = field.shape[1]
    lane = lanes(field.shape)
    left = jnp.where(lane == 0, 0.0, pltpu.roll(field, 1, 1))
    right = jnp.where(lane == n - 1, 0.0, pltpu.roll(field, n - 1, 1))
    return left + right + pltpu.roll(field, 1, 0) + pltpu.roll(field, field.shape[0] - 1, 0)


def curve(field):
    return beside(field) - 4.0 * field


def inside(shape):
    tall = lax.axis_index("gx")
    row = sublanes(shape)
    low = jnp.where(tall == 0, 4, 0)
    high = jnp.where(tall == GX - 1, 20, 24)
    return (row >= low) & (row < high)


def membrane_kernel(
    members, jumps, hlow, hhigh, air_row, sums, start, mono1, mono2, force2, force3, source0, source1, parts, slab, listed, sems
):
    tall = lax.axis_index("gx")
    loaded = pltpu.make_async_copy(air_row, listed, sems.at[0])
    loaded.start()
    for i in range(3):
        at = XE * i
        parts[at : at + 4] = jnp.where(edge_free((4, COLS), tall == 0), hlow[4 * i : 4 * i + 4, :], 0.0)
        parts[at + 4 : at + 20] = members[16 * i : 16 * i + 16]
        parts[at + 20 : at + 24] = jnp.where(edge_free((4, COLS), tall == GX - 1), hhigh[4 * i : 4 * i + 4, :], 0.0)
    for i in range(7):
        at, row = XE * i, 12 + 4 * (i % 4)
        narrow = slice(512 * (i // 4), 512 * (i // 4) + WINDOW)
        slab[at : at + 4] = jnp.where(edge_free((4, WINDOW), tall == 0), hlow[row : row + 4, narrow], 0.0)
        slab[at + 4 : at + 20] = jumps[16 * i : 16 * i + 16]
        slab[at + 20 : at + 24] = jnp.where(edge_free((4, WINDOW), tall == GX - 1), hhigh[row : row + 4, narrow], 0.0)
    within = inside((XE, WINDOW))

    def spread(x):
        return jnp.where(within, beside(x), 0.0)

    older = [slab[96 + XE * k : 96 + XE * (k + 1)] for k in range(3)] + [None]
    newer = [slab[XE * k : XE * (k + 1)] for k in range(4)]
    free = [newer[0]]
    for t in range(3):
        step = []
        for k in range(3 - t):
            own = 2.0 - (7.0 if k == 0 else 6.0) * COURANT
            ring = spread(newer[k]) + newer[k + 1]
            if k:
                ring = ring + newer[k - 1]
            step.append(own * newer[k] - older[k] + COURANT * ring)
        older, newer = newer, step
        free.append(newer[0])
    loaded.wait()
    chooser = chooser_of(listed)
    u0, w0, m0 = parts[0:24], parts[24:48], parts[48:72]
    start[0:24] = u0
    start[24:48] = m0
    free = to_columns(jnp.concatenate(free, axis=0), chooser)
    force3[...] = free[72:96]
    drive, stiff = FORCE * m0, SPEED * m0
    row = sublanes((XE, COLS))
    mine = (row >= HALO) & (row < HALO + BX)
    totals = []

    def gram(fields, curves):
        for i in range(len(fields)):
            for j in range(i, len(fields)):
                product = fields[i] * curves[j]
                part = product[:, 0:128]
                for k in range(1, COLS // 128):
                    part = part + product[:, 128 * k : 128 * (k + 1)]
                totals.append(jnp.sum(part, axis=0, keepdims=True))

    def masked(curves):
        return [jnp.where(mine, -c, 0.0) for c in curves]

    c0 = curve(u0)
    gram([u0], masked([c0]))
    a0 = [drive * free[0:24], stiff * c0]
    u1 = [2.0 * u0 - w0 + a0[0], a0[1]]
    mono1[0:24] = u1[0]
    mono1[24:48] = u1[1]
    c1 = [curve(x) for x in u1]
    gram(u1, masked(c1))
    s0 = to_rows(jnp.concatenate(a0, axis=0), chooser)
    source0[...] = s0
    f1 = to_columns(-s0, chooser)
    a1 = [drive * (free[24:48] + f1[0:24]), drive * f1[24:48], stiff * c1[0], stiff * c1[1]]
    u2 = [2.0 * u1[0] - u0 + a1[0], 2.0 * u1[1] + a1[1], a1[2], a1[3]]
    for i in range(4):
        mono2[24 * i : 24 * (i + 1)] = u2[i]
    c2 = [curve(x) for x in u2]
    gram(u2, masked(c2))
    s1 = to_rows(jnp.concatenate(a1, axis=0), chooser)
    source1[...] = s1
    jump2 = []
    for i in range(4):
        half = SOURCE * s1[24 * i : 24 * (i + 1)]
        if i < 2:
            g1 = SOURCE * s0[24 * i : 24 * (i + 1)]
            half = half + (2.0 - 7.0 * COURANT) * g1 + COURANT * spread(g1)
        jump2.append(-2.0 * half)
    f2 = to_columns(jnp.concatenate(jump2, axis=0), chooser)
    f2 = [f2[24 * i : 24 * (i + 1)] for i in range(4)]
    f2[0] = f2[0] + free[48:72]
    for i in range(4):
        force2[24 * i : 24 * (i + 1)] = f2[i]
    u3 = [2.0 * u2[i] + drive * f2[i] for i in range(4)] + [stiff * c for c in c2]
    u3[0] = u3[0] - u1[0]
    u3[1] = u3[1] - u1[1]
    gram(u3, masked([curve(x) for x in u3]))

    count = len(totals)
    stack = jnp.concatenate(totals + [jnp.zeros((56 - count, 128), jnp.float32)], axis=0)
    column = jnp.sum(stack, axis=1, keepdims=True)
    diagonal = jnp.where(sublanes((56, 128)) == lanes((56, 128)), column, 0.0)
    sums[...] = jnp.sum(diagonal, axis=0, keepdims=True)


def quadratic(sums, at, monos):
    total = 0.0
    for i in range(len(monos)):
        for j in range(i, len(monos)):
            term = monos[i] * (sums(at) * monos[j])
            total = total + (term if i == j else 2.0 * term)
            at += 1
    return total


def finish_kernel(
    share0, share1, share2, share3, air_row, start, mono1, mono2, force2, force3, source0, source1, next_in, last_in,
    out_next, out_last, out_u, out_w, plane_next, plane_last, fields, wide_rows, turned, listed, sems,
):
    wide = lax.axis_index("gy")
    reached = (wide >= FIRST) & (wide <= LAST)
    loaded = pltpu.make_async_copy(air_row, listed, sems.at[4])
    loaded.start()
    loads = [
        pltpu.make_async_copy(next_in.at[:, :, MID - 128 : MID + 128], plane_next, sems.at[0]),
        pltpu.make_async_copy(last_in.at[:, :, MID - 128 : MID + 128], plane_last, sems.at[1]),
    ]

    @pl.when(reached)
    def _():
        for copy in loads:
            copy.start()

    def tension(energy):
        return 1.0 + BERGER * energy / NODES

    def sums(at):
        return (share0[0, at] + share1[0, at]) + (share2[0, at] + share3[0, at])

    t0 = tension(sums(0))
    t1 = tension(quadratic(sums, 1, [1.0, t0]))
    four = [1.0, t0, t1, t0 * t1]
    t2 = tension(quadratic(sums, 4, four))
    t3 = tension(quadratic(sums, 14, four + [t2 * x for x in four]))

    def mixed(ref, factors):
        total = ref[0:24]
        for i in range(1, len(factors)):
            total = total + factors[i] * ref[24 * i : 24 * (i + 1)]
        return total

    loaded.wait()
    chooser = chooser_of(listed)
    m0 = start[24:48]
    drive, stiff = FORCE * m0, SPEED * m0
    u1 = mixed(mono1, four[:2])
    u2 = mixed(mono2, four)
    a2 = stiff * (t2 * curve(u2)) + drive * mixed(force2, four)
    u3 = 2.0 * u2 - u1 + a2
    s0 = mixed(source0, four[:2])
    s1 = mixed(source1, four)
    s2 = to_rows(a2, chooser)
    within = inside((XE, WINDOW))

    def spread(x):
        return jnp.where(within, beside(x), 0.0)

    g1 = SOURCE * s0
    g2 = [SOURCE * s1 + (2.0 - 7.0 * COURANT) * g1 + COURANT * spread(g1), COURANT * g1]
    g3 = [
        SOURCE * s2 + (2.0 - 7.0 * COURANT) * g2[0] - g1 + COURANT * (spread(g2[0]) + g2[1]),
        (2.0 - 6.0 * COURANT) * g2[1] + COURANT * (spread(g2[1]) + g2[0]),
        COURANT * g2[1],
    ]
    f3 = to_columns(-2.0 * g3[0], chooser)
    a3 = stiff * (t3 * curve(u3)) + drive * (f3 + force3[...])
    u4 = 2.0 * u3 - u2 + a3

    tile = pl.ds(pl.multiple_of(128 * (wide // 4), 128), 128)
    back = lax.rem(128 - 32 * lax.rem(wide, 4), 128)
    fields[0:24] = u4
    fields[24:48] = u3
    out_u[...] = pltpu.roll(fields[4:20, tile], back, 1)[:, 0:BY]
    out_w[...] = pltpu.roll(fields[28:44, tile], back, 1)[:, 0:BY]

    @pl.when(reached)
    def _():
        s3 = to_rows(a3, chooser)
        g4 = [
            SOURCE * s3 + (2.0 - 7.0 * COURANT) * g3[0] - g2[0] + COURANT * (spread(g3[0]) + g3[1]),
            (2.0 - 6.0 * COURANT) * g3[1] - g2[1] + COURANT * (spread(g3[1]) + g3[0] + g3[2]),
            (2.0 - 6.0 * COURANT) * g3[2] + COURANT * (spread(g3[2]) + g3[1]),
            COURANT * g3[2],
        ]
        tile = pl.ds(pl.multiple_of(128 * (wide // 4 - ROW0 // 128), 128), 128)
        for copy in loads:
            copy.wait()
        for gains, plane in ((g4, plane_next), (g3 + [None], plane_last)):
            for k in range(4):
                if gains[k] is None:
                    turned[pl.ds(k, BX, stride=8), :] = jnp.zeros((BX, 128), jnp.float32)
                    turned[pl.ds(7 - k, BX, stride=8), :] = jnp.zeros((BX, 128), jnp.float32)
                    continue
                wide_rows[...] = gains[k]
                part = pltpu.roll(wide_rows[4:20, tile], back, 1)
                turned[pl.ds(k, BX, stride=8), :] = part
                turned[pl.ds(7 - k, BX, stride=8), :] = -part
            across = jnp.transpose(turned[...])[0:BY]
            lane = lanes((BY, 128))
            for x in range(BX):
                above = jnp.where(lane < 4, pltpu.roll(across, (128 - 8 * x) % 128, 1), 0.0)
                below = jnp.where(lane >= 124, pltpu.roll(across, (120 - 8 * x) % 128, 1), 0.0)
                plane[x, :, 0:128] = plane[x, :, 0:128] + below
                plane[x, :, 128:256] = plane[x, :, 128:256] + above
        stores = [
            pltpu.make_async_copy(plane_next, out_next.at[:, :, MID - 128 : MID + 128], sems.at[2]),
            pltpu.make_async_copy(plane_last, out_last.at[:, :, MID - 128 : MID + 128], sems.at[3]),
        ]
        for copy in stores:
            copy.start()
        for copy in stores:
            copy.wait()


def ring(count, by):
    return [(i, (i + by) % count) for i in range(count)]


def across(count, by):
    return [(i, (i + 2 * by) % count if by else i ^ 1) for i in range(count)]


def per_device(air_now, air_prev, membrane_now, membrane_prev, inv_mass, air_row):
    def sems(n):
        return pltpu.SemaphoreType.DMA((n,))

    halo_x, halo_y, corner, stripe = f32(7, BY, NZ), f32(BX, 8, NZ), f32(8, 8, NZ), f32(28, COLS)
    *sends, block = pl.pallas_call(
        pack_kernel,
        out_shape=(halo_x, halo_x, halo_y, halo_y, f32(GY, FOLD, 128)),
        in_specs=[HBM] * 5,
        out_specs=(HBM,) * 5,
        scratch_shapes=[
            VMEM((4, BX, 8, NZ), jnp.float32),
            VMEM((2, BX, 8, NZ), jnp.float32),
            VMEM((2, 7, BY, NZ), jnp.float32),
            VMEM((GY, FOLD, 128), jnp.float32),
            VMEM((2, BX, BY, 256), jnp.float32),
            VMEM((3, BX, BY), jnp.float32),
            VMEM((2, 128, 128), jnp.float32),
            VMEM((PACK, 128), jnp.float32),
            sems(18),
        ],
        compiler_params=granted(63),
        name="pack",
    )(air_now, air_prev, membrane_now, membrane_prev, inv_mass)
    blocks = lax.all_to_all(block, "gy", 0, 0)
    to_xlow, to_xhigh, to_ylow, to_yhigh = sends
    xlow = lax.ppermute(to_xhigh, "gx", ring(GX, 1))
    xhigh = lax.ppermute(to_xlow, "gx", ring(GX, -1))
    ylow = lax.ppermute(to_yhigh, "gy", ring(GY, 1))
    yhigh = lax.ppermute(to_ylow, "gy", ring(GY, -1))
    to_clow, to_chigh = pl.pallas_call(
        corner_kernel,
        out_shape=(corner, corner),
        in_specs=[WHOLE] * 2,
        out_specs=(WHOLE,) * 2,
        compiler_params=granted(3),
        name="corners",
    )(xlow, xhigh)
    clow = lax.ppermute(to_chigh, "gy", ring(GY, 1))
    chigh = lax.ppermute(to_clow, "gy", ring(GY, -1))
    air = f32(BX, BY, NZ)
    brick = VMEM((4, XE, YE, 128), jnp.float32)
    next_free, last_free = pl.pallas_call(
        air_kernel,
        out_shape=(air, air),
        in_specs=[HBM, HBM] + [WHOLE] * 6,
        out_specs=(HBM, HBM),
        scratch_shapes=[brick, brick, sems(16)],
        compiler_params=granted(8),
        cost_estimate=pl.CostEstimate(flops=40_000_000, bytes_accessed=8_000_000, transcendentals=0),
        name="air_free",
    )(air_now, air_prev, xlow, xhigh, ylow, yhigh, clow, chigh)
    members, jumps, to_low, to_high = pl.pallas_call(
        unfold_kernel,
        out_shape=(f32(48, COLS), f32(112, WINDOW), stripe, stripe),
        in_specs=[WHOLE],
        out_specs=(WHOLE,) * 4,
        compiler_params=granted(3),
        name="unfold",
    )(blocks)
    hlow = lax.ppermute(to_high, "gx", ring(GX, 1))
    hhigh = lax.ppermute(to_low, "gx", ring(GX, -1))
    listed = air_row.reshape(1, COLS)
    sums, *saved = pl.pallas_call(
        membrane_kernel,
        out_shape=(
            f32(1, 128), f32(48, COLS), f32(48, COLS), f32(96, COLS), f32(96, COLS), f32(24, COLS),
            f32(48, WINDOW), f32(96, WINDOW),
        ),
        in_specs=[WHOLE] * 4 + [HBM],
        out_specs=(WHOLE,) * 8,
        scratch_shapes=[
            VMEM((3 * XE, COLS), jnp.float32),
            VMEM((7 * XE, WINDOW), jnp.float32),
            VMEM((1, COLS), jnp.int32),
            sems(1),
        ],
        compiler_params=granted(10),
        name="membrane",
    )(members, jumps, hlow, hhigh, listed)
    sums = sums + lax.ppermute(sums, "gx", across(GX, 0))
    shares = [sums] + [lax.ppermute(sums, "gx", across(GX, by)) for by in (1, 2, 3)]
    return pl.pallas_call(
        finish_kernel,
        out_shape=(air, air, f32(BX, BY), f32(BX, BY)),
        in_specs=[pl.BlockSpec(memory_space=pltpu.SMEM)] * 4 + [HBM] + [WHOLE] * 7 + [HBM, HBM],
        out_specs=(HBM, HBM, WHOLE, WHOLE),
        scratch_shapes=[
            VMEM((BX, BY, 256), jnp.float32),
            VMEM((BX, BY, 256), jnp.float32),
            VMEM((48, COLS), jnp.float32),
            VMEM((XE, WINDOW), jnp.float32),
            VMEM((128, 128), jnp.float32),
            VMEM((1, COLS), jnp.int32),
            sems(5),
        ],
        input_output_aliases={12: 0, 13: 1},
        compiler_params=granted(8),
        name="finish",
    )(*shares, listed, *saved, next_free, last_free)


def solution(mesh):
    in_specs = (
        P("gx", "gy", None),
        P("gx", "gy", None),
        P("gx", "gy"),
        P("gx", "gy"),
        P("gx", "gy"),
        P(),
    )
    out_specs = (P("gx", "gy", None), P("gx", "gy", None), P("gx", "gy"), P("gx", "gy"))
    return jax.shard_map(
        per_device, mesh=mesh, in_specs=in_specs, out_specs=out_specs, check_vma=False
    )
```

time: 94.7 us -> 67.6 us (0.71)
  blocking collectives: 38.6 us -> 0 us
  starting transfers between devices: 11.2 us -> 34.8 us
  Pallas kernels: 21.9 us -> 16.7 us
  local copies, waits for them, and re-layouts: 4.54 us -> 0.01 us
  waiting for transfers between devices: 17.5 us -> 14.8 us
    all_to_all x1 -> x0, blocking collectives: 22.8 us -> none  [per_device(): blocks = lax.all_to_all(block, 'gy', 0, 0)]
    psum x1 -> x0, blocking collectives: 15.8 us -> none  [per_device(): sums = lax.psum(sums, 'gx')]
    all_to_all x0 -> x1, starting transfers between devices: none -> 12 us  [per_device(): blocks = lax.all_to_all(block, 'gy', 0, 0)]
    ppermute x4 -> x12, waiting for transfers between devices: 17.5 us -> 5.52 us  [the longest x1 4.39 us: per_device(): hhigh = lax.ppermute(to_low, 'gx', ring(GX, -1))]
    ppermute x4 -> x12, starting transfers between devices: 11.2 us -> 22.7 us  [the longest x1 7.34 us: per_device(): hlow = lax.ppermute(to_high, 'gx', ring(GX, 1))]
    all_to_all x0 -> x1, waiting for transfers between devices: none -> 9.28 us  [per_device(): blocks = lax.all_to_all(block, 'gy', 0, 0)]
    pallas_call x3 -> x4, Pallas kernels: 17.3 us -> 11.8 us  [the longest x1 7.27 us: per_device(): pl.pallas_call(air_kernel, out_shape=(air, air), in_specs=[HBM, HBM] + [W...]
    unnamed x12 -> x6, local copies, waits for them, and re-layouts: 4.54 us -> 0.01 us
  transfers between devices with their start and end apart: 4 -> 13, of which waited for: 3 -> 3; matrix products, arithmetic and copies ran while one was open for 0% -> 0% of each run, Pallas kernels for 0% -> 17%
where the time goes in v2:
time: 67.6 us; the launch traced here: 67 us
  starting transfers between devices  34.8 us (51%)
  Pallas kernels  16.7 us (25%)
  waiting for transfers between devices  14.8 us (22%)
  between operations  0.73 us (1%)
    all_to_all x1, starting transfers between devices, per_device(): blocks = lax.all_to_all(block, 'gy', 0, 0)  12 us
    all_to_all x1, waiting for transfers between devices, per_device(): blocks = lax.all_to_all(block, 'gy', 0, 0)  9.28 us
    ppermute x1, starting transfers between devices, per_device(): hlow = lax.ppermute(to_high, 'gx', ring(GX, 1))  7.34 us
    pallas_call x1, Pallas kernels, per_device(): pl.pallas_call(air_kernel, out_shape=(air, air), in_specs=[HBM, HBM] + [W...  7.27 us
    ppermute x1, waiting for transfers between devices, per_device(): hhigh = lax.ppermute(to_low, 'gx', ring(GX, -1))  4.39 us
    ppermute x1, starting transfers between devices, per_device(): chigh = lax.ppermute(to_clow, 'gy', ring(GY, -1))  3.7 us
    ppermute x1, starting transfers between devices, per_device(): yhigh = lax.ppermute(to_ylow, 'gy', ring(GY, -1))  3.5 us
    ppermute x3, starting transfers between devices, per_device(): lax.ppermute(sums, 'gx', across(GX, by))  3.34 us
  transfers between devices with their start and end apart: 13, of which 3 were waited for; matrix products, arithmetic and copies ran while one was open for 0% of the time, Pallas kernels for 17%

profile of v2, /device:TPU:1, one launch (start us, length us, event | category | flops | bytes accessed | tf_op | source)
XLA Modules:
  0.0 67.0 jit_solution(1834865142563772162)
XLA Ops:
  0.6 3.3 %pack.1 = (f32[7,32,512]{2,1,0:T(8,128)}, f32[7,32,512]{2,1,0:T(8,128)}, f32[16,8,512]{2,1,0:T(8,128)}, f32[16,8,512]{2,1,0:T(8,128)}, f32[32,40,128]{2,1,0:T(8,128)}) custom-call(f32[16,32,512]{2,1,0:T(8,128)} %p.3, f32[16,32,512]{2,1,0:T(8,128)} %q.3, f32[16,32]{1,0:T(8,128)} %u.1, f32[16,32]{1,0:T(8,128)} %w.1, f32[16,32]{1,0:T(8,128)} %m.1), custom_call_target="tpu_custom_call" | custom-call | tf_op jit(solution)/shard_map/pack/pallas_call | solution.py:543
  3.9 0.0 copy-start.2
  4.0 12.0 %all-to-all-start = ((f32[32,40,128]{2,1,0:T(8,128)}), f32[32,40,128]{2,1,0:T(8,128)S(1)}, u32[]{:S(2)}, u32[]{:S(2)}) async-start(f32[32,40,128]{2,1,0:T(8,128)} %get-tuple-element.25), calls=%async_computation | async-start | bytes 1310720 | tf_op jit(solution)/shard_map/all_to_all | solution.py:562
  16.0 2.1 %collective-permute-start.6 = (f32[7,32,512]{2,1,0:T(8,128)}, f32[7,32,512]{2,1,0:T(8,128)S(1)}, u32[]{:S(2)}, u32[]{:S(2)}) collective-permute-start(f32[7,32,512]{2,1,0:T(8,128)} %get-tuple-element.38), channel_id=1, source_target_pairs={{0,32},{32,64},{64,96},{96,128},{128,160},{160,192},{192,224},{224... | collective-permute-start | bytes 1376264 | tf_op jit(solution)/shard_map/ppermute | solution.py:564
  18.1 0.0 collective-permute-start.7
  18.1 1.5 %collective-permute-start.8 = (f32[16,8,512]{2,1,0:T(8,128)}, f32[16,8,512]{2,1,0:T(8,128)S(1)}, u32[]{:S(2)}, u32[]{:S(2)}) collective-permute-start(f32[16,8,512]{2,1,0:T(8,128)} %get-tuple-element.40), channel_id=1, source_target_pairs={{0,1},{1,2},{2,3},{3,4},{4,5},{5,6},{6,7},{7,8},{8,9},{9,10},{10,1... | collective-permute-start | bytes 786440 | tf_op jit(solution)/shard_map/ppermute | solution.py:566
  19.6 0.0 copy-start
  19.6 0.0 copy-start.1
  19.6 3.5 %collective-permute-start.9 = (f32[16,8,512]{2,1,0:T(8,128)}, f32[16,8,512]{2,1,0:T(8,128)}, u32[]{:S(2)}, u32[]{:S(2)}) collective-permute-start(f32[16,8,512]{2,1,0:T(8,128)} %get-tuple-element.41), channel_id=1, source_target_pairs={{0,31},{1,0},{2,1},{3,2},{4,3},{5,4},{6,5},{7,6},{8,7},{9,8},{10,9... | collective-permute-start | bytes 786440 | tf_op jit(solution)/shard_map/ppermute | solution.py:567
  23.1 9.3 %all-to-all-done.blocks = f32[32,40,128]{2,1,0:T(8,128)S(1)} async-done(((f32[32,40,128]{2,1,0:T(8,128)}), f32[32,40,128]{2,1,0:T(8,128)S(1)}, u32[]{:S(2)}, u32[]{:S(2)}) %all-to-all-start) | async-done | bytes 655392 | tf_op jit(solution)/shard_map/all_to_all | solution.py:562
  32.4 0.2 unfold.1
  32.6 7.3 %collective-permute-start = (f32[28,1024]{1,0:T(8,128)S(1)}, f32[28,1024]{1,0:T(8,128)S(1)}, u32[]{:S(2)}, u32[]{:S(2)}) collective-permute-start(f32[28,1024]{1,0:T(8,128)S(1)} %get-tuple-element.28), channel_id=1, source_target_pairs={{0,32},{32,64},{64,96},{96,128},{128,160},{160,192},{192,224},{224... | collective-permute-start | bytes 344072 | tf_op jit(solution)/shard_map/ppermute | solution.py:598
  39.9 0.0 collective-permute-done.6.xlow
  39.9 0.0 collective-permute-done.7.xhigh
  39.9 1.0 %corners.1 = (f32[8,8,512]{2,1,0:T(8,128)S(1)}, f32[8,8,512]{2,1,0:T(8,128)S(1)}) custom-call(f32[7,32,512]{2,1,0:T(8,128)S(1)} %collective-permute-done.6.xlow, f32[7,32,512]{2,1,0:T(8,128)} %collective-permute-done.7.xhigh), custom_call_target="tpu_custom_call" | custom-call | tf_op jit(solution)/shard_map/corners/pallas_call | solution.py:568
  40.9 1.2 %collective-permute-start.10 = (f32[8,8,512]{2,1,0:T(8,128)S(1)}, f32[8,8,512]{2,1,0:T(8,128)S(1)}, u32[]{:S(2)}, u32[]{:S(2)}) collective-permute-start(f32[8,8,512]{2,1,0:T(8,128)S(1)} %get-tuple-element.42), channel_id=1, source_target_pairs={{0,1},{1,2},{2,3},{3,4},{4,5},{5,6},{6,7},{7,8},{8,9},{9,10},{10,1... | collective-permute-start | bytes 393224 | tf_op jit(solution)/shard_map/ppermute | solution.py:576
  42.1 3.7 %collective-permute-start.11 = (f32[8,8,512]{2,1,0:T(8,128)S(1)}, f32[8,8,512]{2,1,0:T(8,128)S(1)}, u32[]{:S(2)}, u32[]{:S(2)}) collective-permute-start(f32[8,8,512]{2,1,0:T(8,128)S(1)} %get-tuple-element.43), channel_id=1, source_target_pairs={{0,31},{1,0},{2,1},{3,2},{4,3},{5,4},{6,5},{7,6},{8,7},{9,8},{10,9... | collective-permute-start | bytes 393224 | tf_op jit(solution)/shard_map/ppermute | solution.py:577
  45.8 0.0 collective-permute-done.hlow
  45.8 0.0 collective-permute-start.1
  45.8 4.4 %collective-permute-done.1.hhigh = f32[28,1024]{1,0:T(8,128)S(1)} collective-permute-done((f32[28,1024]{1,0:T(8,128)S(1)}, f32[28,1024]{1,0:T(8,128)S(1)}, u32[]{:S(2)}, u32[]{:S(2)}) %collective-permute-start.1) | collective-permute-done | bytes 114720 | tf_op jit(solution)/shard_map/ppermute | solution.py:599
  50.2 0.0 copy-done.2
  50.2 2.6 %membrane.1 = (f32[1,128]{1,0:T(1,128)S(1)}, f32[48,1024]{1,0:T(8,128)S(1)}, f32[48,1024]{1,0:T(8,128)S(1)}, f32[96,1024]{1,0:T(8,128)S(1)}, f32[96,1024]{1,0:T(...) custom-call(f32[48,1024]{1,0:T(8,128)S(1)} %get-tuple-element.26.members, ...), custom_call_target="tpu_custom_call" | custom-call | tf_op jit(solution)/shard_map/membrane/pallas_call | solution.py:601
  52.8 0.1 collective-permute-start.2
  52.9 1.1 %collective-permute-done.2 = f32[1,128]{1,0:T(1,128)S(1)} collective-permute-done((f32[1,128]{1,0:T(1,128)S(1)}, f32[1,128]{1,0:T(1,128)S(1)}, u32[]{:S(2)}, u32[]{:S(2)}) %collective-permute-start.2) | collective-permute-done | bytes 544 | tf_op jit(solution)/shard_map/ppermute | solution.py:618
  54.1 2.7 %collective-permute-start.5 = (f32[1,128]{1,0:T(1,128)S(1)}, f32[1,128]{1,0:T(1,128)S(1)}, u32[]{:S(2)}, u32[]{:S(2)}) collective-permute-start(f32[1,128]{1,0:T(1,128)S(1)} %add.3.share0), channel_id=1, source_target_pairs={{0,192},{32,224},{64,0},{96,32},{128,64},{160,96},{192,128},{224,1... | collective-permute-start | bytes 1544 | tf_op jit(solution)/shard_map/ppermute | solution.py:619
  56.7 0.0 collective-permute-done.8.ylow
  56.7 0.3 collective-permute-start.4
  57.0 0.0 collective-permute-done.9.yhigh
  57.1 0.3 collective-permute-start.3
  57.4 0.0 collective-permute-done.10.clow
  57.4 0.0 collective-permute-done.11.chigh
  57.4 0.0 copy-done
  57.4 0.0 copy-done.1
  57.4 7.3 %air_free.1 = (f32[16,32,512]{2,1,0:T(8,128)}, f32[16,32,512]{2,1,0:T(8,128)}) custom-call(f32[16,32,512]{2,1,0:T(8,128)S(1)} %copy-done, f32[16,32,512]{2,1,0:T(8,128)S(1)} %copy-done.1, f32[7,32,512]{2,1,0:T(8,128)S(1)} %collective-permute-done.6.xlow, f32[7,32,512]{2,1,0:T(8,128)} %collective-permute-done.7.xhigh, ...), custom_call_target="tpu_custom_call" | custom-call | flops 40000000 | bytes 8000000 | tf_op jit(solution)/shard_map/air_free/pallas_call | solution.py:580
  64.7 0.0 collective-permute-done.5.share3
  64.7 0.0 collective-permute-done.4.share2
  64.7 0.0 collective-permute-done.3.share1
  64.7 2.3 %finish.1 = (f32[16,32,512]{2,1,0:T(8,128)}, f32[16,32,512]{2,1,0:T(8,128)}, f32[16,32]{1,0:T(8,128)}, f32[16,32]{1,0:T(8,128)}) custom-call(f32[1,128]{1,0:T(1,128)S(1)} %add.3.share0, f32[1,128]{1,0:T(1,128)S(1)} %collective-permute-done.3.share1, f32[1,128]{1,0:T(1,128)S(1)} %collective-permute-done.4.share2, ...), custom_call_target="tpu_custom_call", output_to_operand_aliasing={{0}: (12, {}), {1}: (13, {})} | custom-call | tf_op jit(solution)/shard_map/finish/pallas_call | solution.py:620
  (1 shorter events, 0.0 us)
Async XLA Ops:
  3.9 46.3 %copy-start.2 = (s32[1024]{0:T(1024)S(1)}, s32[1024]{0:T(1024)}, u32[]{:S(2)}) copy-start(s32[1024]{0:T(1024)} %param.11) | copy-start | bytes 12292
  4.0 28.4 %all-to-all-start = ((f32[32,40,128]{2,1,0:T(8,128)}), f32[32,40,128]{2,1,0:T(8,128)S(1)}, u32[]{:S(2)}, u32[]{:S(2)}) async-start(f32[32,40,128]{2,1,0:T(8,128)} %get-tuple-element.25), calls=%async_computation | async-start | bytes 1310720 | tf_op jit(solution)/shard_map/all_to_all | solution.py:562
  16.0 23.9 %collective-permute-start.6 = (f32[7,32,512]{2,1,0:T(8,128)}, f32[7,32,512]{2,1,0:T(8,128)S(1)}, u32[]{:S(2)}, u32[]{:S(2)}) collective-permute-start(f32[7,32,512]{2,1,0:T(8,128)} %get-tuple-element.38), channel_id=1, source_target_pairs={{0,32},{32,64},{64,96},{96,128},{128,160},{160,192},{192,224},{224... | collective-permute-start | bytes 1376264 | tf_op jit(solution)/shard_map/ppermute | solution.py:564
  18.1 21.8 %collective-permute-start.7 = (f32[7,32,512]{2,1,0:T(8,128)}, f32[7,32,512]{2,1,0:T(8,128)}, u32[]{:S(2)}, u32[]{:S(2)}) collective-permute-start(f32[7,32,512]{2,1,0:T(8,128)} %get-tuple-element.39), channel_id=1, source_target_pairs={{0,224},{32,0},{64,32},{96,64},{128,96},{160,128},{192,160},{224,1... | collective-permute-start | bytes 1376264 | tf_op jit(solution)/shard_map/ppermute | solution.py:565
  18.1 38.6 %collective-permute-start.8 = (f32[16,8,512]{2,1,0:T(8,128)}, f32[16,8,512]{2,1,0:T(8,128)S(1)}, u32[]{:S(2)}, u32[]{:S(2)}) collective-permute-start(f32[16,8,512]{2,1,0:T(8,128)} %get-tuple-element.40), channel_id=1, source_target_pairs={{0,1},{1,2},{2,3},{3,4},{4,5},{5,6},{6,7},{7,8},{8,9},{9,10},{10,1... | collective-permute-start | bytes 786440 | tf_op jit(solution)/shard_map/ppermute | solution.py:566
  19.6 37.8 %copy-start = (f32[16,32,512]{2,1,0:T(8,128)S(1)}, f32[16,32,512]{2,1,0:T(8,128)}, u32[]{:S(2)}) copy-start(f32[16,32,512]{2,1,0:T(8,128)} %p.3) | copy-start | bytes 3145732
  19.6 37.8 %copy-start.1 = (f32[16,32,512]{2,1,0:T(8,128)S(1)}, f32[16,32,512]{2,1,0:T(8,128)}, u32[]{:S(2)}) copy-start(f32[16,32,512]{2,1,0:T(8,128)} %q.3) | copy-start | bytes 3145732
  19.6 37.5 %collective-permute-start.9 = (f32[16,8,512]{2,1,0:T(8,128)}, f32[16,8,512]{2,1,0:T(8,128)}, u32[]{:S(2)}, u32[]{:S(2)}) collective-permute-start(f32[16,8,512]{2,1,0:T(8,128)} %get-tuple-element.41), channel_id=1, source_target_pairs={{0,31},{1,0},{2,1},{3,2},{4,3},{5,4},{6,5},{7,6},{8,7},{9,8},{10,9... | collective-permute-start | bytes 786440 | tf_op jit(solution)/shard_map/ppermute | solution.py:567
  32.6 13.3 %collective-permute-start = (f32[28,1024]{1,0:T(8,128)S(1)}, f32[28,1024]{1,0:T(8,128)S(1)}, u32[]{:S(2)}, u32[]{:S(2)}) collective-permute-start(f32[28,1024]{1,0:T(8,128)S(1)} %get-tuple-element.28), channel_id=1, source_target_pairs={{0,32},{32,64},{64,96},{96,128},{128,160},{160,192},{192,224},{224... | collective-permute-start | bytes 344072 | tf_op jit(solution)/shard_map/ppermute | solution.py:598
  40.9 16.5 %collective-permute-start.10 = (f32[8,8,512]{2,1,0:T(8,128)S(1)}, f32[8,8,512]{2,1,0:T(8,128)S(1)}, u32[]{:S(2)}, u32[]{:S(2)}) collective-permute-start(f32[8,8,512]{2,1,0:T(8,128)S(1)} %get-tuple-element.42), channel_id=1, source_target_pairs={{0,1},{1,2},{2,3},{3,4},{4,5},{5,6},{6,7},{7,8},{8,9},{9,10},{10,1... | collective-permute-start | bytes 393224 | tf_op jit(solution)/shard_map/ppermute | solution.py:576
  42.1 15.3 %collective-permute-start.11 = (f32[8,8,512]{2,1,0:T(8,128)S(1)}, f32[8,8,512]{2,1,0:T(8,128)S(1)}, u32[]{:S(2)}, u32[]{:S(2)}) collective-permute-start(f32[8,8,512]{2,1,0:T(8,128)S(1)} %get-tuple-element.43), channel_id=1, source_target_pairs={{0,31},{1,0},{2,1},{3,2},{4,3},{5,4},{6,5},{7,6},{8,7},{9,8},{10,9... | collective-permute-start | bytes 393224 | tf_op jit(solution)/shard_map/ppermute | solution.py:577
  45.8 4.4 %collective-permute-start.1 = (f32[28,1024]{1,0:T(8,128)S(1)}, f32[28,1024]{1,0:T(8,128)S(1)}, u32[]{:S(2)}, u32[]{:S(2)}) collective-permute-start(f32[28,1024]{1,0:T(8,128)S(1)} %get-tuple-element.29), channel_id=1, source_target_pairs={{0,224},{32,0},{64,32},{96,64},{128,96},{160,128},{192,160},{224,1... | collective-permute-start | bytes 344072 | tf_op jit(solution)/shard_map/ppermute | solution.py:599
  52.8 1.2 %collective-permute-start.2 = (f32[1,128]{1,0:T(1,128)S(1)}, f32[1,128]{1,0:T(1,128)S(1)}, u32[]{:S(2)}, u32[]{:S(2)}) collective-permute-start(f32[1,128]{1,0:T(1,128)S(1)} %get-tuple-element.30), channel_id=1, source_target_pairs={{0,32},{32,0},{64,96},{96,64},{128,160},{160,128},{192,224},{224,1... | collective-permute-start | bytes 1544 | tf_op jit(solution)/shard_map/ppermute | solution.py:618
  54.1 10.6 %collective-permute-start.5 = (f32[1,128]{1,0:T(1,128)S(1)}, f32[1,128]{1,0:T(1,128)S(1)}, u32[]{:S(2)}, u32[]{:S(2)}) collective-permute-start(f32[1,128]{1,0:T(1,128)S(1)} %add.3.share0), channel_id=1, source_target_pairs={{0,192},{32,224},{64,0},{96,32},{128,64},{160,96},{192,128},{224,1... | collective-permute-start | bytes 1544 | tf_op jit(solution)/shard_map/ppermute | solution.py:619
  56.7 8.0 %collective-permute-start.4 = (f32[1,128]{1,0:T(1,128)S(1)}, f32[1,128]{1,0:T(1,128)S(1)}, u32[]{:S(2)}, u32[]{:S(2)}) collective-permute-start(f32[1,128]{1,0:T(1,128)S(1)} %add.3.share0), channel_id=1, source_target_pairs={{0,128},{32,160},{64,192},{96,224},{128,0},{160,32},{192,64},{224,... | collective-permute-start | bytes 1544 | tf_op jit(solution)/shard_map/ppermute | solution.py:619
  57.1 7.7 %collective-permute-start.3 = (f32[1,128]{1,0:T(1,128)S(1)}, f32[1,128]{1,0:T(1,128)S(1)}, u32[]{:S(2)}, u32[]{:S(2)}) collective-permute-start(f32[1,128]{1,0:T(1,128)S(1)} %add.3.share0), channel_id=1, source_target_pairs={{0,64},{32,96},{64,128},{96,160},{128,192},{160,224},{192,0},{224,... | collective-permute-start | bytes 1544 | tf_op jit(solution)/shard_map/ppermute | solution.py:619

commit v3 on v2

--- a/solution.py
+++ b/solution.py
@@ -125,7 +125,7 @@
             corner_high[at] = jnp.where(lower, pltpu.roll(halo[j, 24:32], 4, 0), halo[i, 24:32])
 
 
-def unfold_kernel(blocks, members, jumps, to_low, to_high):
+def unfold_kernel(blocks, after, members, jumps, to_low, to_high):
     quarter = lanes((FOLD, 128)) // 32
     for g in range(4):
         for t in range(8):
@@ -158,7 +158,7 @@
     return jnp.broadcast_to(edge.astype(jnp.int32), shape) == 0
 
 
-def air_kernel(p, q, xlow, xhigh, ylow, yhigh, clow, chigh, out_next, out_last, a, b, sems):
+def air_kernel(p, q, xlow, xhigh, ylow, yhigh, clow, chigh, out_next, out_last, done, a, b, sems):
     tall = lax.axis_index("gx")
     wide = lax.axis_index("gy")
     first, last = tall == 0, tall == GX - 1
@@ -259,6 +259,7 @@
     sent = sent + results(a, out_next, 12)
     for copy in sent[4:]:
         copy.start()
+    done[...] = jnp.zeros((8, 128), jnp.float32)
     for copy in sent:
         copy.wait()
 
@@ -577,11 +578,11 @@
     chigh = lax.ppermute(to_clow, "gy", ring(GY, -1))
     air = f32(BX, BY, NZ)
     brick = VMEM((4, XE, YE, 128), jnp.float32)
-    next_free, last_free = pl.pallas_call(
+    next_free, last_free, done = pl.pallas_call(
         air_kernel,
-        out_shape=(air, air),
+        out_shape=(air, air, f32(8, 128)),
         in_specs=[HBM, HBM] + [WHOLE] * 6,
-        out_specs=(HBM, HBM),
+        out_specs=(HBM, HBM, WHOLE),
         scratch_shapes=[brick, brick, sems(16)],
         compiler_params=granted(8),
         cost_estimate=pl.CostEstimate(flops=40_000_000, bytes_accessed=8_000_000, transcendentals=0),
@@ -590,11 +591,11 @@
     members, jumps, to_low, to_high = pl.pallas_call(
         unfold_kernel,
         out_shape=(f32(48, COLS), f32(112, WINDOW), stripe, stripe),
-        in_specs=[WHOLE],
+        in_specs=[WHOLE, ANY],
         out_specs=(WHOLE,) * 4,
         compiler_params=granted(3),
         name="unfold",
-    )(blocks)
+    )(blocks, done)
     hlow = lax.ppermute(to_high, "gx", ring(GX, 1))
     hhigh = lax.ppermute(to_low, "gx", ring(GX, -1))
     listed = air_row.reshape(1, COLS)

time: 67.6 us -> 69.9 us (1.034)
  waiting for transfers between devices: 14.8 us -> 24.1 us
  starting transfers between devices: 34.8 us -> 30.2 us
  Pallas kernels: 16.7 us -> 14.7 us
    all_to_all x1, waiting for transfers between devices: 9.28 us -> 0.01 us  [per_device(): blocks = lax.all_to_all(block, 'gy', 0, 0)]
    ppermute x1, waiting for transfers between devices: 0.01 us -> 9 us  [per_device(): ylow = lax.ppermute(to_yhigh, 'gy', ring(GY, 1))]
    ppermute x1, starting transfers between devices: 7.34 us -> 2.55 us  [per_device(): hlow = lax.ppermute(to_high, 'gx', ring(GX, 1))]
    ppermute x3, waiting for transfers between devices: 0.01 us -> 3.29 us  [per_device(): lax.ppermute(sums, 'gx', across(GX, by))]
    ppermute x1, waiting for transfers between devices: 0.01 us -> 2.81 us  [per_device(): clow = lax.ppermute(to_chigh, 'gy', ring(GY, 1))]
    ppermute x1, waiting for transfers between devices: 0.01 us -> 2.67 us  [per_device(): xhigh = lax.ppermute(to_xlow, 'gx', ring(GX, -1))]
    ppermute x1, waiting for transfers between devices: 4.39 us -> 2.44 us  [per_device(): hhigh = lax.ppermute(to_low, 'gx', ring(GX, -1))]
    ppermute x1, waiting for transfers between devices: 0.01 us -> 1.94 us  [per_device(): hlow = lax.ppermute(to_high, 'gx', ring(GX, 1))]
  transfers between devices with their start and end apart: 13 -> 13, of which waited for: 3 -> 9; matrix products, arithmetic and copies ran while one was open for 0% -> 0% of each run, Pallas kernels for 17% -> 9%
where the time goes in v3:
time: 69.9 us; the launch traced here: 69.7 us
  starting transfers between devices  30.2 us (43%)
  waiting for transfers between devices  24.1 us (34%)
  Pallas kernels  14.7 us (21%)
  between operations  0.72 us (1%)
    all_to_all x1, starting transfers between devices, per_device(): blocks = lax.all_to_all(block, 'gy', 0, 0)  12.2 us
    ppermute x1, waiting for transfers between devices, per_device(): ylow = lax.ppermute(to_yhigh, 'gy', ring(GY, 1))  9 us
    pallas_call x1, Pallas kernels, per_device(): pl.pallas_call(air_kernel, out_shape=(air, air, f32(8, 128)), in_specs=[H...  6.2 us
    ppermute x1, starting transfers between devices, per_device(): chigh = lax.ppermute(to_clow, 'gy', ring(GY, -1))  3.5 us
    ppermute x1, starting transfers between devices, per_device(): yhigh = lax.ppermute(to_ylow, 'gy', ring(GY, -1))  3.42 us
    ppermute x3, starting transfers between devices, per_device(): lax.ppermute(sums, 'gx', across(GX, by))  3.31 us
    pallas_call x1, Pallas kernels, per_device(): pl.pallas_call(pack_kernel, out_shape=(halo_x, halo_x, halo_y, halo_y, f3...  3.31 us
    ppermute x3, waiting for transfers between devices, per_device(): lax.ppermute(sums, 'gx', across(GX, by))  3.29 us
  transfers between devices with their start and end apart: 13, of which 9 were waited for; matrix products, arithmetic and copies ran while one was open for 0% of the time, Pallas kernels for 9%

profile of v3, /device:TPU:1, one launch (start us, length us, event | category | flops | bytes accessed | tf_op | source)
XLA Modules:
  0.0 69.7 jit_solution(6984810769633253302)
XLA Ops:
  0.6 3.3 %pack.1 = (f32[7,32,512]{2,1,0:T(8,128)}, f32[7,32,512]{2,1,0:T(8,128)}, f32[16,8,512]{2,1,0:T(8,128)}, f32[16,8,512]{2,1,0:T(8,128)}, f32[32,40,128]{2,1,0:T(8,128)}) custom-call(f32[16,32,512]{2,1,0:T(8,128)} %p.3, f32[16,32,512]{2,1,0:T(8,128)} %q.3, f32[16,32]{1,0:T(8,128)} %u.1, f32[16,32]{1,0:T(8,128)} %w.1, f32[16,32]{1,0:T(8,128)} %m.1), custom_call_target="tpu_custom_call" | custom-call | tf_op jit(solution)/shard_map/pack/pallas_call | solution.py:544
  3.9 0.0 copy-start
  4.0 0.0 copy-start.1
  4.0 12.2 %all-to-all-start = ((f32[32,40,128]{2,1,0:T(8,128)}), f32[32,40,128]{2,1,0:T(8,128)S(1)}, u32[]{:S(2)}, u32[]{:S(2)}) async-start(f32[32,40,128]{2,1,0:T(8,128)} %get-tuple-element.26), calls=%async_computation | async-start | bytes 1310720 | tf_op jit(solution)/shard_map/all_to_all | solution.py:563
  16.2 2.1 %collective-permute-start = (f32[7,32,512]{2,1,0:T(8,128)}, f32[7,32,512]{2,1,0:T(8,128)S(1)}, u32[]{:S(2)}, u32[]{:S(2)}) collective-permute-start(f32[7,32,512]{2,1,0:T(8,128)} %get-tuple-element.27), channel_id=1, source_target_pairs={{0,32},{32,64},{64,96},{96,128},{128,160},{160,192},{192,224},{224... | collective-permute-start | bytes 1376264 | tf_op jit(solution)/shard_map/ppermute | solution.py:565
  18.2 0.0 collective-permute-start.1
  18.2 1.5 %collective-permute-start.2 = (f32[16,8,512]{2,1,0:T(8,128)}, f32[16,8,512]{2,1,0:T(8,128)S(1)}, u32[]{:S(2)}, u32[]{:S(2)}) collective-permute-start(f32[16,8,512]{2,1,0:T(8,128)} %get-tuple-element.29), channel_id=1, source_target_pairs={{0,1},{1,2},{2,3},{3,4},{4,5},{5,6},{6,7},{7,8},{8,9},{9,10},{10,1... | collective-permute-start | bytes 786440 | tf_op jit(solution)/shard_map/ppermute | solution.py:567
  19.7 3.4 %collective-permute-start.3 = (f32[16,8,512]{2,1,0:T(8,128)}, f32[16,8,512]{2,1,0:T(8,128)S(1)}, u32[]{:S(2)}, u32[]{:S(2)}) collective-permute-start(f32[16,8,512]{2,1,0:T(8,128)} %get-tuple-element.30), channel_id=1, source_target_pairs={{0,31},{1,0},{2,1},{3,2},{4,3},{5,4},{6,5},{7,6},{8,7},{9,8},{10,9... | collective-permute-start | bytes 786440 | tf_op jit(solution)/shard_map/ppermute | solution.py:568
  23.2 0.8 %collective-permute-done.xlow = f32[7,32,512]{2,1,0:T(8,128)S(1)} collective-permute-done((f32[7,32,512]{2,1,0:T(8,128)}, f32[7,32,512]{2,1,0:T(8,128)S(1)}, u32[]{:S(2)}, u32[]{:S(2)}) %collective-permute-start) | collective-permute-done | bytes 458784 | tf_op jit(solution)/shard_map/ppermute | solution.py:565
  24.0 2.7 %collective-permute-done.1.xhigh = f32[7,32,512]{2,1,0:T(8,128)S(1)} collective-permute-done((f32[7,32,512]{2,1,0:T(8,128)}, f32[7,32,512]{2,1,0:T(8,128)S(1)}, u32[]{:S(2)}, u32[]{:S(2)}) %collective-permute-start.1) | collective-permute-done | bytes 458784 | tf_op jit(solution)/shard_map/ppermute | solution.py:566
  26.7 1.6 %collective-permute-start.4 = (f32[8,8,512]{2,1,0:T(8,128)S(1)}, f32[8,8,512]{2,1,0:T(8,128)S(1)}, u32[]{:S(2)}, u32[]{:S(2)}) collective-permute-start(f32[8,8,512]{2,1,0:T(8,128)S(1)} %get-tuple-element.31), channel_id=1, source_target_pairs={{0,1},{1,2},{2,3},{3,4},{4,5},{5,6},{6,7},{7,8},{8,9},{9,10},{10,1... | collective-permute-start | bytes 393224 | tf_op jit(solution)/shard_map/ppermute | solution.py:577
  28.3 3.5 %collective-permute-start.5 = (f32[8,8,512]{2,1,0:T(8,128)S(1)}, f32[8,8,512]{2,1,0:T(8,128)S(1)}, u32[]{:S(2)}, u32[]{:S(2)}) collective-permute-start(f32[8,8,512]{2,1,0:T(8,128)S(1)} %get-tuple-element.32), channel_id=1, source_target_pairs={{0,31},{1,0},{2,1},{3,2},{4,3},{5,4},{6,5},{7,6},{8,7},{9,8},{10,9... | collective-permute-start | bytes 393224 | tf_op jit(solution)/shard_map/ppermute | solution.py:578
  31.8 9.0 %collective-permute-done.2.ylow = f32[16,8,512]{2,1,0:T(8,128)S(1)} collective-permute-done((f32[16,8,512]{2,1,0:T(8,128)}, f32[16,8,512]{2,1,0:T(8,128)S(1)}, u32[]{:S(2)}, u32[]{:S(2)}) %collective-permute-start.2) | collective-permute-done | bytes 262176 | tf_op jit(solution)/shard_map/ppermute | solution.py:567
  40.8 0.0 collective-permute-done.3.yhigh
  40.8 2.8 %collective-permute-done.4.clow = f32[8,8,512]{2,1,0:T(8,128)S(1)} collective-permute-done((f32[8,8,512]{2,1,0:T(8,128)S(1)}, f32[8,8,512]{2,1,0:T(8,128)S(1)}, u32[]{:S(2)}, u32[]{:S(2)}) %collective-permute-start.4) | collective-permute-done | bytes 131104 | tf_op jit(solution)/shard_map/ppermute | solution.py:577
  43.6 0.0 collective-permute-done.5.chigh
  43.6 0.0 copy-done
  43.6 0.0 copy-done.1
  43.6 6.2 %air_free.1 = (f32[16,32,512]{2,1,0:T(8,128)}, f32[16,32,512]{2,1,0:T(8,128)}, f32[8,128]{1,0:T(8,128)S(1)}) custom-call(f32[16,32,512]{2,1,0:T(8,128)S(1)} %copy-done, f32[16,32,512]{2,1,0:T(8,128)S(1)} %copy-done.1, f32[7,32,512]{2,1,0:T(8,128)S(1)} %collective-permute-done.xlow, f32[7,32,512]{2,1,0:T(8,128)S(1)} %collective-permute-done.1.xhigh, ...), custom_call_target="tpu_custom_call" | custom-call | flops 40000000 | bytes 8000000 | tf_op jit(solution)/shard_map/air_free/pallas_call | solution.py:581
  49.8 0.0 all-to-all-done.blocks
  49.8 0.2 unfold.1
  50.0 0.0 copy-start.2
  50.0 2.5 %collective-permute-start.6 = (f32[28,1024]{1,0:T(8,128)S(1)}, f32[28,1024]{1,0:T(8,128)S(1)}, u32[]{:S(2)}, u32[]{:S(2)}) collective-permute-start(f32[28,1024]{1,0:T(8,128)S(1)} %get-tuple-element.36), channel_id=1, source_target_pairs={{0,32},{32,64},{64,96},{96,128},{128,160},{160,192},{192,224},{224... | collective-permute-start | bytes 344072 | tf_op jit(solution)/shard_map/ppermute | solution.py:599
  52.5 0.0 collective-permute-start.7
  52.5 1.9 %collective-permute-done.6.hlow = f32[28,1024]{1,0:T(8,128)S(1)} collective-permute-done((f32[28,1024]{1,0:T(8,128)S(1)}, f32[28,1024]{1,0:T(8,128)S(1)}, u32[]{:S(2)}, u32[]{:S(2)}) %collective-permute-start.6) | collective-permute-done | bytes 114720 | tf_op jit(solution)/shard_map/ppermute | solution.py:599
  54.5 2.4 %collective-permute-done.7.hhigh = f32[28,1024]{1,0:T(8,128)S(1)} collective-permute-done((f32[28,1024]{1,0:T(8,128)S(1)}, f32[28,1024]{1,0:T(8,128)S(1)}, u32[]{:S(2)}, u32[]{:S(2)}) %collective-permute-start.7) | collective-permute-done | bytes 114720 | tf_op jit(solution)/shard_map/ppermute | solution.py:600
  56.9 0.0 copy-done.2
  56.9 2.7 %membrane.1 = (f32[1,128]{1,0:T(1,128)S(1)}, f32[48,1024]{1,0:T(8,128)S(1)}, f32[48,1024]{1,0:T(8,128)S(1)}, f32[96,1024]{1,0:T(8,128)S(1)}, f32[96,1024]{1,0:T(...) custom-call(f32[48,1024]{1,0:T(8,128)S(1)} %get-tuple-element.34.members, ...), custom_call_target="tpu_custom_call" | custom-call | tf_op jit(solution)/shard_map/membrane/pallas_call | solution.py:602
  59.6 0.1 collective-permute-start.8
  59.7 1.1 %collective-permute-done.8 = f32[1,128]{1,0:T(1,128)S(1)} collective-permute-done((f32[1,128]{1,0:T(1,128)S(1)}, f32[1,128]{1,0:T(1,128)S(1)}, u32[]{:S(2)}, u32[]{:S(2)}) %collective-permute-start.8) | collective-permute-done | bytes 544 | tf_op jit(solution)/shard_map/ppermute | solution.py:619
  60.8 2.2 %collective-permute-start.11 = (f32[1,128]{1,0:T(1,128)S(1)}, f32[1,128]{1,0:T(1,128)S(1)}, u32[]{:S(2)}, u32[]{:S(2)}) collective-permute-start(f32[1,128]{1,0:T(1,128)S(1)} %add.3.share0), channel_id=1, source_target_pairs={{0,192},{32,224},{64,0},{96,32},{128,64},{160,96},{192,128},{224,1... | collective-permute-start | bytes 1544 | tf_op jit(solution)/shard_map/ppermute | solution.py:620
  63.0 0.8 %collective-permute-start.10 = (f32[1,128]{1,0:T(1,128)S(1)}, f32[1,128]{1,0:T(1,128)S(1)}, u32[]{:S(2)}, u32[]{:S(2)}) collective-permute-start(f32[1,128]{1,0:T(1,128)S(1)} %add.3.share0), channel_id=1, source_target_pairs={{0,128},{32,160},{64,192},{96,224},{128,0},{160,32},{192,64},{224,... | collective-permute-start | bytes 1544 | tf_op jit(solution)/shard_map/ppermute | solution.py:620
  63.8 0.3 collective-permute-start.9
  64.1 0.0 collective-permute-done.11.share3
  64.1 2.7 %collective-permute-done.10.share2 = f32[1,128]{1,0:T(1,128)S(1)} collective-permute-done((f32[1,128]{1,0:T(1,128)S(1)}, f32[1,128]{1,0:T(1,128)S(1)}, u32[]{:S(2)}, u32[]{:S(2)}) %collective-permute-start.10) | collective-permute-done | bytes 544 | tf_op jit(solution)/shard_map/ppermute | solution.py:620
  66.9 0.5 collective-permute-done.9.share1
  67.4 2.3 %finish.1 = (f32[16,32,512]{2,1,0:T(8,128)}, f32[16,32,512]{2,1,0:T(8,128)}, f32[16,32]{1,0:T(8,128)}, f32[16,32]{1,0:T(8,128)}) custom-call(f32[1,128]{1,0:T(1,128)S(1)} %add.3.share0, f32[1,128]{1,0:T(1,128)S(1)} %collective-permute-done.9.share1, f32[1,128]{1,0:T(1,128)S(1)} %collective-permute-done.10.share2, ...), custom_call_target="tpu_custom_call", output_to_operand_aliasing={{0}: (12, {}), {1}: (13, {})} | custom-call | tf_op jit(solution)/shard_map/finish/pallas_call | solution.py:621
  (2 shorter events, 0.0 us)
Async XLA Ops:
  3.9 39.6 %copy-start = (f32[16,32,512]{2,1,0:T(8,128)S(1)}, f32[16,32,512]{2,1,0:T(8,128)}, u32[]{:S(2)}) copy-start(f32[16,32,512]{2,1,0:T(8,128)} %p.3) | copy-start | bytes 3145732
  4.0 39.6 %copy-start.1 = (f32[16,32,512]{2,1,0:T(8,128)S(1)}, f32[16,32,512]{2,1,0:T(8,128)}, u32[]{:S(2)}) copy-start(f32[16,32,512]{2,1,0:T(8,128)} %q.3) | copy-start | bytes 3145732
  4.0 45.8 %all-to-all-start = ((f32[32,40,128]{2,1,0:T(8,128)}), f32[32,40,128]{2,1,0:T(8,128)S(1)}, u32[]{:S(2)}, u32[]{:S(2)}) async-start(f32[32,40,128]{2,1,0:T(8,128)} %get-tuple-element.26), calls=%async_computation | async-start | bytes 1310720 | tf_op jit(solution)/shard_map/all_to_all | solution.py:563
  16.2 7.8 %collective-permute-start = (f32[7,32,512]{2,1,0:T(8,128)}, f32[7,32,512]{2,1,0:T(8,128)S(1)}, u32[]{:S(2)}, u32[]{:S(2)}) collective-permute-start(f32[7,32,512]{2,1,0:T(8,128)} %get-tuple-element.27), channel_id=1, source_target_pairs={{0,32},{32,64},{64,96},{96,128},{128,160},{160,192},{192,224},{224... | collective-permute-start | bytes 1376264 | tf_op jit(solution)/shard_map/ppermute | solution.py:565
  18.2 8.4 %collective-permute-start.1 = (f32[7,32,512]{2,1,0:T(8,128)}, f32[7,32,512]{2,1,0:T(8,128)S(1)}, u32[]{:S(2)}, u32[]{:S(2)}) collective-permute-start(f32[7,32,512]{2,1,0:T(8,128)} %get-tuple-element.28), channel_id=1, source_target_pairs={{0,224},{32,0},{64,32},{96,64},{128,96},{160,128},{192,160},{224,1... | collective-permute-start | bytes 1376264 | tf_op jit(solution)/shard_map/ppermute | solution.py:566
  18.2 22.5 %collective-permute-start.2 = (f32[16,8,512]{2,1,0:T(8,128)}, f32[16,8,512]{2,1,0:T(8,128)S(1)}, u32[]{:S(2)}, u32[]{:S(2)}) collective-permute-start(f32[16,8,512]{2,1,0:T(8,128)} %get-tuple-element.29), channel_id=1, source_target_pairs={{0,1},{1,2},{2,3},{3,4},{4,5},{5,6},{6,7},{7,8},{8,9},{9,10},{10,1... | collective-permute-start | bytes 786440 | tf_op jit(solution)/shard_map/ppermute | solution.py:567
  19.7 21.0 %collective-permute-start.3 = (f32[16,8,512]{2,1,0:T(8,128)}, f32[16,8,512]{2,1,0:T(8,128)S(1)}, u32[]{:S(2)}, u32[]{:S(2)}) collective-permute-start(f32[16,8,512]{2,1,0:T(8,128)} %get-tuple-element.30), channel_id=1, source_target_pairs={{0,31},{1,0},{2,1},{3,2},{4,3},{5,4},{6,5},{7,6},{8,7},{9,8},{10,9... | collective-permute-start | bytes 786440 | tf_op jit(solution)/shard_map/ppermute | solution.py:568
  26.7 16.9 %collective-permute-start.4 = (f32[8,8,512]{2,1,0:T(8,128)S(1)}, f32[8,8,512]{2,1,0:T(8,128)S(1)}, u32[]{:S(2)}, u32[]{:S(2)}) collective-permute-start(f32[8,8,512]{2,1,0:T(8,128)S(1)} %get-tuple-element.31), channel_id=1, source_target_pairs={{0,1},{1,2},{2,3},{3,4},{4,5},{5,6},{6,7},{7,8},{8,9},{9,10},{10,1... | collective-permute-start | bytes 393224 | tf_op jit(solution)/shard_map/ppermute | solution.py:577
  28.3 15.3 %collective-permute-start.5 = (f32[8,8,512]{2,1,0:T(8,128)S(1)}, f32[8,8,512]{2,1,0:T(8,128)S(1)}, u32[]{:S(2)}, u32[]{:S(2)}) collective-permute-start(f32[8,8,512]{2,1,0:T(8,128)S(1)} %get-tuple-element.32), channel_id=1, source_target_pairs={{0,31},{1,0},{2,1},{3,2},{4,3},{5,4},{6,5},{7,6},{8,7},{9,8},{10,9... | collective-permute-start | bytes 393224 | tf_op jit(solution)/shard_map/ppermute | solution.py:578
  50.0 7.0 %copy-start.2 = (s32[1024]{0:T(1024)S(1)}, s32[1024]{0:T(1024)}, u32[]{:S(2)}) copy-start(s32[1024]{0:T(1024)} %param.11) | copy-start | bytes 12292
  50.0 4.5 %collective-permute-start.6 = (f32[28,1024]{1,0:T(8,128)S(1)}, f32[28,1024]{1,0:T(8,128)S(1)}, u32[]{:S(2)}, u32[]{:S(2)}) collective-permute-start(f32[28,1024]{1,0:T(8,128)S(1)} %get-tuple-element.36), channel_id=1, source_target_pairs={{0,32},{32,64},{64,96},{96,128},{128,160},{160,192},{192,224},{224... | collective-permute-start | bytes 344072 | tf_op jit(solution)/shard_map/ppermute | solution.py:599
  52.5 4.4 %collective-permute-start.7 = (f32[28,1024]{1,0:T(8,128)S(1)}, f32[28,1024]{1,0:T(8,128)S(1)}, u32[]{:S(2)}, u32[]{:S(2)}) collective-permute-start(f32[28,1024]{1,0:T(8,128)S(1)} %get-tuple-element.37), channel_id=1, source_target_pairs={{0,224},{32,0},{64,32},{96,64},{128,96},{160,128},{192,160},{224,1... | collective-permute-start | bytes 344072 | tf_op jit(solution)/shard_map/ppermute | solution.py:600
  59.6 1.2 %collective-permute-start.8 = (f32[1,128]{1,0:T(1,128)S(1)}, f32[1,128]{1,0:T(1,128)S(1)}, u32[]{:S(2)}, u32[]{:S(2)}) collective-permute-start(f32[1,128]{1,0:T(1,128)S(1)} %get-tuple-element.38), channel_id=1, source_target_pairs={{0,32},{32,0},{64,96},{96,64},{128,160},{160,128},{192,224},{224,1... | collective-permute-start | bytes 1544 | tf_op jit(solution)/shard_map/ppermute | solution.py:619
  60.8 3.3 %collective-permute-start.11 = (f32[1,128]{1,0:T(1,128)S(1)}, f32[1,128]{1,0:T(1,128)S(1)}, u32[]{:S(2)}, u32[]{:S(2)}) collective-permute-start(f32[1,128]{1,0:T(1,128)S(1)} %add.3.share0), channel_id=1, source_target_pairs={{0,192},{32,224},{64,0},{96,32},{128,64},{160,96},{192,128},{224,1... | collective-permute-start | bytes 1544 | tf_op jit(solution)/shard_map/ppermute | solution.py:620
  63.0 3.9 %collective-permute-start.10 = (f32[1,128]{1,0:T(1,128)S(1)}, f32[1,128]{1,0:T(1,128)S(1)}, u32[]{:S(2)}, u32[]{:S(2)}) collective-permute-start(f32[1,128]{1,0:T(1,128)S(1)} %add.3.share0), channel_id=1, source_target_pairs={{0,128},{32,160},{64,192},{96,224},{128,0},{160,32},{192,64},{224,... | collective-permute-start | bytes 1544 | tf_op jit(solution)/shard_map/ppermute | solution.py:620
  63.8 3.6 %collective-permute-start.9 = (f32[1,128]{1,0:T(1,128)S(1)}, f32[1,128]{1,0:T(1,128)S(1)}, u32[]{:S(2)}, u32[]{:S(2)}) collective-permute-start(f32[1,128]{1,0:T(1,128)S(1)} %add.3.share0), channel_id=1, source_target_pairs={{0,64},{32,96},{64,128},{96,160},{128,192},{160,224},{192,0},{224,... | collective-permute-start | bytes 1544 | tf_op jit(solution)/shard_map/ppermute | solution.py:620

commit v4 on v2

--- a/solution.py
+++ b/solution.py
@@ -58,8 +58,8 @@
 
 
 def pack_kernel(
-    p, q, u, w, m, xlow, xhigh, ylow, yhigh, block,
-    edges, sides, tips, copied, planes, members, turned, rows, sems,
+    p, q, u, w, m, xlow, xhigh, block,
+    tips, copied, planes, members, turned, rows, sems,
 ):
     wide = lax.axis_index("gy")
 
@@ -71,7 +71,6 @@
 
     mids = started([(x.at[:, :, MID - 128 : MID + 128], planes.at[i]) for i, x in enumerate((p, q))], 0)
     own = started([(x, members.at[i]) for i, x in enumerate((u, w, m))], 2)
-    ins = started([(x.at[:, at : at + 8], edges.at[i]) for i, (x, at) in enumerate(((p, 0), (q, 0), (p, 24), (q, 24)))], 5)
     ends = started(
         [
             (p.at[0:4], tips.at[0, 0:4]),
@@ -79,7 +78,7 @@
             (p.at[12:16], tips.at[1, 0:4]),
             (q.at[13:16], tips.at[1, 4:7]),
         ],
-        9,
+        5,
     )
     lane = lanes((BY, 128))
     for i in range(2):
@@ -102,27 +101,26 @@
     folded = fold(rows, wide)
     for i in range(GY):
         copied[i] = folded
-    sent = started([(copied, block)], 13)
-    lower = sublanes((8, NZ)) < 4
-    for copy in ins:
-        copy.wait()
-    for r in range(BX):
-        sides[0, r] = jnp.where(lower, edges[0, r], pltpu.roll(edges[1, r], 4, 0))
-        sides[1, r] = jnp.where(lower, pltpu.roll(edges[3, r], 4, 0), edges[2, r])
-    sent += started([(sides.at[0], ylow), (sides.at[1], yhigh)], 14)
+    sent = started([(copied, block)], 9)
     for copy in ends:
         copy.wait()
-    sent += started([(tips.at[0], xlow), (tips.at[1], xhigh)], 16)
+    sent += started([(tips.at[0], xlow), (tips.at[1], xhigh)], 10)
     for copy in sent:
         copy.wait()
 
 
-def corner_kernel(xlow, xhigh, corner_low, corner_high):
+def sides_kernel(p, q, xlow, xhigh, ylow, yhigh):
     lower = sublanes((8, NZ)) < 4
+
+    def row(r, pt, qt):
+        ylow[r] = jnp.where(lower, pt[0:8], pltpu.roll(qt[0:8], 4, 0))
+        yhigh[r] = jnp.where(lower, pltpu.roll(qt[24:32], 4, 0), pt[24:32])
+
+    for r in range(BX):
+        row(4 + r, p.at[r], q.at[r])
     for i in range(4):
-        for at, halo, j in ((i, xlow, 4 + max(i - 1, 0)), (4 + i, xhigh, 4 + min(i, 2))):
-            corner_low[at] = jnp.where(lower, halo[i, 0:8], pltpu.roll(halo[j, 0:8], 4, 0))
-            corner_high[at] = jnp.where(lower, pltpu.roll(halo[j, 24:32], 4, 0), halo[i, 24:32])
+        row(i, xlow.at[i], xlow.at[4 + max(i - 1, 0)])
+        row(20 + i, xhigh.at[i], xhigh.at[4 + min(i, 2)])
 
 
 def unfold_kernel(blocks, members, jumps, to_low, to_high):
@@ -158,7 +156,7 @@
     return jnp.broadcast_to(edge.astype(jnp.int32), shape) == 0
 
 
-def air_kernel(p, q, xlow, xhigh, ylow, yhigh, clow, chigh, out_next, out_last, a, b, sems):
+def air_kernel(p, q, xlow, xhigh, ylow, yhigh, out_next, out_last, a, b, sems):
     tall = lax.axis_index("gx")
     wide = lax.axis_index("gy")
     first, last = tall == 0, tall == GX - 1
@@ -180,13 +178,11 @@
             b[k, 1 + i, 8:40] = jnp.where(inner_low, xlow[4 + i, :, layers[k]], 0.0)
             b[k, 20 + i, 8:40] = jnp.where(inner_high, xhigh[4 + i, :, layers[k]], 0.0)
         for r in range(XE):
-            if 4 <= r < 20:
-                lo, hi = ylow[r - 4, :, layers[k]], yhigh[r - 4, :, layers[k]]
-            else:
-                i = r if r < 4 else r - 16
+            lo, hi = ylow[r, :, layers[k]], yhigh[r, :, layers[k]]
+            if r < 4 or r >= 20:
                 free = (inner_low if r < 4 else inner_high)[0:8]
-                lo = jnp.where(free, clow[i, :, layers[k]], 0.0)
-                hi = jnp.where(free, chigh[i, :, layers[k]], 0.0)
+                lo = jnp.where(free, lo, 0.0)
+                hi = jnp.where(free, hi, 0.0)
             lo = jnp.where(tile_low, lo, 0.0)
             hi = jnp.where(tile_high, hi, 0.0)
             a[k, r, 0:8] = lo
@@ -539,54 +535,27 @@
     def sems(n):
         return pltpu.SemaphoreType.DMA((n,))
 
-    halo_x, halo_y, corner, stripe = f32(7, BY, NZ), f32(BX, 8, NZ), f32(8, 8, NZ), f32(28, COLS)
-    *sends, block = pl.pallas_call(
+    halo_x, halo_y, stripe = f32(7, BY, NZ), f32(XE, 8, NZ), f32(28, COLS)
+    to_xlow, to_xhigh, block = pl.pallas_call(
         pack_kernel,
-        out_shape=(halo_x, halo_x, halo_y, halo_y, f32(GY, FOLD, 128)),
+        out_shape=(halo_x, halo_x, f32(GY, FOLD, 128)),
         in_specs=[HBM] * 5,
-        out_specs=(HBM,) * 5,
+        out_specs=(HBM,) * 3,
         scratch_shapes=[
-            VMEM((4, BX, 8, NZ), jnp.float32),
-            VMEM((2, BX, 8, NZ), jnp.float32),
             VMEM((2, 7, BY, NZ), jnp.float32),
             VMEM((GY, FOLD, 128), jnp.float32),
             VMEM((2, BX, BY, 256), jnp.float32),
             VMEM((3, BX, BY), jnp.float32),
             VMEM((2, 128, 128), jnp.float32),
             VMEM((PACK, 128), jnp.float32),
-            sems(18),
+            sems(12),
         ],
         compiler_params=granted(63),
         name="pack",
     )(air_now, air_prev, membrane_now, membrane_prev, inv_mass)
     blocks = lax.all_to_all(block, "gy", 0, 0)
-    to_xlow, to_xhigh, to_ylow, to_yhigh = sends
     xlow = lax.ppermute(to_xhigh, "gx", ring(GX, 1))
     xhigh = lax.ppermute(to_xlow, "gx", ring(GX, -1))
-    ylow = lax.ppermute(to_yhigh, "gy", ring(GY, 1))
-    yhigh = lax.ppermute(to_ylow, "gy", ring(GY, -1))
-    to_clow, to_chigh = pl.pallas_call(
-        corner_kernel,
-        out_shape=(corner, corner),
-        in_specs=[WHOLE] * 2,
-        out_specs=(WHOLE,) * 2,
-        compiler_params=granted(3),
-        name="corners",
-    )(xlow, xhigh)
-    clow = lax.ppermute(to_chigh, "gy", ring(GY, 1))
-    chigh = lax.ppermute(to_clow, "gy", ring(GY, -1))
-    air = f32(BX, BY, NZ)
-    brick = VMEM((4, XE, YE, 128), jnp.float32)
-    next_free, last_free = pl.pallas_call(
-        air_kernel,
-        out_shape=(air, air),
-        in_specs=[HBM, HBM] + [WHOLE] * 6,
-        out_specs=(HBM, HBM),
-        scratch_shapes=[brick, brick, sems(16)],
-        compiler_params=granted(8),
-        cost_estimate=pl.CostEstimate(flops=40_000_000, bytes_accessed=8_000_000, transcendentals=0),
-        name="air_free",
-    )(air_now, air_prev, xlow, xhigh, ylow, yhigh, clow, chigh)
     members, jumps, to_low, to_high = pl.pallas_call(
         unfold_kernel,
         out_shape=(f32(48, COLS), f32(112, WINDOW), stripe, stripe),
@@ -597,6 +566,28 @@
     )(blocks)
     hlow = lax.ppermute(to_high, "gx", ring(GX, 1))
     hhigh = lax.ppermute(to_low, "gx", ring(GX, -1))
+    to_ylow, to_yhigh = pl.pallas_call(
+        sides_kernel,
+        out_shape=(halo_y, halo_y),
+        in_specs=[WHOLE] * 4,
+        out_specs=(WHOLE,) * 2,
+        compiler_params=granted(8),
+        name="sides",
+    )(air_now, air_prev, xlow, xhigh)
+    ylow = lax.ppermute(to_yhigh, "gy", ring(GY, 1))
+    yhigh = lax.ppermute(to_ylow, "gy", ring(GY, -1))
+    air = f32(BX, BY, NZ)
+    brick = VMEM((4, XE, YE, 128), jnp.float32)
+    next_free, last_free = pl.pallas_call(
+        air_kernel,
+        out_shape=(air, air),
+        in_specs=[HBM, HBM] + [WHOLE] * 4,
+        out_specs=(HBM, HBM),
+        scratch_shapes=[brick, brick, sems(16)],
+        compiler_params=granted(8),
+        cost_estimate=pl.CostEstimate(flops=40_000_000, bytes_accessed=8_000_000, transcendentals=0),
+        name="air_free",
+    )(air_now, air_prev, xlow, xhigh, ylow, yhigh)
     listed = air_row.reshape(1, COLS)
     sums, *saved = pl.pallas_call(
         membrane_kernel,

time: 67.6 us -> 61.9 us (0.916)
  starting transfers between devices: 34.8 us -> 26.7 us
  local copies, waits for them, and re-layouts: 0.01 us -> 3.02 us
    all_to_all x1, waiting for transfers between devices: 9.28 us -> 0.01 us  [per_device(): blocks = lax.all_to_all(block, 'gy', 0, 0)]
    ppermute x1, waiting for transfers between devices: 0.01 us -> 5.74 us  [per_device(): xlow = lax.ppermute(to_xhigh, 'gx', ring(GX, 1))]
    ppermute x2 -> x0, starting transfers between devices: 4.86 us -> none  [the longest x1 3.7 us: per_device(): chigh = lax.ppermute(to_clow, 'gy', ring(GY, -1))]
    ppermute x1, starting transfers between devices: 7.34 us -> 4.14 us  [per_device(): hlow = lax.ppermute(to_high, 'gx', ring(GX, 1))]
    unnamed x6 -> x12, local copies, waits for them, and re-layouts: 0.01 us -> 3.02 us
    ppermute x1, waiting for transfers between devices: 0.01 us -> 2.67 us  [per_device(): xhigh = lax.ppermute(to_xlow, 'gx', ring(GX, -1))]
    ppermute x1, waiting for transfers between devices: 0.01 us -> 1.94 us  [per_device(): hlow = lax.ppermute(to_high, 'gx', ring(GX, 1))]
    ppermute x1, waiting for transfers between devices: 4.39 us -> 2.84 us  [per_device(): hhigh = lax.ppermute(to_low, 'gx', ring(GX, -1))]
  transfers between devices with their start and end apart: 13 -> 11, of which waited for: 3 -> 5; matrix products, arithmetic and copies ran while one was open for 0% -> 0% of each run, Pallas kernels for 17% -> 18%
where the time goes in v4:
time: 61.9 us; the launch traced here: 61.2 us
  starting transfers between devices  26.7 us (43%)
  Pallas kernels  16.5 us (27%)
  waiting for transfers between devices  14.3 us (23%)
  local copies, waits for them, and re-layouts  3.02 us (5%)
  between operations  0.73 us (1%)
    all_to_all x1, starting transfers between devices, per_device(): blocks = lax.all_to_all(block, 'gy', 0, 0)  12.2 us
    pallas_call x1, Pallas kernels, per_device(): pl.pallas_call(air_kernel, out_shape=(air, air), in_specs=[HBM, HBM] + [W...  7.29 us
    ppermute x1, waiting for transfers between devices, per_device(): xlow = lax.ppermute(to_xhigh, 'gx', ring(GX, 1))  5.74 us
    ppermute x1, starting transfers between devices, per_device(): hlow = lax.ppermute(to_high, 'gx', ring(GX, 1))  4.14 us
    ppermute x1, starting transfers between devices, per_device(): yhigh = lax.ppermute(to_ylow, 'gy', ring(GY, -1))  3.42 us
    ppermute x3, starting transfers between devices, per_device(): lax.ppermute(sums, 'gx', across(GX, by))  3.31 us
    pallas_call x1, Pallas kernels, per_device(): pl.pallas_call(pack_kernel, out_shape=(halo_x, halo_x, f32(GY, FOLD, 128)...  3.09 us
    unnamed x12, local copies, waits for them, and re-layouts  3.02 us
  transfers between devices with their start and end apart: 11, of which 5 were waited for; matrix products, arithmetic and copies ran while one was open for 0% of the time, Pallas kernels for 18%

profile of v4, /device:TPU:1, one launch (start us, length us, event | category | flops | bytes accessed | tf_op | source)
XLA Modules:
  0.0 61.2 jit_solution(9066557828527693352)
XLA Ops:
  0.6 3.1 %pack.1 = (f32[7,32,512]{2,1,0:T(8,128)}, f32[7,32,512]{2,1,0:T(8,128)}, f32[32,40,128]{2,1,0:T(8,128)}) custom-call(f32[16,32,512]{2,1,0:T(8,128)} %p.5, f32[16,32,512]{2,1,0:T(8,128)} %q.5, f32[16,32]{1,0:T(8,128)} %u.1, f32[16,32]{1,0:T(8,128)} %w.1, f32[16,32]{1,0:T(8,128)} %m.1), custom_call_target="tpu_custom_call" | custom-call | tf_op jit(solution)/shard_map/pack/pallas_call | solution.py:539
  3.7 0.0 copy-start
  3.7 12.2 %all-to-all-start = ((f32[32,40,128]{2,1,0:T(8,128)}), f32[32,40,128]{2,1,0:T(8,128)S(1)}, u32[]{:S(2)}, u32[]{:S(2)}) async-start(f32[32,40,128]{2,1,0:T(8,128)} %get-tuple-element.23), calls=%async_computation | async-start | bytes 1310720 | tf_op jit(solution)/shard_map/all_to_all | solution.py:556
  15.9 2.1 %collective-permute-start.6 = (f32[7,32,512]{2,1,0:T(8,128)}, f32[7,32,512]{2,1,0:T(8,128)S(1)}, u32[]{:S(2)}, u32[]{:S(2)}) collective-permute-start(f32[7,32,512]{2,1,0:T(8,128)} %get-tuple-element.36), channel_id=1, source_target_pairs={{0,32},{32,64},{64,96},{96,128},{128,160},{160,192},{192,224},{224... | collective-permute-start | bytes 1376264 | tf_op jit(solution)/shard_map/ppermute | solution.py:557
  18.0 0.0 collective-permute-start.7
  18.0 5.7 %collective-permute-done.6.xlow = f32[7,32,512]{2,1,0:T(8,128)S(1)} collective-permute-done((f32[7,32,512]{2,1,0:T(8,128)}, f32[7,32,512]{2,1,0:T(8,128)S(1)}, u32[]{:S(2)}, u32[]{:S(2)}) %collective-permute-start.6) | collective-permute-done | bytes 458784 | tf_op jit(solution)/shard_map/ppermute | solution.py:557
  23.7 2.7 %collective-permute-done.7.xhigh = f32[7,32,512]{2,1,0:T(8,128)S(1)} collective-permute-done((f32[7,32,512]{2,1,0:T(8,128)}, f32[7,32,512]{2,1,0:T(8,128)S(1)}, u32[]{:S(2)}, u32[]{:S(2)}) %collective-permute-start.7) | collective-permute-done | bytes 458784 | tf_op jit(solution)/shard_map/ppermute | solution.py:558
  26.4 0.0 copy-done
  26.4 0.0 copy-start.1
  26.4 1.2 %copy-done.1 = f32[16,32,512]{2,1,0:T(8,128)S(1)} copy-done((f32[16,32,512]{2,1,0:T(8,128)S(1)}, f32[16,32,512]{2,1,0:T(8,128)}, u32[]{:S(2)}) %copy-start.1) | copy-done | bytes 1048600
  27.6 0.0 copy-start.5
  27.6 1.0 %sides.1 = (f32[24,8,512]{2,1,0:T(8,128)}, f32[24,8,512]{2,1,0:T(8,128)}) custom-call(f32[16,32,512]{2,1,0:T(8,128)S(1)} %copy-done, f32[16,32,512]{2,1,0:T(8,128)S(1)} %copy-done.1, f32[7,32,512]{2,1,0:T(8,128)S(1)} %collective-permute-done.6.xlow, f32[7,32,512]{2,1,0:T(8,128)S(1)} %collective-permute-done.7.xhigh), custom_call_target="tpu_custom_call" | custom-call | tf_op jit(solution)/shard_map/sides/pallas_call | solution.py:569
  28.6 0.0 copy-start.3
  28.6 0.8 %copy-done.3 = f32[7,32,512]{2,1,0:T(8,128)} copy-done((f32[7,32,512]{2,1,0:T(8,128)}, f32[7,32,512]{2,1,0:T(8,128)S(1)}, u32[]{:S(2)}) %copy-start.3) | copy-done | bytes 458776
  29.4 0.0 copy-start.2
  29.4 1.5 %collective-permute-start.8 = (f32[24,8,512]{2,1,0:T(8,128)}, f32[24,8,512]{2,1,0:T(8,128)}, u32[]{:S(2)}, u32[]{:S(2)}) collective-permute-start(f32[24,8,512]{2,1,0:T(8,128)} %get-tuple-element.38), channel_id=1, source_target_pairs={{0,1},{1,2},{2,3},{3,4},{4,5},{5,6},{6,7},{7,8},{8,9},{9,10},{10,1... | collective-permute-start | bytes 1179656 | tf_op jit(solution)/shard_map/ppermute | solution.py:577
  30.9 3.4 %collective-permute-start.9 = (f32[24,8,512]{2,1,0:T(8,128)}, f32[24,8,512]{2,1,0:T(8,128)}, u32[]{:S(2)}, u32[]{:S(2)}) collective-permute-start(f32[24,8,512]{2,1,0:T(8,128)} %get-tuple-element.39), channel_id=1, source_target_pairs={{0,31},{1,0},{2,1},{3,2},{4,3},{5,4},{6,5},{7,6},{8,7},{9,8},{10,9... | collective-permute-start | bytes 1179656 | tf_op jit(solution)/shard_map/ppermute | solution.py:578
  34.3 0.0 all-to-all-done.blocks
  34.3 0.2 unfold.1
  34.5 4.1 %collective-permute-start = (f32[28,1024]{1,0:T(8,128)S(1)}, f32[28,1024]{1,0:T(8,128)S(1)}, u32[]{:S(2)}, u32[]{:S(2)}) collective-permute-start(f32[28,1024]{1,0:T(8,128)S(1)} %get-tuple-element.26), channel_id=1, source_target_pairs={{0,32},{32,64},{64,96},{96,128},{128,160},{160,192},{192,224},{224... | collective-permute-start | bytes 344072 | tf_op jit(solution)/shard_map/ppermute | solution.py:567
  38.6 0.0 collective-permute-start.1
  38.6 1.9 %collective-permute-done.hlow = f32[28,1024]{1,0:T(8,128)S(1)} collective-permute-done((f32[28,1024]{1,0:T(8,128)S(1)}, f32[28,1024]{1,0:T(8,128)S(1)}, u32[]{:S(2)}, u32[]{:S(2)}) %collective-permute-start) | collective-permute-done | bytes 114720 | tf_op jit(solution)/shard_map/ppermute | solution.py:567
  40.6 2.8 %collective-permute-done.1.hhigh = f32[28,1024]{1,0:T(8,128)S(1)} collective-permute-done((f32[28,1024]{1,0:T(8,128)S(1)}, f32[28,1024]{1,0:T(8,128)S(1)}, u32[]{:S(2)}, u32[]{:S(2)}) %collective-permute-start.1) | collective-permute-done | bytes 114720 | tf_op jit(solution)/shard_map/ppermute | solution.py:568
  43.4 0.0 copy-done.5
  43.4 2.7 %membrane.1 = (f32[1,128]{1,0:T(1,128)S(1)}, f32[48,1024]{1,0:T(8,128)S(1)}, f32[48,1024]{1,0:T(8,128)S(1)}, f32[96,1024]{1,0:T(8,128)S(1)}, f32[96,1024]{1,0:T(...) custom-call(f32[48,1024]{1,0:T(8,128)S(1)} %get-tuple-element.24.members, ...), custom_call_target="tpu_custom_call" | custom-call | tf_op jit(solution)/shard_map/membrane/pallas_call | solution.py:592
  46.1 0.1 collective-permute-start.2
  46.2 1.1 %collective-permute-done.2 = f32[1,128]{1,0:T(1,128)S(1)} collective-permute-done((f32[1,128]{1,0:T(1,128)S(1)}, f32[1,128]{1,0:T(1,128)S(1)}, u32[]{:S(2)}, u32[]{:S(2)}) %collective-permute-start.2) | collective-permute-done | bytes 544 | tf_op jit(solution)/shard_map/ppermute | solution.py:609
  47.3 2.7 %collective-permute-start.5 = (f32[1,128]{1,0:T(1,128)S(1)}, f32[1,128]{1,0:T(1,128)S(1)}, u32[]{:S(2)}, u32[]{:S(2)}) collective-permute-start(f32[1,128]{1,0:T(1,128)S(1)} %add.3.share0), channel_id=1, source_target_pairs={{0,192},{32,224},{64,0},{96,32},{128,64},{160,96},{192,128},{224,1... | collective-permute-start | bytes 1544 | tf_op jit(solution)/shard_map/ppermute | solution.py:610
  50.0 0.3 collective-permute-start.4
  50.3 0.3 collective-permute-start.3
  50.6 0.0 collective-permute-done.8.ylow
  50.6 0.0 collective-permute-done.9.yhigh
  50.6 0.0 copy-done.2
  50.6 0.0 copy-start.4
  50.6 1.0 %copy-done.4 = f32[7,32,512]{2,1,0:T(8,128)S(1)} copy-done((f32[7,32,512]{2,1,0:T(8,128)S(1)}, f32[7,32,512]{2,1,0:T(8,128)}, u32[]{:S(2)}) %copy-start.4) | copy-done | bytes 458776
  51.6 7.3 %air_free.1 = (f32[16,32,512]{2,1,0:T(8,128)}, f32[16,32,512]{2,1,0:T(8,128)}) custom-call(f32[16,32,512]{2,1,0:T(8,128)S(1)} %copy-done, f32[16,32,512]{2,1,0:T(8,128)S(1)} %copy-done.2, f32[7,32,512]{2,1,0:T(8,128)S(1)} %collective-permute-done.6.xlow, f32[7,32,512]{2,1,0:T(8,128)S(1)} %copy-done.4, f32[24,8,512]{2,1,0:T(8,128)} %collective-permute-done.8.ylow, ...), custom_call_target="tpu_custom_call" | custom-call | flops 40000000 | bytes 8000000 | tf_op jit(solution)/shard_map/air_free/pallas_call | solution.py:581
  58.9 0.0 collective-permute-done.5.share3
  58.9 0.0 collective-permute-done.4.share2
  58.9 0.0 collective-permute-done.3.share1
  59.0 2.3 %finish.1 = (f32[16,32,512]{2,1,0:T(8,128)}, f32[16,32,512]{2,1,0:T(8,128)}, f32[16,32]{1,0:T(8,128)}, f32[16,32]{1,0:T(8,128)}) custom-call(f32[1,128]{1,0:T(1,128)S(1)} %add.3.share0, f32[1,128]{1,0:T(1,128)S(1)} %collective-permute-done.3.share1, f32[1,128]{1,0:T(1,128)S(1)} %collective-permute-done.4.share2, ...), custom_call_target="tpu_custom_call", output_to_operand_aliasing={{0}: (12, {}), {1}: (13, {})} | custom-call | tf_op jit(solution)/shard_map/finish/pallas_call | solution.py:611
  (1 shorter events, 0.0 us)
Async XLA Ops:
  3.7 22.7 %copy-start = (f32[16,32,512]{2,1,0:T(8,128)S(1)}, f32[16,32,512]{2,1,0:T(8,128)}, u32[]{:S(2)}) copy-start(f32[16,32,512]{2,1,0:T(8,128)} %p.5) | copy-start | bytes 3145732
  3.7 30.6 %all-to-all-start = ((f32[32,40,128]{2,1,0:T(8,128)}), f32[32,40,128]{2,1,0:T(8,128)S(1)}, u32[]{:S(2)}, u32[]{:S(2)}) async-start(f32[32,40,128]{2,1,0:T(8,128)} %get-tuple-element.23), calls=%async_computation | async-start | bytes 1310720 | tf_op jit(solution)/shard_map/all_to_all | solution.py:556
  15.9 7.8 %collective-permute-start.6 = (f32[7,32,512]{2,1,0:T(8,128)}, f32[7,32,512]{2,1,0:T(8,128)S(1)}, u32[]{:S(2)}, u32[]{:S(2)}) collective-permute-start(f32[7,32,512]{2,1,0:T(8,128)} %get-tuple-element.36), channel_id=1, source_target_pairs={{0,32},{32,64},{64,96},{96,128},{128,160},{160,192},{192,224},{224... | collective-permute-start | bytes 1376264 | tf_op jit(solution)/shard_map/ppermute | solution.py:557
  18.0 8.4 %collective-permute-start.7 = (f32[7,32,512]{2,1,0:T(8,128)}, f32[7,32,512]{2,1,0:T(8,128)S(1)}, u32[]{:S(2)}, u32[]{:S(2)}) collective-permute-start(f32[7,32,512]{2,1,0:T(8,128)} %get-tuple-element.37), channel_id=1, source_target_pairs={{0,224},{32,0},{64,32},{96,64},{128,96},{160,128},{192,160},{224,1... | collective-permute-start | bytes 1376264 | tf_op jit(solution)/shard_map/ppermute | solution.py:558
  26.4 1.2 %copy-start.1 = (f32[16,32,512]{2,1,0:T(8,128)S(1)}, f32[16,32,512]{2,1,0:T(8,128)}, u32[]{:S(2)}) copy-start(f32[16,32,512]{2,1,0:T(8,128)} %q.5) | copy-start | bytes 3145732
  27.6 15.8 %copy-start.5 = (s32[1024]{0:T(1024)S(1)}, s32[1024]{0:T(1024)}, u32[]{:S(2)}) copy-start(s32[1024]{0:T(1024)} %param.11) | copy-start | bytes 12292
  28.6 0.8 %copy-start.3 = (f32[7,32,512]{2,1,0:T(8,128)}, f32[7,32,512]{2,1,0:T(8,128)S(1)}, u32[]{:S(2)}) copy-start(f32[7,32,512]{2,1,0:T(8,128)S(1)} %collective-permute-done.7.xhigh) | copy-start | bytes 1376260
  29.4 21.2 %copy-start.2 = (f32[16,32,512]{2,1,0:T(8,128)S(1)}, f32[16,32,512]{2,1,0:T(8,128)}, u32[]{:S(2)}) copy-start(f32[16,32,512]{2,1,0:T(8,128)} %q.5) | copy-start | bytes 3145732
  29.4 21.2 %collective-permute-start.8 = (f32[24,8,512]{2,1,0:T(8,128)}, f32[24,8,512]{2,1,0:T(8,128)}, u32[]{:S(2)}, u32[]{:S(2)}) collective-permute-start(f32[24,8,512]{2,1,0:T(8,128)} %get-tuple-element.38), channel_id=1, source_target_pairs={{0,1},{1,2},{2,3},{3,4},{4,5},{5,6},{6,7},{7,8},{8,9},{9,10},{10,1... | collective-permute-start | bytes 1179656 | tf_op jit(solution)/shard_map/ppermute | solution.py:577
  30.9 19.7 %collective-permute-start.9 = (f32[24,8,512]{2,1,0:T(8,128)}, f32[24,8,512]{2,1,0:T(8,128)}, u32[]{:S(2)}, u32[]{:S(2)}) collective-permute-start(f32[24,8,512]{2,1,0:T(8,128)} %get-tuple-element.39), channel_id=1, source_target_pairs={{0,31},{1,0},{2,1},{3,2},{4,3},{5,4},{6,5},{7,6},{8,7},{9,8},{10,9... | collective-permute-start | bytes 1179656 | tf_op jit(solution)/shard_map/ppermute | solution.py:578
  34.5 6.1 %collective-permute-start = (f32[28,1024]{1,0:T(8,128)S(1)}, f32[28,1024]{1,0:T(8,128)S(1)}, u32[]{:S(2)}, u32[]{:S(2)}) collective-permute-start(f32[28,1024]{1,0:T(8,128)S(1)} %get-tuple-element.26), channel_id=1, source_target_pairs={{0,32},{32,64},{64,96},{96,128},{128,160},{160,192},{192,224},{224... | collective-permute-start | bytes 344072 | tf_op jit(solution)/shard_map/ppermute | solution.py:567
  38.6 4.8 %collective-permute-start.1 = (f32[28,1024]{1,0:T(8,128)S(1)}, f32[28,1024]{1,0:T(8,128)S(1)}, u32[]{:S(2)}, u32[]{:S(2)}) collective-permute-start(f32[28,1024]{1,0:T(8,128)S(1)} %get-tuple-element.27), channel_id=1, source_target_pairs={{0,224},{32,0},{64,32},{96,64},{128,96},{160,128},{192,160},{224,1... | collective-permute-start | bytes 344072 | tf_op jit(solution)/shard_map/ppermute | solution.py:568
  46.1 1.2 %collective-permute-start.2 = (f32[1,128]{1,0:T(1,128)S(1)}, f32[1,128]{1,0:T(1,128)S(1)}, u32[]{:S(2)}, u32[]{:S(2)}) collective-permute-start(f32[1,128]{1,0:T(1,128)S(1)} %get-tuple-element.28), channel_id=1, source_target_pairs={{0,32},{32,0},{64,96},{96,64},{128,160},{160,128},{192,224},{224,1... | collective-permute-start | bytes 1544 | tf_op jit(solution)/shard_map/ppermute | solution.py:609
  47.3 11.6 %collective-permute-start.5 = (f32[1,128]{1,0:T(1,128)S(1)}, f32[1,128]{1,0:T(1,128)S(1)}, u32[]{:S(2)}, u32[]{:S(2)}) collective-permute-start(f32[1,128]{1,0:T(1,128)S(1)} %add.3.share0), channel_id=1, source_target_pairs={{0,192},{32,224},{64,0},{96,32},{128,64},{160,96},{192,128},{224,1... | collective-permute-start | bytes 1544 | tf_op jit(solution)/shard_map/ppermute | solution.py:610
  50.0 9.0 %collective-permute-start.4 = (f32[1,128]{1,0:T(1,128)S(1)}, f32[1,128]{1,0:T(1,128)S(1)}, u32[]{:S(2)}, u32[]{:S(2)}) collective-permute-start(f32[1,128]{1,0:T(1,128)S(1)} %add.3.share0), channel_id=1, source_target_pairs={{0,128},{32,160},{64,192},{96,224},{128,0},{160,32},{192,64},{224,... | collective-permute-start | bytes 1544 | tf_op jit(solution)/shard_map/ppermute | solution.py:610
  50.3 8.7 %collective-permute-start.3 = (f32[1,128]{1,0:T(1,128)S(1)}, f32[1,128]{1,0:T(1,128)S(1)}, u32[]{:S(2)}, u32[]{:S(2)}) collective-permute-start(f32[1,128]{1,0:T(1,128)S(1)} %add.3.share0), channel_id=1, source_target_pairs={{0,64},{32,96},{64,128},{96,160},{128,192},{160,224},{192,0},{224,... | collective-permute-start | bytes 1544 | tf_op jit(solution)/shard_map/ppermute | solution.py:610
  50.6 1.0 %copy-start.4 = (f32[7,32,512]{2,1,0:T(8,128)S(1)}, f32[7,32,512]{2,1,0:T(8,128)}, u32[]{:S(2)}) copy-start(f32[7,32,512]{2,1,0:T(8,128)} %copy-done.3) | copy-start | bytes 1376260

commit v5 on v4

--- a/solution.py
+++ b/solution.py
@@ -58,8 +58,8 @@
 
 
 def pack_kernel(
-    p, q, u, w, m, xlow, xhigh, block,
-    tips, copied, planes, members, turned, rows, sems,
+    p, q, u, w, m, xlow, xhigh, ylow, yhigh, block,
+    edges, planes, members, turned, rows, sems,
 ):
     wide = lax.axis_index("gy")
 
@@ -71,12 +71,13 @@
 
     mids = started([(x.at[:, :, MID - 128 : MID + 128], planes.at[i]) for i, x in enumerate((p, q))], 0)
     own = started([(x, members.at[i]) for i, x in enumerate((u, w, m))], 2)
+    ins = started([(x.at[:, at : at + 8], edges.at[i]) for i, (x, at) in enumerate(((p, 0), (q, 0), (p, 24), (q, 24)))], 12)
     ends = started(
         [
-            (p.at[0:4], tips.at[0, 0:4]),
-            (q.at[0:3], tips.at[0, 4:7]),
-            (p.at[12:16], tips.at[1, 0:4]),
-            (q.at[13:16], tips.at[1, 4:7]),
+            (p.at[0:4], xlow.at[0:4]),
+            (q.at[0:3], xlow.at[4:7]),
+            (p.at[12:16], xhigh.at[0:4]),
+            (q.at[13:16], xhigh.at[4:7]),
         ],
         5,
     )
@@ -100,27 +101,36 @@
         rows[16 * i : 16 * i + 16, 0:BY] = members[i]
     folded = fold(rows, wide)
     for i in range(GY):
-        copied[i] = folded
-    sent = started([(copied, block)], 9)
+        block[i] = folded
+    lower = sublanes((8, NZ)) < 4
+    for copy in ins:
+        copy.wait()
+    for r in range(BX):
+        ylow[r] = jnp.where(lower, edges[0, r], pltpu.roll(edges[1, r], 4, 0))
+        yhigh[r] = jnp.where(lower, pltpu.roll(edges[3, r], 4, 0), edges[2, r])
     for copy in ends:
         copy.wait()
-    sent += started([(tips.at[0], xlow), (tips.at[1], xhigh)], 10)
-    for copy in sent:
+
+
+def corner_kernel(xlow, xhigh, own_low, own_high, out_ylow, out_yhigh, corners, sems):
+    copies = [
+        pltpu.make_async_copy(own, out.at[4:20], sems.at[4 + i])
+        for i, (own, out) in enumerate(((own_low, out_ylow), (own_high, out_yhigh)))
+    ]
+    for copy in copies:
+        copy.start()
+    lower = sublanes((8, NZ)) < 4
+    for i in range(4):
+        for at, halo, j in ((0, xlow, 4 + max(i - 1, 0)), (1, xhigh, 4 + min(i, 2))):
+            corners[0, at, i] = jnp.where(lower, halo[i, 0:8], pltpu.roll(halo[j, 0:8], 4, 0))
+            corners[1, at, i] = jnp.where(lower, pltpu.roll(halo[j, 24:32], 4, 0), halo[i, 24:32])
+    for i, out in enumerate((out_ylow, out_yhigh)):
+        for at in range(2):
+            copy = pltpu.make_async_copy(corners.at[i, at], out.at[20 * at : 20 * at + 4], sems.at[2 * i + at])
+            copy.start()
+            copies.append(copy)
+    for copy in copies:
         copy.wait()
-
-
-def sides_kernel(p, q, xlow, xhigh, ylow, yhigh):
-    lower = sublanes((8, NZ)) < 4
-
-    def row(r, pt, qt):
-        ylow[r] = jnp.where(lower, pt[0:8], pltpu.roll(qt[0:8], 4, 0))
-        yhigh[r] = jnp.where(lower, pltpu.roll(qt[24:32], 4, 0), pt[24:32])
-
-    for r in range(BX):
-        row(4 + r, p.at[r], q.at[r])
-    for i in range(4):
-        row(i, xlow.at[i], xlow.at[4 + max(i - 1, 0)])
-        row(20 + i, xhigh.at[i], xhigh.at[4 + min(i, 2)])
 
 
 def unfold_kernel(blocks, members, jumps, to_low, to_high):
@@ -162,36 +172,43 @@
     first, last = tall == 0, tall == GX - 1
     bottom, top = wide == 0, wide == GY - 1
     layers = [slice(128 * k, 128 * (k + 1)) for k in range(4)]
-    copies = []
+    pairs = []
     for k in range(4):
-        copies.append(pltpu.make_async_copy(p.at[:, :, layers[k]], a.at[k, 4:20, 8:40], sems.at[k]))
-        copies.append(pltpu.make_async_copy(q.at[:, :, layers[k]], b.at[k, 4:20, 8:40], sems.at[4 + k]))
+        z = layers[k]
+        pairs += [
+            (p.at[:, :, z], a.at[k, 4:20, 8:40]),
+            (q.at[:, :, z], b.at[k, 4:20, 8:40]),
+            (xlow.at[0:4, :, z], a.at[k, 0:4, 8:40]),
+            (xlow.at[4:7, :, z], b.at[k, 1:4, 8:40]),
+            (xhigh.at[0:4, :, z], a.at[k, 20:24, 8:40]),
+            (xhigh.at[4:7, :, z], b.at[k, 20:23, 8:40]),
+            (ylow.at[:, :, z], a.at[k, :, 0:8]),
+            (yhigh.at[:, :, z], a.at[k, :, 40:48]),
+        ]
+    copies = [pltpu.make_async_copy(x, y, sems.at[i]) for i, (x, y) in enumerate(pairs)]
     for copy in copies:
         copy.start()
-    inner_low, inner_high = edge_free((BY, 128), first), edge_free((BY, 128), last)
-    tile_low, tile_high = edge_free((8, 128), bottom), edge_free((8, 128), top)
-    for k in range(4):
-        for i in range(4):
-            a[k, i, 8:40] = jnp.where(inner_low, xlow[i, :, layers[k]], 0.0)
-            a[k, 20 + i, 8:40] = jnp.where(inner_high, xhigh[i, :, layers[k]], 0.0)
-        for i in range(3):
-            b[k, 1 + i, 8:40] = jnp.where(inner_low, xlow[4 + i, :, layers[k]], 0.0)
-            b[k, 20 + i, 8:40] = jnp.where(inner_high, xhigh[4 + i, :, layers[k]], 0.0)
-        for r in range(XE):
-            lo, hi = ylow[r, :, layers[k]], yhigh[r, :, layers[k]]
-            if r < 4 or r >= 20:
-                free = (inner_low if r < 4 else inner_high)[0:8]
-                lo = jnp.where(free, lo, 0.0)
-                hi = jnp.where(free, hi, 0.0)
-            lo = jnp.where(tile_low, lo, 0.0)
-            hi = jnp.where(tile_high, hi, 0.0)
-            a[k, r, 0:8] = lo
-            a[k, r, 40:48] = hi
-            b[k, r, 0:8] = pltpu.roll(lo, 4, 0)
-            b[k, r, 40:48] = pltpu.roll(hi, 4, 0)
     for copy in copies:
         copy.wait()
 
+    def cleared(edge, ref, at):
+        @pl.when(edge)
+        def _():
+            for k in range(4):
+                ref.at[(k, *at)][...] = jnp.zeros(ref.at[(k, *at)].shape, jnp.float32)
+
+    cleared(first, a, (slice(0, 4),))
+    cleared(first, b, (slice(1, 4),))
+    cleared(last, a, (slice(20, 24),))
+    cleared(last, b, (slice(20, 23),))
+    cleared(bottom, a, (slice(0, XE), slice(0, 8)))
+    cleared(top, a, (slice(0, XE), slice(40, 48)))
+    for k in range(4):
+        for r in range(1, XE - 1):
+            b[k, r, 0:8] = pltpu.roll(a[k, r, 0:8], 4, 0)
+            b[k, r, 40:48] = pltpu.roll(a[k, r, 40:48], 4, 0)
+
+    tile_low, tile_high = edge_free((8, 128), bottom), edge_free((8, 128), top)
     lane = lanes((8, 128))
 
     def advance(now, old, r, tile):
@@ -218,8 +235,14 @@
                 new = jnp.where(tile_high, new, 0.0)
             old[k, r, at : at + 8] = new
 
-    def results(x, out, at):
-        return [pltpu.make_async_copy(x.at[k, 4:20, 8:40], out.at[:, :, layers[k]], sems.at[at + k]) for k in range(4)]
+    sent = []
+
+    def send(x, out, rows, at):
+        for k in range(4):
+            target = out.at[rows, :, layers[k]]
+            copy = pltpu.make_async_copy(x.at[k, rows.start + 4 : rows.stop + 4, 8:40], target, sems.at[at + k])
+            copy.start()
+            sent.append(copy)
 
     for t in range(4):
         now, old = (a, b) if t % 2 == 0 else (b, a)
@@ -235,12 +258,10 @@
                 for r in range(t + 1, 4):
                     row(r)
 
-        def body(i, carry):
-            for r in range(8):
-                row(4 + 8 * i + r)
-            return carry
-
-        lax.fori_loop(0, 2, body, 0)
+        for r in range(4, 20):
+            row(r)
+            if t == 3 and r in (11, 19):
+                send(a, out_next, slice(r - 11, r - 3), 36 + 4 * (r // 19))
         if t < 3:
 
             @pl.when(jnp.logical_not(last))
@@ -249,12 +270,7 @@
                     row(r)
 
         if t == 2:
-            sent = results(b, out_last, 8)
-            for copy in sent:
-                copy.start()
-    sent = sent + results(a, out_next, 12)
-    for copy in sent[4:]:
-        copy.start()
+            send(b, out_last, slice(0, 16), 32)
     for copy in sent:
         copy.wait()
 
@@ -535,22 +551,26 @@
     def sems(n):
         return pltpu.SemaphoreType.DMA((n,))
 
-    halo_x, halo_y, stripe = f32(7, BY, NZ), f32(XE, 8, NZ), f32(28, COLS)
-    to_xlow, to_xhigh, block = pl.pallas_call(
+    halo_x, halo_y, own_y, stripe = f32(7, BY, NZ), f32(XE, 8, NZ), f32(BX, 8, NZ), f32(28, COLS)
+    listed = air_row.reshape(1, COLS)
+    air_now, air_prev, membrane_now, membrane_prev, inv_mass, listed = (
+        pltpu.with_memory_space_constraint(x, pltpu.HBM)
+        for x in (air_now, air_prev, membrane_now, membrane_prev, inv_mass, listed)
+    )
+    to_xlow, to_xhigh, to_ylow, to_yhigh, block = pl.pallas_call(
         pack_kernel,
-        out_shape=(halo_x, halo_x, f32(GY, FOLD, 128)),
+        out_shape=(halo_x, halo_x, own_y, own_y, f32(GY, FOLD, 128)),
         in_specs=[HBM] * 5,
-        out_specs=(HBM,) * 3,
+        out_specs=(WHOLE,) * 5,
         scratch_shapes=[
-            VMEM((2, 7, BY, NZ), jnp.float32),
-            VMEM((GY, FOLD, 128), jnp.float32),
+            VMEM((4, BX, 8, NZ), jnp.float32),
             VMEM((2, BX, BY, 256), jnp.float32),
             VMEM((3, BX, BY), jnp.float32),
             VMEM((2, 128, 128), jnp.float32),
             VMEM((PACK, 128), jnp.float32),
-            sems(12),
+            sems(16),
         ],
-        compiler_params=granted(63),
+        compiler_params=granted(8),
         name="pack",
     )(air_now, air_prev, membrane_now, membrane_prev, inv_mass)
     blocks = lax.all_to_all(block, "gy", 0, 0)
@@ -567,13 +587,14 @@
     hlow = lax.ppermute(to_high, "gx", ring(GX, 1))
     hhigh = lax.ppermute(to_low, "gx", ring(GX, -1))
     to_ylow, to_yhigh = pl.pallas_call(
-        sides_kernel,
+        corner_kernel,
         out_shape=(halo_y, halo_y),
-        in_specs=[WHOLE] * 4,
-        out_specs=(WHOLE,) * 2,
-        compiler_params=granted(8),
-        name="sides",
-    )(air_now, air_prev, xlow, xhigh)
+        in_specs=[WHOLE] * 2 + [ANY] * 2,
+        out_specs=(HBM,) * 2,
+        scratch_shapes=[VMEM((2, 2, 4, 8, NZ), jnp.float32), sems(6)],
+        compiler_params=granted(3),
+        name="corners",
+    )(xlow, xhigh, to_ylow, to_yhigh)
     ylow = lax.ppermute(to_yhigh, "gy", ring(GY, 1))
     yhigh = lax.ppermute(to_ylow, "gy", ring(GY, -1))
     air = f32(BX, BY, NZ)
@@ -581,14 +602,13 @@
     next_free, last_free = pl.pallas_call(
         air_kernel,
         out_shape=(air, air),
-        in_specs=[HBM, HBM] + [WHOLE] * 4,
+        in_specs=[HBM] * 2 + [ANY] * 4,
         out_specs=(HBM, HBM),
-        scratch_shapes=[brick, brick, sems(16)],
+        scratch_shapes=[brick, brick, sems(44)],
         compiler_params=granted(8),
         cost_estimate=pl.CostEstimate(flops=40_000_000, bytes_accessed=8_000_000, transcendentals=0),
         name="air_free",
     )(air_now, air_prev, xlow, xhigh, ylow, yhigh)
-    listed = air_row.reshape(1, COLS)
     sums, *saved = pl.pallas_call(
         membrane_kernel,
         out_shape=(

time: 61.9 us -> 61.3 us (level)
  local copies, waits for them, and re-layouts: 3.02 us -> 0 us
  starting transfers between devices: 26.7 us -> 28.7 us
    unnamed x12 -> x0, local copies, waits for them, and re-layouts: 3.02 us -> none
    ppermute x1, starting transfers between devices: 4.14 us -> 6.09 us  [per_device(): hlow = lax.ppermute(to_high, 'gx', ring(GX, 1))]
    pallas_call x3, Pallas kernels: 11.4 us -> 10.5 us  [the longest x1 7.2 us: per_device(): pl.pallas_call(air_kernel, out_shape=(air, air), in_specs=[HBM] * 2 + [AN...]
  transfers between devices with their start and end apart: 11 -> 11, of which waited for: 5 -> 6; matrix products, arithmetic and copies ran while one was open for 0% -> 0% of each run, Pallas kernels for 18% -> 18%
where the time goes in v5:
time: 61.3 us; the launch traced here: 60.6 us
  starting transfers between devices  28.7 us (47%)
  Pallas kernels  16.7 us (27%)
  waiting for transfers between devices  14.6 us (24%)
  between operations  0.71 us (1%)
    all_to_all x1, starting transfers between devices, per_device(): blocks = lax.all_to_all(block, 'gy', 0, 0)  12 us
    pallas_call x1, Pallas kernels, per_device(): pl.pallas_call(air_kernel, out_shape=(air, air), in_specs=[HBM] * 2 + [AN...  7.2 us
    ppermute x1, starting transfers between devices, per_device(): hlow = lax.ppermute(to_high, 'gx', ring(GX, 1))  6.09 us
    ppermute x1, waiting for transfers between devices, per_device(): xlow = lax.ppermute(to_xhigh, 'gx', ring(GX, 1))  5.42 us
    ppermute x1, starting transfers between devices, per_device(): yhigh = lax.ppermute(to_ylow, 'gy', ring(GY, -1))  3.5 us
    ppermute x3, starting transfers between devices, per_device(): lax.ppermute(sums, 'gx', across(GX, by))  3.27 us
    pallas_call x1, Pallas kernels, per_device(): pl.pallas_call(membrane_kernel, out_shape=(f32(1, 128), f32(48, COLS), f3...  3.12 us
    pallas_call x1, Pallas kernels, per_device(): pl.pallas_call(pack_kernel, out_shape=(halo_x, halo_x, own_y, own_y, f32(...  2.89 us
  transfers between devices with their start and end apart: 11, of which 6 were waited for; matrix products, arithmetic and copies ran while one was open for 0% of the time, Pallas kernels for 18%

profile of v5, /device:TPU:1, one launch (start us, length us, event | category | flops | bytes accessed | tf_op | source)
XLA Modules:
  0.0 60.6 jit_solution(2289513619787868156)
XLA Ops:
  0.6 2.9 %pack.1 = (f32[7,32,512]{2,1,0:T(8,128)S(1)}, f32[7,32,512]{2,1,0:T(8,128)S(1)}, f32[16,8,512]{2,1,0:T(8,128)S(1)}, f32[16,8,512]{2,1,0:T(8,128)S(1)}, f32[32,40,128]{2,1,0:T(8,128)}) custom-call(f32[16,32,512]{2,1,0:T(8,128)} %p.3, f32[16,32,512]{2,1,0:T(8,128)} %q.3, f32[16,32]{1,0:T(8,128)} %u.1, f32[16,32]{1,0:T(8,128)} %w.1, f32[16,32]{1,0:T(8,128)} %m.1), custom_call_target="tpu_custom_call" | custom-call | tf_op jit(solution)/shard_map/pack/pallas_call | solution.py:560
  3.5 12.0 %all-to-all-start = ((f32[32,40,128]{2,1,0:T(8,128)}), f32[32,40,128]{2,1,0:T(8,128)S(1)}, u32[]{:S(2)}, u32[]{:S(2)}) async-start(f32[32,40,128]{2,1,0:T(8,128)} %get-tuple-element.25), calls=%async_computation | async-start | bytes 1310720 | tf_op jit(solution)/shard_map/all_to_all | solution.py:576
  15.6 2.1 %collective-permute-start.6 = (f32[7,32,512]{2,1,0:T(8,128)S(1)}, f32[7,32,512]{2,1,0:T(8,128)S(1)}, u32[]{:S(2)}, u32[]{:S(2)}) collective-permute-start(f32[7,32,512]{2,1,0:T(8,128)S(1)} %get-tuple-element.38), channel_id=1, source_target_pairs={{0,32},{32,64},{64,96},{96,128},{128,160},{160,192},{192,224},{224... | collective-permute-start | bytes 1376264 | tf_op jit(solution)/shard_map/ppermute | solution.py:577
  17.6 0.0 collective-permute-start.7
  17.6 5.4 %collective-permute-done.6.xlow = f32[7,32,512]{2,1,0:T(8,128)S(1)} collective-permute-done((f32[7,32,512]{2,1,0:T(8,128)S(1)}, f32[7,32,512]{2,1,0:T(8,128)S(1)}, u32[]{:S(2)}, u32[]{:S(2)}) %collective-permute-start.6) | collective-permute-done | bytes 458784 | tf_op jit(solution)/shard_map/ppermute | solution.py:577
  23.1 2.8 %collective-permute-done.7.xhigh = f32[7,32,512]{2,1,0:T(8,128)S(1)} collective-permute-done((f32[7,32,512]{2,1,0:T(8,128)S(1)}, f32[7,32,512]{2,1,0:T(8,128)S(1)}, u32[]{:S(2)}, u32[]{:S(2)}) %collective-permute-start.7) | collective-permute-done | bytes 458784 | tf_op jit(solution)/shard_map/ppermute | solution.py:578
  25.8 0.5 corners.1
  26.3 1.6 %collective-permute-start.8 = (f32[24,8,512]{2,1,0:T(8,128)S(1)}, f32[24,8,512]{2,1,0:T(8,128)S(1)}, u32[]{:S(2)}, u32[]{:S(2)}) collective-permute-start(f32[24,8,512]{2,1,0:T(8,128)S(1)} %get-tuple-element.42), channel_id=1, source_target_pairs={{0,1},{1,2},{2,3},{3,4},{4,5},{5,6},{6,7},{7,8},{8,9},{9,10},{10,1... | collective-permute-start | bytes 1179656 | tf_op jit(solution)/shard_map/ppermute | solution.py:598
  27.9 3.5 %collective-permute-start.9 = (f32[24,8,512]{2,1,0:T(8,128)S(1)}, f32[24,8,512]{2,1,0:T(8,128)S(1)}, u32[]{:S(2)}, u32[]{:S(2)}) collective-permute-start(f32[24,8,512]{2,1,0:T(8,128)S(1)} %get-tuple-element.43), channel_id=1, source_target_pairs={{0,31},{1,0},{2,1},{3,2},{4,3},{5,4},{6,5},{7,6},{8,7},{9,8},{10,9... | collective-permute-start | bytes 1179656 | tf_op jit(solution)/shard_map/ppermute | solution.py:599
  31.4 0.6 all-to-all-done.blocks
  32.0 0.2 unfold.1
  32.1 6.1 %collective-permute-start = (f32[28,1024]{1,0:T(8,128)S(1)}, f32[28,1024]{1,0:T(8,128)S(1)}, u32[]{:S(2)}, u32[]{:S(2)}) collective-permute-start(f32[28,1024]{1,0:T(8,128)S(1)} %get-tuple-element.28), channel_id=1, source_target_pairs={{0,32},{32,64},{64,96},{96,128},{128,160},{160,192},{192,224},{224... | collective-permute-start | bytes 344072 | tf_op jit(solution)/shard_map/ppermute | solution.py:587
  38.2 0.0 collective-permute-start.1
  38.2 1.9 %collective-permute-done.hlow = f32[28,1024]{1,0:T(8,128)S(1)} collective-permute-done((f32[28,1024]{1,0:T(8,128)S(1)}, f32[28,1024]{1,0:T(8,128)S(1)}, u32[]{:S(2)}, u32[]{:S(2)}) %collective-permute-start) | collective-permute-done | bytes 114720 | tf_op jit(solution)/shard_map/ppermute | solution.py:587
  40.2 2.7 %collective-permute-done.1.hhigh = f32[28,1024]{1,0:T(8,128)S(1)} collective-permute-done((f32[28,1024]{1,0:T(8,128)S(1)}, f32[28,1024]{1,0:T(8,128)S(1)}, u32[]{:S(2)}, u32[]{:S(2)}) %collective-permute-start.1) | collective-permute-done | bytes 114720 | tf_op jit(solution)/shard_map/ppermute | solution.py:588
  42.9 3.1 %membrane.1 = (f32[1,128]{1,0:T(1,128)S(1)}, f32[48,1024]{1,0:T(8,128)S(1)}, f32[48,1024]{1,0:T(8,128)S(1)}, f32[96,1024]{1,0:T(8,128)S(1)}, f32[96,1024]{1,0:T(...) custom-call(f32[48,1024]{1,0:T(8,128)S(1)} %get-tuple-element.26.members, ...), custom_call_target="tpu_custom_call" | custom-call | tf_op jit(solution)/shard_map/membrane/pallas_call | solution.py:612
  46.0 0.1 collective-permute-start.2
  46.1 1.1 %collective-permute-done.2 = f32[1,128]{1,0:T(1,128)S(1)} collective-permute-done((f32[1,128]{1,0:T(1,128)S(1)}, f32[1,128]{1,0:T(1,128)S(1)}, u32[]{:S(2)}, u32[]{:S(2)}) %collective-permute-start.2) | collective-permute-done | bytes 544 | tf_op jit(solution)/shard_map/ppermute | solution.py:629
  47.3 2.7 %collective-permute-start.5 = (f32[1,128]{1,0:T(1,128)S(1)}, f32[1,128]{1,0:T(1,128)S(1)}, u32[]{:S(2)}, u32[]{:S(2)}) collective-permute-start(f32[1,128]{1,0:T(1,128)S(1)} %add.3.share0), channel_id=1, source_target_pairs={{0,192},{32,224},{64,0},{96,32},{128,64},{160,96},{192,128},{224,1... | collective-permute-start | bytes 1544 | tf_op jit(solution)/shard_map/ppermute | solution.py:630
  49.9 0.3 collective-permute-start.4
  50.3 0.3 collective-permute-start.3
  50.5 0.0 collective-permute-done.8.ylow
  50.5 0.0 collective-permute-done.9.yhigh
  50.5 7.2 %air_free.1 = (f32[16,32,512]{2,1,0:T(8,128)}, f32[16,32,512]{2,1,0:T(8,128)}) custom-call(f32[16,32,512]{2,1,0:T(8,128)} %p.3, f32[16,32,512]{2,1,0:T(8,128)} %q.3, f32[7,32,512]{2,1,0:T(8,128)S(1)} %collective-permute-done.6.xlow, f32[7,32,512]{2,1,0:T(8,128)S(1)} %collective-permute-done.7.xhigh, f32[24,8,512]{2,1,0:T(8,128)S(1)} %collective-permute-done.8.ylow, ...), custom_call_target="tpu_custom_call" | custom-call | flops 40000000 | bytes 8000000 | tf_op jit(solution)/shard_map/air_free/pallas_call | solution.py:602
  57.7 0.0 collective-permute-done.5.share3
  57.8 0.0 collective-permute-done.4.share2
  57.8 0.0 collective-permute-done.3.share1
  57.8 2.8 %finish.1 = (f32[16,32,512]{2,1,0:T(8,128)}, f32[16,32,512]{2,1,0:T(8,128)}, f32[16,32]{1,0:T(8,128)}, f32[16,32]{1,0:T(8,128)}) custom-call(f32[1,128]{1,0:T(1,128)S(1)} %add.3.share0, f32[1,128]{1,0:T(1,128)S(1)} %collective-permute-done.3.share1, f32[1,128]{1,0:T(1,128)S(1)} %collective-permute-done.4.share2, ...), custom_call_target="tpu_custom_call", output_to_operand_aliasing={{0}: (12, {}), {1}: (13, {})} | custom-call | tf_op jit(solution)/shard_map/finish/pallas_call | solution.py:631
  (1 shorter events, 0.0 us)
Async XLA Ops:
  3.5 28.4 %all-to-all-start = ((f32[32,40,128]{2,1,0:T(8,128)}), f32[32,40,128]{2,1,0:T(8,128)S(1)}, u32[]{:S(2)}, u32[]{:S(2)}) async-start(f32[32,40,128]{2,1,0:T(8,128)} %get-tuple-element.25), calls=%async_computation | async-start | bytes 1310720 | tf_op jit(solution)/shard_map/all_to_all | solution.py:576
  15.6 7.5 %collective-permute-start.6 = (f32[7,32,512]{2,1,0:T(8,128)S(1)}, f32[7,32,512]{2,1,0:T(8,128)S(1)}, u32[]{:S(2)}, u32[]{:S(2)}) collective-permute-start(f32[7,32,512]{2,1,0:T(8,128)S(1)} %get-tuple-element.38), channel_id=1, source_target_pairs={{0,32},{32,64},{64,96},{96,128},{128,160},{160,192},{192,224},{224... | collective-permute-start | bytes 1376264 | tf_op jit(solution)/shard_map/ppermute | solution.py:577
  17.6 8.2 %collective-permute-start.7 = (f32[7,32,512]{2,1,0:T(8,128)S(1)}, f32[7,32,512]{2,1,0:T(8,128)S(1)}, u32[]{:S(2)}, u32[]{:S(2)}) collective-permute-start(f32[7,32,512]{2,1,0:T(8,128)S(1)} %get-tuple-element.39), channel_id=1, source_target_pairs={{0,224},{32,0},{64,32},{96,64},{128,96},{160,128},{192,160},{224,1... | collective-permute-start | bytes 1376264 | tf_op jit(solution)/shard_map/ppermute | solution.py:578
  26.3 24.2 %collective-permute-start.8 = (f32[24,8,512]{2,1,0:T(8,128)S(1)}, f32[24,8,512]{2,1,0:T(8,128)S(1)}, u32[]{:S(2)}, u32[]{:S(2)}) collective-permute-start(f32[24,8,512]{2,1,0:T(8,128)S(1)} %get-tuple-element.42), channel_id=1, source_target_pairs={{0,1},{1,2},{2,3},{3,4},{4,5},{5,6},{6,7},{7,8},{8,9},{9,10},{10,1... | collective-permute-start | bytes 1179656 | tf_op jit(solution)/shard_map/ppermute | solution.py:598
  27.9 22.6 %collective-permute-start.9 = (f32[24,8,512]{2,1,0:T(8,128)S(1)}, f32[24,8,512]{2,1,0:T(8,128)S(1)}, u32[]{:S(2)}, u32[]{:S(2)}) collective-permute-start(f32[24,8,512]{2,1,0:T(8,128)S(1)} %get-tuple-element.43), channel_id=1, source_target_pairs={{0,31},{1,0},{2,1},{3,2},{4,3},{5,4},{6,5},{7,6},{8,7},{9,8},{10,9... | collective-permute-start | bytes 1179656 | tf_op jit(solution)/shard_map/ppermute | solution.py:599
  32.1 8.0 %collective-permute-start = (f32[28,1024]{1,0:T(8,128)S(1)}, f32[28,1024]{1,0:T(8,128)S(1)}, u32[]{:S(2)}, u32[]{:S(2)}) collective-permute-start(f32[28,1024]{1,0:T(8,128)S(1)} %get-tuple-element.28), channel_id=1, source_target_pairs={{0,32},{32,64},{64,96},{96,128},{128,160},{160,192},{192,224},{224... | collective-permute-start | bytes 344072 | tf_op jit(solution)/shard_map/ppermute | solution.py:587
  38.2 4.7 %collective-permute-start.1 = (f32[28,1024]{1,0:T(8,128)S(1)}, f32[28,1024]{1,0:T(8,128)S(1)}, u32[]{:S(2)}, u32[]{:S(2)}) collective-permute-start(f32[28,1024]{1,0:T(8,128)S(1)} %get-tuple-element.29), channel_id=1, source_target_pairs={{0,224},{32,0},{64,32},{96,64},{128,96},{160,128},{192,160},{224,1... | collective-permute-start | bytes 344072 | tf_op jit(solution)/shard_map/ppermute | solution.py:588
  46.0 1.2 %collective-permute-start.2 = (f32[1,128]{1,0:T(1,128)S(1)}, f32[1,128]{1,0:T(1,128)S(1)}, u32[]{:S(2)}, u32[]{:S(2)}) collective-permute-start(f32[1,128]{1,0:T(1,128)S(1)} %get-tuple-element.30), channel_id=1, source_target_pairs={{0,32},{32,0},{64,96},{96,64},{128,160},{160,128},{192,224},{224,1... | collective-permute-start | bytes 1544 | tf_op jit(solution)/shard_map/ppermute | solution.py:629
  47.3 10.5 %collective-permute-start.5 = (f32[1,128]{1,0:T(1,128)S(1)}, f32[1,128]{1,0:T(1,128)S(1)}, u32[]{:S(2)}, u32[]{:S(2)}) collective-permute-start(f32[1,128]{1,0:T(1,128)S(1)} %add.3.share0), channel_id=1, source_target_pairs={{0,192},{32,224},{64,0},{96,32},{128,64},{160,96},{192,128},{224,1... | collective-permute-start | bytes 1544 | tf_op jit(solution)/shard_map/ppermute | solution.py:630
  49.9 7.8 %collective-permute-start.4 = (f32[1,128]{1,0:T(1,128)S(1)}, f32[1,128]{1,0:T(1,128)S(1)}, u32[]{:S(2)}, u32[]{:S(2)}) collective-permute-start(f32[1,128]{1,0:T(1,128)S(1)} %add.3.share0), channel_id=1, source_target_pairs={{0,128},{32,160},{64,192},{96,224},{128,0},{160,32},{192,64},{224,... | collective-permute-start | bytes 1544 | tf_op jit(solution)/shard_map/ppermute | solution.py:630
  50.3 7.5 %collective-permute-start.3 = (f32[1,128]{1,0:T(1,128)S(1)}, f32[1,128]{1,0:T(1,128)S(1)}, u32[]{:S(2)}, u32[]{:S(2)}) collective-permute-start(f32[1,128]{1,0:T(1,128)S(1)} %add.3.share0), channel_id=1, source_target_pairs={{0,64},{32,96},{64,128},{96,160},{128,192},{160,224},{192,0},{224,... | collective-permute-start | bytes 1544 | tf_op jit(solution)/shard_map/ppermute | solution.py:630

commit v6 on v5

--- a/solution.py
+++ b/solution.py
@@ -57,33 +57,21 @@
     return pltpu.roll(folded, 32 * lax.rem(wide, 4), 1)
 
 
-def pack_kernel(
-    p, q, u, w, m, xlow, xhigh, ylow, yhigh, block,
-    edges, planes, members, turned, rows, sems,
-):
+def started(pairs, sems):
+    copies = [pltpu.make_async_copy(x, y, sems.at[i]) for i, (x, y) in enumerate(pairs)]
+    for copy in copies:
+        copy.start()
+    return copies
+
+
+def block_kernel(p, q, u, w, m, block, planes, members, turned, rows, sems):
     wide = lax.axis_index("gy")
-
-    def started(pairs, at):
-        copies = [pltpu.make_async_copy(x, y, sems.at[at + i]) for i, (x, y) in enumerate(pairs)]
-        for copy in copies:
-            copy.start()
-        return copies
-
-    mids = started([(x.at[:, :, MID - 128 : MID + 128], planes.at[i]) for i, x in enumerate((p, q))], 0)
-    own = started([(x, members.at[i]) for i, x in enumerate((u, w, m))], 2)
-    ins = started([(x.at[:, at : at + 8], edges.at[i]) for i, (x, at) in enumerate(((p, 0), (q, 0), (p, 24), (q, 24)))], 12)
-    ends = started(
-        [
-            (p.at[0:4], xlow.at[0:4]),
-            (q.at[0:3], xlow.at[4:7]),
-            (p.at[12:16], xhigh.at[0:4]),
-            (q.at[13:16], xhigh.at[4:7]),
-        ],
-        5,
-    )
+    middle = slice(MID - 128, MID + 128)
+    pairs = [(p.at[:, :, middle], planes.at[0]), (q.at[:, :, middle], planes.at[1])]
+    copies = started(pairs + [(x, members.at[i]) for i, x in enumerate((u, w, m))], sems)
     lane = lanes((BY, 128))
     for i in range(2):
-        mids[i].wait()
+        copies[i].wait()
         total = jnp.zeros((BY, 128), jnp.float32)
         for x in range(BX):
             above = pltpu.roll(planes[i, x, :, 128:256], 8 * x, 1)
@@ -97,18 +85,29 @@
             at = 48 + 64 * i + 16 * k
             rows[at : at + 16, :] = turned[i, pl.ds(7 - k, BX, stride=8), :] - turned[i, pl.ds(k, BX, stride=8), :]
     for i in range(3):
-        own[i].wait()
+        copies[2 + i].wait()
         rows[16 * i : 16 * i + 16, 0:BY] = members[i]
     folded = fold(rows, wide)
     for i in range(GY):
         block[i] = folded
+
+
+def pack_kernel(p, q, after, xlow, xhigh, ylow, yhigh, edges, sems):
+    pairs = [(x.at[:, at : at + 8], edges.at[i]) for i, (x, at) in enumerate(((p, 0), (q, 0), (p, 24), (q, 24)))]
+    pairs += [
+        (p.at[0:4], xlow.at[0:4]),
+        (q.at[0:3], xlow.at[4:7]),
+        (p.at[12:16], xhigh.at[0:4]),
+        (q.at[13:16], xhigh.at[4:7]),
+    ]
+    copies = started(pairs, sems)
     lower = sublanes((8, NZ)) < 4
-    for copy in ins:
+    for copy in copies[0:4]:
         copy.wait()
     for r in range(BX):
         ylow[r] = jnp.where(lower, edges[0, r], pltpu.roll(edges[1, r], 4, 0))
         yhigh[r] = jnp.where(lower, pltpu.roll(edges[3, r], 4, 0), edges[2, r])
-    for copy in ends:
+    for copy in copies[4:]:
         copy.wait()
 
 
@@ -319,11 +318,9 @@
 
 
 def membrane_kernel(
-    members, jumps, hlow, hhigh, air_row, sums, start, mono1, mono2, force2, force3, source0, source1, parts, slab, listed, sems
+    members, jumps, hlow, hhigh, air_row, sums, start, mono1, mono2, force2, force3, source0, source1, parts, slab
 ):
     tall = lax.axis_index("gx")
-    loaded = pltpu.make_async_copy(air_row, listed, sems.at[0])
-    loaded.start()
     for i in range(3):
         at = XE * i
         parts[at : at + 4] = jnp.where(edge_free((4, COLS), tall == 0), hlow[4 * i : 4 * i + 4, :], 0.0)
@@ -353,8 +350,7 @@
             step.append(own * newer[k] - older[k] + COURANT * ring)
         older, newer = newer, step
         free.append(newer[0])
-    loaded.wait()
-    chooser = chooser_of(listed)
+    chooser = chooser_of(air_row)
     u0, w0, m0 = parts[0:24], parts[24:48], parts[48:72]
     start[0:24] = u0
     start[24:48] = m0
@@ -432,12 +428,10 @@
 
 def finish_kernel(
     share0, share1, share2, share3, air_row, start, mono1, mono2, force2, force3, source0, source1, next_in, last_in,
-    out_next, out_last, out_u, out_w, plane_next, plane_last, fields, wide_rows, turned, listed, sems,
+    out_next, out_last, out_u, out_w, plane_next, plane_last, fields, wide_rows, turned, sems,
 ):
     wide = lax.axis_index("gy")
     reached = (wide >= FIRST) & (wide <= LAST)
-    loaded = pltpu.make_async_copy(air_row, listed, sems.at[4])
-    loaded.start()
     loads = [
         pltpu.make_async_copy(next_in.at[:, :, MID - 128 : MID + 128], plane_next, sems.at[0]),
         pltpu.make_async_copy(last_in.at[:, :, MID - 128 : MID + 128], plane_last, sems.at[1]),
@@ -466,8 +460,7 @@
             total = total + factors[i] * ref[24 * i : 24 * (i + 1)]
         return total
 
-    loaded.wait()
-    chooser = chooser_of(listed)
+    chooser = chooser_of(air_row)
     m0 = start[24:48]
     drive, stiff = FORCE * m0, SPEED * m0
     u1 = mixed(mono1, four[:2])
@@ -553,26 +546,34 @@
 
     halo_x, halo_y, own_y, stripe = f32(7, BY, NZ), f32(XE, 8, NZ), f32(BX, 8, NZ), f32(28, COLS)
     listed = air_row.reshape(1, COLS)
-    air_now, air_prev, membrane_now, membrane_prev, inv_mass, listed = (
+    air_now, air_prev, membrane_now, membrane_prev, inv_mass = (
         pltpu.with_memory_space_constraint(x, pltpu.HBM)
-        for x in (air_now, air_prev, membrane_now, membrane_prev, inv_mass, listed)
+        for x in (air_now, air_prev, membrane_now, membrane_prev, inv_mass)
     )
-    to_xlow, to_xhigh, to_ylow, to_yhigh, block = pl.pallas_call(
-        pack_kernel,
-        out_shape=(halo_x, halo_x, own_y, own_y, f32(GY, FOLD, 128)),
+    block = pl.pallas_call(
+        block_kernel,
+        out_shape=f32(GY, FOLD, 128),
         in_specs=[HBM] * 5,
-        out_specs=(WHOLE,) * 5,
+        out_specs=WHOLE,
         scratch_shapes=[
-            VMEM((4, BX, 8, NZ), jnp.float32),
             VMEM((2, BX, BY, 256), jnp.float32),
             VMEM((3, BX, BY), jnp.float32),
             VMEM((2, 128, 128), jnp.float32),
             VMEM((PACK, 128), jnp.float32),
-            sems(16),
+            sems(5),
         ],
-        compiler_params=granted(8),
+        compiler_params=granted(6),
+        name="block",
+    )(air_now, air_prev, membrane_now, membrane_prev, inv_mass)
+    to_xlow, to_xhigh, to_ylow, to_yhigh = pl.pallas_call(
+        pack_kernel,
+        out_shape=(halo_x, halo_x, own_y, own_y),
+        in_specs=[HBM] * 2 + [ANY],
+        out_specs=(WHOLE,) * 4,
+        scratch_shapes=[VMEM((4, BX, 8, NZ), jnp.float32), sems(8)],
+        compiler_params=granted(4),
         name="pack",
-    )(air_now, air_prev, membrane_now, membrane_prev, inv_mass)
+    )(air_now, air_prev, block)
     blocks = lax.all_to_all(block, "gy", 0, 0)
     xlow = lax.ppermute(to_xhigh, "gx", ring(GX, 1))
     xhigh = lax.ppermute(to_xlow, "gx", ring(GX, -1))
@@ -615,13 +616,11 @@
             f32(1, 128), f32(48, COLS), f32(48, COLS), f32(96, COLS), f32(96, COLS), f32(24, COLS),
             f32(48, WINDOW), f32(96, WINDOW),
         ),
-        in_specs=[WHOLE] * 4 + [HBM],
+        in_specs=[WHOLE] * 5,
         out_specs=(WHOLE,) * 8,
         scratch_shapes=[
             VMEM((3 * XE, COLS), jnp.float32),
             VMEM((7 * XE, WINDOW), jnp.float32),
-            VMEM((1, COLS), jnp.int32),
-            sems(1),
         ],
         compiler_params=granted(10),
         name="membrane",
@@ -631,7 +630,7 @@
     return pl.pallas_call(
         finish_kernel,
         out_shape=(air, air, f32(BX, BY), f32(BX, BY)),
-        in_specs=[pl.BlockSpec(memory_space=pltpu.SMEM)] * 4 + [HBM] + [WHOLE] * 7 + [HBM, HBM],
+        in_specs=[pl.BlockSpec(memory_space=pltpu.SMEM)] * 4 + [WHOLE] * 8 + [HBM, HBM],
         out_specs=(HBM, HBM, WHOLE, WHOLE),
         scratch_shapes=[
             VMEM((BX, BY, 256), jnp.float32),
@@ -639,8 +638,7 @@
             VMEM((48, COLS), jnp.float32),
             VMEM((XE, WINDOW), jnp.float32),
             VMEM((128, 128), jnp.float32),
-            VMEM((1, COLS), jnp.int32),
-            sems(5),
+            sems(4),
         ],
         input_output_aliases={12: 0, 13: 1},
         compiler_params=granted(8),

time: 61.3 us -> 59.8 us (0.976)
  starting transfers between devices: 28.7 us -> 27.7 us
    pallas_call x1 -> x2, Pallas kernels: 2.89 us -> 4.26 us  [the longest x1 2.72 us: per_device(): pl.pallas_call(block_kernel, out_shape=f32(GY, FOLD, 128), in_specs=[HBM]...]
    ppermute x1, starting transfers between devices: 6.09 us -> 5.14 us  [per_device(): hlow = lax.ppermute(to_high, 'gx', ring(GX, 1))]
    pallas_call x1, Pallas kernels: 2.82 us -> 2.1 us  [per_device(): pl.pallas_call(finish_kernel, out_shape=(air, air, f32(BX, BY), f32(BX, B...]
  transfers between devices with their start and end apart: 11 -> 11, of which waited for: 6 -> 5; matrix products, arithmetic and copies ran while one was open for 0% -> 0% of each run, Pallas kernels for 18% -> 20%
where the time goes in v6:
time: 59.8 us; the launch traced here: 59.2 us
  starting transfers between devices  27.7 us (46%)
  Pallas kernels  16.8 us (28%)
  waiting for transfers between devices  14 us (23%)
  between operations  0.72 us (1%)
    all_to_all x1, starting transfers between devices, per_device(): blocks = lax.all_to_all(block, 'gy', 0, 0)  12 us
    pallas_call x1, Pallas kernels, per_device(): pl.pallas_call(air_kernel, out_shape=(air, air), in_specs=[HBM] * 2 + [AN...  7.2 us
    ppermute x1, waiting for transfers between devices, per_device(): xlow = lax.ppermute(to_xhigh, 'gx', ring(GX, 1))  5.42 us
    ppermute x1, starting transfers between devices, per_device(): hlow = lax.ppermute(to_high, 'gx', ring(GX, 1))  5.14 us
    ppermute x1, starting transfers between devices, per_device(): yhigh = lax.ppermute(to_ylow, 'gy', ring(GY, -1))  3.5 us
    ppermute x3, starting transfers between devices, per_device(): lax.ppermute(sums, 'gx', across(GX, by))  3.31 us
    ppermute x1, waiting for transfers between devices, per_device(): xhigh = lax.ppermute(to_xlow, 'gx', ring(GX, -1))  2.77 us
    ppermute x1, waiting for transfers between devices, per_device(): hhigh = lax.ppermute(to_low, 'gx', ring(GX, -1))  2.74 us
  transfers between devices with their start and end apart: 11, of which 5 were waited for; matrix products, arithmetic and copies ran while one was open for 0% of the time, Pallas kernels for 20%

profile of v6, /device:TPU:1, one launch (start us, length us, event | category | flops | bytes accessed | tf_op | source)
XLA Modules:
  0.0 59.2 jit_solution(18126560975046446464)
XLA Ops:
  0.6 2.7 %block.1.after = f32[32,40,128]{2,1,0:T(8,128)} custom-call(f32[16,32,512]{2,1,0:T(8,128)} %p.5, f32[16,32,512]{2,1,0:T(8,128)} %q.5, f32[16,32]{1,0:T(8,128)} %u.1, f32[16,32]{1,0:T(8,128)} %w.1, f32[16,32]{1,0:T(8,128)} %m.1), custom_call_target="tpu_custom_call" | custom-call | tf_op jit(solution)/shard_map/block/pallas_call | solution.py:553
  3.4 12.0 %all-to-all-start = ((f32[32,40,128]{2,1,0:T(8,128)}), f32[32,40,128]{2,1,0:T(8,128)S(1)}, u32[]{:S(2)}, u32[]{:S(2)}) async-start(f32[32,40,128]{2,1,0:T(8,128)} %block.1.after), calls=%async_computation | async-start | bytes 1310720 | tf_op jit(solution)/shard_map/all_to_all | solution.py:577
  15.4 1.5 %pack.1 = (f32[7,32,512]{2,1,0:T(8,128)S(1)}, f32[7,32,512]{2,1,0:T(8,128)S(1)}, f32[16,8,512]{2,1,0:T(8,128)S(1)}, f32[16,8,512]{2,1,0:T(8,128)S(1)}) custom-call(f32[16,32,512]{2,1,0:T(8,128)} %p.5, f32[16,32,512]{2,1,0:T(8,128)} %q.5, f32[32,40,128]{2,1,0:T(8,128)} %block.1.after), custom_call_target="tpu_custom_call" | custom-call | tf_op jit(solution)/shard_map/pack/pallas_call | solution.py:568
  17.0 2.1 %collective-permute-start.6 = (f32[7,32,512]{2,1,0:T(8,128)S(1)}, f32[7,32,512]{2,1,0:T(8,128)S(1)}, u32[]{:S(2)}, u32[]{:S(2)}) collective-permute-start(f32[7,32,512]{2,1,0:T(8,128)S(1)} %get-tuple-element.36), channel_id=1, source_target_pairs={{0,32},{32,64},{64,96},{96,128},{128,160},{160,192},{192,224},{224... | collective-permute-start | bytes 1376264 | tf_op jit(solution)/shard_map/ppermute | solution.py:578
  19.0 0.0 collective-permute-start.7
  19.0 5.4 %collective-permute-done.6.xlow = f32[7,32,512]{2,1,0:T(8,128)S(1)} collective-permute-done((f32[7,32,512]{2,1,0:T(8,128)S(1)}, f32[7,32,512]{2,1,0:T(8,128)S(1)}, u32[]{:S(2)}, u32[]{:S(2)}) %collective-permute-start.6) | collective-permute-done | bytes 458784 | tf_op jit(solution)/shard_map/ppermute | solution.py:578
  24.4 2.8 %collective-permute-done.7.xhigh = f32[7,32,512]{2,1,0:T(8,128)S(1)} collective-permute-done((f32[7,32,512]{2,1,0:T(8,128)S(1)}, f32[7,32,512]{2,1,0:T(8,128)S(1)}, u32[]{:S(2)}, u32[]{:S(2)}) %collective-permute-start.7) | collective-permute-done | bytes 458784 | tf_op jit(solution)/shard_map/ppermute | solution.py:579
  27.2 0.5 corners.1
  27.7 1.6 %collective-permute-start.8 = (f32[24,8,512]{2,1,0:T(8,128)S(1)}, f32[24,8,512]{2,1,0:T(8,128)S(1)}, u32[]{:S(2)}, u32[]{:S(2)}) collective-permute-start(f32[24,8,512]{2,1,0:T(8,128)S(1)} %get-tuple-element.40), channel_id=1, source_target_pairs={{0,1},{1,2},{2,3},{3,4},{4,5},{5,6},{6,7},{7,8},{8,9},{9,10},{10,1... | collective-permute-start | bytes 1179656 | tf_op jit(solution)/shard_map/ppermute | solution.py:599
  29.3 3.5 %collective-permute-start.9 = (f32[24,8,512]{2,1,0:T(8,128)S(1)}, f32[24,8,512]{2,1,0:T(8,128)S(1)}, u32[]{:S(2)}, u32[]{:S(2)}) collective-permute-start(f32[24,8,512]{2,1,0:T(8,128)S(1)} %get-tuple-element.41), channel_id=1, source_target_pairs={{0,31},{1,0},{2,1},{3,2},{4,3},{5,4},{6,5},{7,6},{8,7},{9,8},{10,9... | collective-permute-start | bytes 1179656 | tf_op jit(solution)/shard_map/ppermute | solution.py:600
  32.8 0.0 all-to-all-done.blocks
  32.8 0.2 unfold.1
  33.0 0.0 copy-start
  33.0 5.1 %collective-permute-start = (f32[28,1024]{1,0:T(8,128)S(1)}, f32[28,1024]{1,0:T(8,128)S(1)}, u32[]{:S(2)}, u32[]{:S(2)}) collective-permute-start(f32[28,1024]{1,0:T(8,128)S(1)} %get-tuple-element.26), channel_id=1, source_target_pairs={{0,32},{32,64},{64,96},{96,128},{128,160},{160,192},{192,224},{224... | collective-permute-start | bytes 344072 | tf_op jit(solution)/shard_map/ppermute | solution.py:588
  38.1 0.0 collective-permute-start.1
  38.1 1.9 %collective-permute-done.hlow = f32[28,1024]{1,0:T(8,128)S(1)} collective-permute-done((f32[28,1024]{1,0:T(8,128)S(1)}, f32[28,1024]{1,0:T(8,128)S(1)}, u32[]{:S(2)}, u32[]{:S(2)}) %collective-permute-start) | collective-permute-done | bytes 114720 | tf_op jit(solution)/shard_map/ppermute | solution.py:588
  40.1 2.7 %collective-permute-done.1.hhigh = f32[28,1024]{1,0:T(8,128)S(1)} collective-permute-done((f32[28,1024]{1,0:T(8,128)S(1)}, f32[28,1024]{1,0:T(8,128)S(1)}, u32[]{:S(2)}, u32[]{:S(2)}) %collective-permute-start.1) | collective-permute-done | bytes 114720 | tf_op jit(solution)/shard_map/ppermute | solution.py:589
  42.8 0.0 copy-done
  42.8 2.6 %membrane.1 = (f32[1,128]{1,0:T(1,128)S(1)}, f32[48,1024]{1,0:T(8,128)S(1)}, f32[48,1024]{1,0:T(8,128)S(1)}, f32[96,1024]{1,0:T(8,128)S(1)}, f32[96,1024]{1,0:T(...) custom-call(f32[48,1024]{1,0:T(8,128)S(1)} %get-tuple-element.24.members, ...), custom_call_target="tpu_custom_call" | custom-call | tf_op jit(solution)/shard_map/membrane/pallas_call | solution.py:613
  45.4 0.0 collective-permute-start.2
  45.4 1.1 %collective-permute-done.2 = f32[1,128]{1,0:T(1,128)S(1)} collective-permute-done((f32[1,128]{1,0:T(1,128)S(1)}, f32[1,128]{1,0:T(1,128)S(1)}, u32[]{:S(2)}, u32[]{:S(2)}) %collective-permute-start.2) | collective-permute-done | bytes 544 | tf_op jit(solution)/shard_map/ppermute | solution.py:628
  46.5 2.7 %collective-permute-start.5 = (f32[1,128]{1,0:T(1,128)S(1)}, f32[1,128]{1,0:T(1,128)S(1)}, u32[]{:S(2)}, u32[]{:S(2)}) collective-permute-start(f32[1,128]{1,0:T(1,128)S(1)} %add.3.share0), channel_id=1, source_target_pairs={{0,192},{32,224},{64,0},{96,32},{128,64},{160,96},{192,128},{224,1... | collective-permute-start | bytes 1544 | tf_op jit(solution)/shard_map/ppermute | solution.py:629
  49.2 0.4 collective-permute-start.4
  49.6 0.3 collective-permute-start.3
  49.9 0.0 collective-permute-done.8.ylow
  49.9 0.0 collective-permute-done.9.yhigh
  49.9 7.2 %air_free.1 = (f32[16,32,512]{2,1,0:T(8,128)}, f32[16,32,512]{2,1,0:T(8,128)}) custom-call(f32[16,32,512]{2,1,0:T(8,128)} %p.5, f32[16,32,512]{2,1,0:T(8,128)} %q.5, f32[7,32,512]{2,1,0:T(8,128)S(1)} %collective-permute-done.6.xlow, f32[7,32,512]{2,1,0:T(8,128)S(1)} %collective-permute-done.7.xhigh, f32[24,8,512]{2,1,0:T(8,128)S(1)} %collective-permute-done.8.ylow, ...), custom_call_target="tpu_custom_call" | custom-call | flops 40000000 | bytes 8000000 | tf_op jit(solution)/shard_map/air_free/pallas_call | solution.py:603
  57.1 0.0 collective-permute-done.5.share3
  57.1 0.0 collective-permute-done.4.share2
  57.1 0.0 collective-permute-done.3.share1
  57.1 2.1 %finish.1 = (f32[16,32,512]{2,1,0:T(8,128)}, f32[16,32,512]{2,1,0:T(8,128)}, f32[16,32]{1,0:T(8,128)}, f32[16,32]{1,0:T(8,128)}) custom-call(f32[1,128]{1,0:T(1,128)S(1)} %add.3.share0, f32[1,128]{1,0:T(1,128)S(1)} %collective-permute-done.3.share1, f32[1,128]{1,0:T(1,128)S(1)} %collective-permute-done.4.share2, ...), custom_call_target="tpu_custom_call", output_to_operand_aliasing={{0}: (12, {}), {1}: (13, {})} | custom-call | tf_op jit(solution)/shard_map/finish/pallas_call | solution.py:630
  (1 shorter events, 0.0 us)
Async XLA Ops:
  3.4 29.4 %all-to-all-start = ((f32[32,40,128]{2,1,0:T(8,128)}), f32[32,40,128]{2,1,0:T(8,128)S(1)}, u32[]{:S(2)}, u32[]{:S(2)}) async-start(f32[32,40,128]{2,1,0:T(8,128)} %block.1.after), calls=%async_computation | async-start | bytes 1310720 | tf_op jit(solution)/shard_map/all_to_all | solution.py:577
  17.0 7.5 %collective-permute-start.6 = (f32[7,32,512]{2,1,0:T(8,128)S(1)}, f32[7,32,512]{2,1,0:T(8,128)S(1)}, u32[]{:S(2)}, u32[]{:S(2)}) collective-permute-start(f32[7,32,512]{2,1,0:T(8,128)S(1)} %get-tuple-element.36), channel_id=1, source_target_pairs={{0,32},{32,64},{64,96},{96,128},{128,160},{160,192},{192,224},{224... | collective-permute-start | bytes 1376264 | tf_op jit(solution)/shard_map/ppermute | solution.py:578
  19.0 8.2 %collective-permute-start.7 = (f32[7,32,512]{2,1,0:T(8,128)S(1)}, f32[7,32,512]{2,1,0:T(8,128)S(1)}, u32[]{:S(2)}, u32[]{:S(2)}) collective-permute-start(f32[7,32,512]{2,1,0:T(8,128)S(1)} %get-tuple-element.37), channel_id=1, source_target_pairs={{0,224},{32,0},{64,32},{96,64},{128,96},{160,128},{192,160},{224,1... | collective-permute-start | bytes 1376264 | tf_op jit(solution)/shard_map/ppermute | solution.py:579
  27.7 22.2 %collective-permute-start.8 = (f32[24,8,512]{2,1,0:T(8,128)S(1)}, f32[24,8,512]{2,1,0:T(8,128)S(1)}, u32[]{:S(2)}, u32[]{:S(2)}) collective-permute-start(f32[24,8,512]{2,1,0:T(8,128)S(1)} %get-tuple-element.40), channel_id=1, source_target_pairs={{0,1},{1,2},{2,3},{3,4},{4,5},{5,6},{6,7},{7,8},{8,9},{9,10},{10,1... | collective-permute-start | bytes 1179656 | tf_op jit(solution)/shard_map/ppermute | solution.py:599
  29.3 20.6 %collective-permute-start.9 = (f32[24,8,512]{2,1,0:T(8,128)S(1)}, f32[24,8,512]{2,1,0:T(8,128)S(1)}, u32[]{:S(2)}, u32[]{:S(2)}) collective-permute-start(f32[24,8,512]{2,1,0:T(8,128)S(1)} %get-tuple-element.41), channel_id=1, source_target_pairs={{0,31},{1,0},{2,1},{3,2},{4,3},{5,4},{6,5},{7,6},{8,7},{9,8},{10,9... | collective-permute-start | bytes 1179656 | tf_op jit(solution)/shard_map/ppermute | solution.py:600
  33.0 9.8 %copy-start = (s32[1024]{0:T(1024)S(1)}, s32[1024]{0:T(1024)}, u32[]{:S(2)}) copy-start(s32[1024]{0:T(1024)} %param.11) | copy-start | bytes 12292
  33.0 7.1 %collective-permute-start = (f32[28,1024]{1,0:T(8,128)S(1)}, f32[28,1024]{1,0:T(8,128)S(1)}, u32[]{:S(2)}, u32[]{:S(2)}) collective-permute-start(f32[28,1024]{1,0:T(8,128)S(1)} %get-tuple-element.26), channel_id=1, source_target_pairs={{0,32},{32,64},{64,96},{96,128},{128,160},{160,192},{192,224},{224... | collective-permute-start | bytes 344072 | tf_op jit(solution)/shard_map/ppermute | solution.py:588
  38.1 4.7 %collective-permute-start.1 = (f32[28,1024]{1,0:T(8,128)S(1)}, f32[28,1024]{1,0:T(8,128)S(1)}, u32[]{:S(2)}, u32[]{:S(2)}) collective-permute-start(f32[28,1024]{1,0:T(8,128)S(1)} %get-tuple-element.27), channel_id=1, source_target_pairs={{0,224},{32,0},{64,32},{96,64},{128,96},{160,128},{192,160},{224,1... | collective-permute-start | bytes 344072 | tf_op jit(solution)/shard_map/ppermute | solution.py:589
  45.4 1.1 %collective-permute-start.2 = (f32[1,128]{1,0:T(1,128)S(1)}, f32[1,128]{1,0:T(1,128)S(1)}, u32[]{:S(2)}, u32[]{:S(2)}) collective-permute-start(f32[1,128]{1,0:T(1,128)S(1)} %get-tuple-element.28), channel_id=1, source_target_pairs={{0,32},{32,0},{64,96},{96,64},{128,160},{160,128},{192,224},{224,1... | collective-permute-start | bytes 1544 | tf_op jit(solution)/shard_map/ppermute | solution.py:628
  46.5 10.5 %collective-permute-start.5 = (f32[1,128]{1,0:T(1,128)S(1)}, f32[1,128]{1,0:T(1,128)S(1)}, u32[]{:S(2)}, u32[]{:S(2)}) collective-permute-start(f32[1,128]{1,0:T(1,128)S(1)} %add.3.share0), channel_id=1, source_target_pairs={{0,192},{32,224},{64,0},{96,32},{128,64},{160,96},{192,128},{224,1... | collective-permute-start | bytes 1544 | tf_op jit(solution)/shard_map/ppermute | solution.py:629
  49.2 7.9 %collective-permute-start.4 = (f32[1,128]{1,0:T(1,128)S(1)}, f32[1,128]{1,0:T(1,128)S(1)}, u32[]{:S(2)}, u32[]{:S(2)}) collective-permute-start(f32[1,128]{1,0:T(1,128)S(1)} %add.3.share0), channel_id=1, source_target_pairs={{0,128},{32,160},{64,192},{96,224},{128,0},{160,32},{192,64},{224,... | collective-permute-start | bytes 1544 | tf_op jit(solution)/shard_map/ppermute | solution.py:629
  49.6 7.5 %collective-permute-start.3 = (f32[1,128]{1,0:T(1,128)S(1)}, f32[1,128]{1,0:T(1,128)S(1)}, u32[]{:S(2)}, u32[]{:S(2)}) collective-permute-start(f32[1,128]{1,0:T(1,128)S(1)} %add.3.share0), channel_id=1, source_target_pairs={{0,64},{32,96},{64,128},{96,160},{128,192},{160,224},{192,0},{224,... | collective-permute-start | bytes 1544 | tf_op jit(solution)/shard_map/ppermute | solution.py:629

commit v7 on v6

--- a/solution.py
+++ b/solution.py
@@ -26,6 +26,7 @@
 FIRST, LAST = 22, 30
 PACK = 160
 FOLD = 40
+STRIPE_ROWS = (4, 3, 3, 3, 3, 3, 3, 2, 2, 2)
 
 VMEM = pltpu.VMEM
 WHOLE = pl.BlockSpec(memory_space=pltpu.VMEM)
@@ -132,6 +133,10 @@
         copy.wait()
 
 
+def stripe_slot(row):
+    return 10 + (row - 10) // 2, 512 * (row % 2)
+
+
 def unfold_kernel(blocks, members, jumps, to_low, to_high):
     quarter = lanes((FOLD, 128)) // 32
     for g in range(4):
@@ -152,17 +157,26 @@
                     jumps[0:32, narrow] = merged[8:40]
             else:
                 jumps[40 * g - 48 : 40 * g - 8, narrow] = merged
-    for out, at in ((to_low, 0), (to_high, 12)):
-        for i in range(3):
-            out[4 * i : 4 * i + 4, :] = members[16 * i + at : 16 * i + at + 4, :]
-        for k in range(4):
-            out[12 + 4 * k : 16 + 4 * k, 0:WINDOW] = jumps[16 * k + at : 16 * k + at + 4, :]
-        for k in range(3):
-            out[12 + 4 * k : 16 + 4 * k, 512 : 512 + WINDOW] = jumps[64 + 16 * k + at : 68 + 16 * k + at, :]
+    for out, end in ((to_low, 0), (to_high, BX)):
+        for i, n in enumerate(STRIPE_ROWS):
+            row, at = sum(STRIPE_ROWS[:i]), 16 * i + (end - n if end else 0)
+            if i < 3:
+                out[row : row + n, :] = members[at : at + n, :]
+            else:
+                for j in range(n):
+                    slot, lane = stripe_slot(row + j)
+                    out[slot : slot + 1, lane : lane + WINDOW] = jumps[at - 48 + j : at - 47 + j, :]
 
 
 def edge_free(shape, edge):
     return jnp.broadcast_to(edge.astype(jnp.int32), shape) == 0
+
+
+def stage_kernel(p, q, after, out_p, out_q, done, sems):
+    copies = started([(p, out_p), (q, out_q)], sems)
+    done[...] = jnp.zeros((8, 128), jnp.float32)
+    for copy in copies:
+        copy.wait()
 
 
 def air_kernel(p, q, xlow, xhigh, ylow, yhigh, out_next, out_last, a, b, sems):
@@ -318,20 +332,30 @@
 
 
 def membrane_kernel(
-    members, jumps, hlow, hhigh, air_row, sums, start, mono1, mono2, force2, force3, source0, source1, parts, slab
+    members, jumps, hlow, hhigh, air_row, after, sums, start, mono1, mono2, force2, force3, source0, source1, parts, slab
 ):
     tall = lax.axis_index("gx")
-    for i in range(3):
-        at = XE * i
-        parts[at : at + 4] = jnp.where(edge_free((4, COLS), tall == 0), hlow[4 * i : 4 * i + 4, :], 0.0)
-        parts[at + 4 : at + 20] = members[16 * i : 16 * i + 16]
-        parts[at + 20 : at + 24] = jnp.where(edge_free((4, COLS), tall == GX - 1), hhigh[4 * i : 4 * i + 4, :], 0.0)
-    for i in range(7):
-        at, row = XE * i, 12 + 4 * (i % 4)
-        narrow = slice(512 * (i // 4), 512 * (i // 4) + WINDOW)
-        slab[at : at + 4] = jnp.where(edge_free((4, WINDOW), tall == 0), hlow[row : row + 4, narrow], 0.0)
-        slab[at + 4 : at + 20] = jumps[16 * i : 16 * i + 16]
-        slab[at + 20 : at + 24] = jnp.where(edge_free((4, WINDOW), tall == GX - 1), hhigh[row : row + 4, narrow], 0.0)
+    first, last = tall == 0, tall == GX - 1
+    for i, n in enumerate(STRIPE_ROWS):
+        row = sum(STRIPE_ROWS[:i])
+        if i < 3:
+            ref, at, own, width = parts, XE * i, members[16 * i : 16 * i + 16], COLS
+        else:
+            ref, at, own, width = slab, XE * (i - 3), jumps[16 * (i - 3) : 16 * (i - 3) + 16], WINDOW
+        ref[at + 4 : at + 20] = own
+        if n < 4:
+            ref[at : at + 4 - n] = jnp.zeros((4 - n, width), jnp.float32)
+            ref[at + 20 + n : at + 24] = jnp.zeros((4 - n, width), jnp.float32)
+        low, high = at + 4 - n, at + 20
+        if i < 3:
+            ref[low : low + n] = jnp.where(edge_free((n, width), first), hlow[row : row + n, :], 0.0)
+            ref[high : high + n] = jnp.where(edge_free((n, width), last), hhigh[row : row + n, :], 0.0)
+        else:
+            for j in range(n):
+                slot, lane = stripe_slot(row + j)
+                here = slice(lane, lane + WINDOW)
+                ref[low + j : low + j + 1] = jnp.where(edge_free((1, width), first), hlow[slot : slot + 1, here], 0.0)
+                ref[high + j : high + j + 1] = jnp.where(edge_free((1, width), last), hhigh[slot : slot + 1, here], 0.0)
     within = inside((XE, WINDOW))
 
     def spread(x):
@@ -544,7 +568,7 @@
     def sems(n):
         return pltpu.SemaphoreType.DMA((n,))
 
-    halo_x, halo_y, own_y, stripe = f32(7, BY, NZ), f32(XE, 8, NZ), f32(BX, 8, NZ), f32(28, COLS)
+    halo_x, halo_y, own_y, stripe = f32(7, BY, NZ), f32(XE, 8, NZ), f32(BX, 8, NZ), f32(19, COLS)
     listed = air_row.reshape(1, COLS)
     air_now, air_prev, membrane_now, membrane_prev, inv_mass = (
         pltpu.with_memory_space_constraint(x, pltpu.HBM)
@@ -599,24 +623,34 @@
     ylow = lax.ppermute(to_yhigh, "gy", ring(GY, 1))
     yhigh = lax.ppermute(to_ylow, "gy", ring(GY, -1))
     air = f32(BX, BY, NZ)
+    *staged, done = pl.pallas_call(
+        stage_kernel,
+        out_shape=(air, air, f32(8, 128)),
+        in_specs=[HBM] * 2 + [ANY],
+        out_specs=(WHOLE,) * 3,
+        scratch_shapes=[sems(2)],
+        compiler_params=granted(3),
+        cost_estimate=pl.CostEstimate(flops=0, bytes_accessed=8_000_000, transcendentals=0),
+        name="stage",
+    )(air_now, air_prev, to_low)
     brick = VMEM((4, XE, YE, 128), jnp.float32)
     next_free, last_free = pl.pallas_call(
         air_kernel,
         out_shape=(air, air),
-        in_specs=[HBM] * 2 + [ANY] * 4,
+        in_specs=[ANY] * 6,
         out_specs=(HBM, HBM),
         scratch_shapes=[brick, brick, sems(44)],
         compiler_params=granted(8),
         cost_estimate=pl.CostEstimate(flops=40_000_000, bytes_accessed=8_000_000, transcendentals=0),
         name="air_free",
-    )(air_now, air_prev, xlow, xhigh, ylow, yhigh)
+    )(*staged, xlow, xhigh, ylow, yhigh)
     sums, *saved = pl.pallas_call(
         membrane_kernel,
         out_shape=(
             f32(1, 128), f32(48, COLS), f32(48, COLS), f32(96, COLS), f32(96, COLS), f32(24, COLS),
             f32(48, WINDOW), f32(96, WINDOW),
         ),
-        in_specs=[WHOLE] * 5,
+        in_specs=[WHOLE] * 5 + [ANY],
         out_specs=(WHOLE,) * 8,
         scratch_shapes=[
             VMEM((3 * XE, COLS), jnp.float32),
@@ -624,7 +658,7 @@
         ],
         compiler_params=granted(10),
         name="membrane",
-    )(members, jumps, hlow, hhigh, listed)
+    )(members, jumps, hlow, hhigh, listed, done)
     sums = sums + lax.ppermute(sums, "gx", across(GX, 0))
     shares = [sums] + [lax.ppermute(sums, "gx", across(GX, by)) for by in (1, 2, 3)]
     return pl.pallas_call(

time: 59.8 us -> 58.8 us (0.983)
  waiting for transfers between devices: 14 us -> 12.1 us
  Pallas kernels: 16.8 us -> 17.5 us
    ppermute x1, waiting for transfers between devices: 1.94 us -> 0.06 us  [per_device(): hlow = lax.ppermute(to_high, 'gx', ring(GX, 1))]
    pallas_call x1 -> x2, Pallas kernels: 7.2 us -> 7.93 us  [the longest x1 6.37 us: per_device(): pl.pallas_call(air_kernel, out_shape=(air, air), in_specs=[ANY] * 6, out_...]
  transfers between devices with their start and end apart: 11 -> 11, of which waited for: 5 -> 5; matrix products, arithmetic and copies ran while one was open for 0% -> 0% of each run, Pallas kernels for 20% -> 22%
where the time goes in v7:
time: 58.8 us; the launch traced here: 58.2 us
  starting transfers between devices  27.7 us (47%)
  Pallas kernels  17.5 us (30%)
  waiting for transfers between devices  12.1 us (21%)
  between operations  0.89 us (2%)
    all_to_all x1, starting transfers between devices, per_device(): blocks = lax.all_to_all(block, 'gy', 0, 0)  12 us
    pallas_call x1, Pallas kernels, per_device(): pl.pallas_call(air_kernel, out_shape=(air, air), in_specs=[ANY] * 6, out_...  6.37 us
    ppermute x1, waiting for transfers between devices, per_device(): xlow = lax.ppermute(to_xhigh, 'gx', ring(GX, 1))  5.42 us
    ppermute x1, starting transfers between devices, per_device(): hlow = lax.ppermute(to_high, 'gx', ring(GX, 1))  5.14 us
    ppermute x1, starting transfers between devices, per_device(): yhigh = lax.ppermute(to_ylow, 'gy', ring(GY, -1))  3.5 us
    ppermute x3, starting transfers between devices, per_device(): lax.ppermute(sums, 'gx', across(GX, by))  3.31 us
    ppermute x1, waiting for transfers between devices, per_device(): xhigh = lax.ppermute(to_xlow, 'gx', ring(GX, -1))  2.77 us
    pallas_call x1, Pallas kernels, per_device(): pl.pallas_call(block_kernel, out_shape=f32(GY, FOLD, 128), in_specs=[HBM]...  2.72 us
  transfers between devices with their start and end apart: 11, of which 5 were waited for; matrix products, arithmetic and copies ran while one was open for 0% of the time, Pallas kernels for 22%

profile of v7, /device:TPU:1, one launch (start us, length us, event | category | flops | bytes accessed | tf_op | source)
XLA Modules:
  0.0 58.2 jit_solution(7771533218924999876)
XLA Ops:
  0.6 2.7 %block.1.after = f32[32,40,128]{2,1,0:T(8,128)} custom-call(f32[16,32,512]{2,1,0:T(8,128)} %p.5, f32[16,32,512]{2,1,0:T(8,128)} %q.5, f32[16,32]{1,0:T(8,128)} %u.1, f32[16,32]{1,0:T(8,128)} %w.1, f32[16,32]{1,0:T(8,128)} %m.1), custom_call_target="tpu_custom_call" | custom-call | tf_op jit(solution)/shard_map/block/pallas_call | solution.py:577
  3.4 12.0 %all-to-all-start = ((f32[32,40,128]{2,1,0:T(8,128)}), f32[32,40,128]{2,1,0:T(8,128)S(1)}, u32[]{:S(2)}, u32[]{:S(2)}) async-start(f32[32,40,128]{2,1,0:T(8,128)} %block.1.after), calls=%async_computation | async-start | bytes 1310720 | tf_op jit(solution)/shard_map/all_to_all | solution.py:601
  15.4 1.5 %pack.1 = (f32[7,32,512]{2,1,0:T(8,128)S(1)}, f32[7,32,512]{2,1,0:T(8,128)S(1)}, f32[16,8,512]{2,1,0:T(8,128)S(1)}, f32[16,8,512]{2,1,0:T(8,128)S(1)}) custom-call(f32[16,32,512]{2,1,0:T(8,128)} %p.5, f32[16,32,512]{2,1,0:T(8,128)} %q.5, f32[32,40,128]{2,1,0:T(8,128)} %block.1.after), custom_call_target="tpu_custom_call" | custom-call | tf_op jit(solution)/shard_map/pack/pallas_call | solution.py:592
  17.0 2.1 %collective-permute-start.6 = (f32[7,32,512]{2,1,0:T(8,128)S(1)}, f32[7,32,512]{2,1,0:T(8,128)S(1)}, u32[]{:S(2)}, u32[]{:S(2)}) collective-permute-start(f32[7,32,512]{2,1,0:T(8,128)S(1)} %get-tuple-element.42), channel_id=1, source_target_pairs={{0,32},{32,64},{64,96},{96,128},{128,160},{160,192},{192,224},{224... | collective-permute-start | bytes 1376264 | tf_op jit(solution)/shard_map/ppermute | solution.py:602
  19.0 0.0 collective-permute-start.7
  19.0 5.4 %collective-permute-done.6.xlow = f32[7,32,512]{2,1,0:T(8,128)S(1)} collective-permute-done((f32[7,32,512]{2,1,0:T(8,128)S(1)}, f32[7,32,512]{2,1,0:T(8,128)S(1)}, u32[]{:S(2)}, u32[]{:S(2)}) %collective-permute-start.6) | collective-permute-done | bytes 458784 | tf_op jit(solution)/shard_map/ppermute | solution.py:602
  24.4 2.8 %collective-permute-done.7.xhigh = f32[7,32,512]{2,1,0:T(8,128)S(1)} collective-permute-done((f32[7,32,512]{2,1,0:T(8,128)S(1)}, f32[7,32,512]{2,1,0:T(8,128)S(1)}, u32[]{:S(2)}, u32[]{:S(2)}) %collective-permute-start.7) | collective-permute-done | bytes 458784 | tf_op jit(solution)/shard_map/ppermute | solution.py:603
  27.2 0.5 corners.1
  27.7 1.6 %collective-permute-start.8 = (f32[24,8,512]{2,1,0:T(8,128)S(1)}, f32[24,8,512]{2,1,0:T(8,128)S(1)}, u32[]{:S(2)}, u32[]{:S(2)}) collective-permute-start(f32[24,8,512]{2,1,0:T(8,128)S(1)} %get-tuple-element.46), channel_id=1, source_target_pairs={{0,1},{1,2},{2,3},{3,4},{4,5},{5,6},{6,7},{7,8},{8,9},{9,10},{10,1... | collective-permute-start | bytes 1179656 | tf_op jit(solution)/shard_map/ppermute | solution.py:623
  29.3 3.5 %collective-permute-start.9 = (f32[24,8,512]{2,1,0:T(8,128)S(1)}, f32[24,8,512]{2,1,0:T(8,128)S(1)}, u32[]{:S(2)}, u32[]{:S(2)}) collective-permute-start(f32[24,8,512]{2,1,0:T(8,128)S(1)} %get-tuple-element.47), channel_id=1, source_target_pairs={{0,31},{1,0},{2,1},{3,2},{4,3},{5,4},{6,5},{7,6},{8,7},{9,8},{10,9... | collective-permute-start | bytes 1179656 | tf_op jit(solution)/shard_map/ppermute | solution.py:624
  32.8 0.0 all-to-all-done.blocks
  32.8 0.1 unfold.1
  32.9 5.1 %collective-permute-start = (f32[19,1024]{1,0:T(8,128)S(1)}, f32[19,1024]{1,0:T(8,128)S(1)}, u32[]{:S(2)}, u32[]{:S(2)}) collective-permute-start(f32[19,1024]{1,0:T(8,128)S(1)} %get-tuple-element.29), channel_id=1, source_target_pairs={{0,32},{32,64},{64,96},{96,128},{128,160},{160,192},{192,224},{224... | collective-permute-start | bytes 233480 | tf_op jit(solution)/shard_map/ppermute | solution.py:612
  38.1 0.0 collective-permute-start.1
  38.1 1.6 %stage.1 = (f32[16,32,512]{2,1,0:T(8,128)S(1)}, f32[16,32,512]{2,1,0:T(8,128)S(1)}, f32[8,128]{1,0:T(8,128)S(1)}) custom-call(f32[16,32,512]{2,1,0:T(8,128)} %p.5, f32[16,32,512]{2,1,0:T(8,128)} %q.5, f32[19,1024]{1,0:T(8,128)S(1)} %get-tuple-element.30.after), custom_call_target="tpu_custom_call" | custom-call | bytes 8000000 | tf_op jit(solution)/shard_map/stage/pallas_call | solution.py:626
  39.6 0.0 copy-start
  39.7 0.1 collective-permute-done.hlow
  39.7 2.7 %collective-permute-done.1.hhigh = f32[19,1024]{1,0:T(8,128)S(1)} collective-permute-done((f32[19,1024]{1,0:T(8,128)S(1)}, f32[19,1024]{1,0:T(8,128)S(1)}, u32[]{:S(2)}, u32[]{:S(2)}) %collective-permute-start.1) | collective-permute-done | bytes 77856 | tf_op jit(solution)/shard_map/ppermute | solution.py:613
  42.4 0.0 copy-done
  42.4 2.6 %membrane.1 = (f32[1,128]{1,0:T(1,128)S(1)}, f32[48,1024]{1,0:T(8,128)S(1)}, f32[48,1024]{1,0:T(8,128)S(1)}, f32[96,1024]{1,0:T(8,128)S(1)}, f32[96,1024]{1,0:T(...) custom-call(f32[48,1024]{1,0:T(8,128)S(1)} %get-tuple-element.27.members, ...), custom_call_target="tpu_custom_call" | custom-call | tf_op jit(solution)/shard_map/membrane/pallas_call | solution.py:647
  45.0 0.0 collective-permute-start.2
  45.1 1.1 %collective-permute-done.2 = f32[1,128]{1,0:T(1,128)S(1)} collective-permute-done((f32[1,128]{1,0:T(1,128)S(1)}, f32[1,128]{1,0:T(1,128)S(1)}, u32[]{:S(2)}, u32[]{:S(2)}) %collective-permute-start.2) | collective-permute-done | bytes 544 | tf_op jit(solution)/shard_map/ppermute | solution.py:662
  46.2 2.7 %collective-permute-start.5 = (f32[1,128]{1,0:T(1,128)S(1)}, f32[1,128]{1,0:T(1,128)S(1)}, u32[]{:S(2)}, u32[]{:S(2)}) collective-permute-start(f32[1,128]{1,0:T(1,128)S(1)} %add.3.share0), channel_id=1, source_target_pairs={{0,192},{32,224},{64,0},{96,32},{128,64},{160,96},{192,128},{224,1... | collective-permute-start | bytes 1544 | tf_op jit(solution)/shard_map/ppermute | solution.py:663
  48.9 0.4 collective-permute-start.4
  49.2 0.3 collective-permute-start.3
  49.5 0.0 collective-permute-done.8.ylow
  49.5 0.0 collective-permute-done.9.yhigh
  49.5 6.4 %air_free.1 = (f32[16,32,512]{2,1,0:T(8,128)}, f32[16,32,512]{2,1,0:T(8,128)}) custom-call(f32[16,32,512]{2,1,0:T(8,128)S(1)} %get-tuple-element.40.p, f32[16,32,512]{2,1,0:T(8,128)S(1)} %get-tuple-element.41.q, f32[7,32,512]{2,1,0:T(8,128)S(1)} %collective-permute-done.6.xlow, f32[7,32,512]{2,1,0:T(8,128)S(1)} %collective-permute-done.7.xhigh, ...), custom_call_target="tpu_custom_call" | custom-call | flops 40000000 | bytes 8000000 | tf_op jit(solution)/shard_map/air_free/pallas_call | solution.py:637
  55.9 0.0 collective-permute-done.5.share3
  55.9 0.0 collective-permute-done.4.share2
  55.9 0.0 collective-permute-done.3.share1
  55.9 2.1 %finish.1 = (f32[16,32,512]{2,1,0:T(8,128)}, f32[16,32,512]{2,1,0:T(8,128)}, f32[16,32]{1,0:T(8,128)}, f32[16,32]{1,0:T(8,128)}) custom-call(f32[1,128]{1,0:T(1,128)S(1)} %add.3.share0, f32[1,128]{1,0:T(1,128)S(1)} %collective-permute-done.3.share1, f32[1,128]{1,0:T(1,128)S(1)} %collective-permute-done.4.share2, ...), custom_call_target="tpu_custom_call", output_to_operand_aliasing={{0}: (12, {}), {1}: (13, {})} | custom-call | tf_op jit(solution)/shard_map/finish/pallas_call | solution.py:664
  (1 shorter events, 0.0 us)
Async XLA Ops:
  3.4 29.4 %all-to-all-start = ((f32[32,40,128]{2,1,0:T(8,128)}), f32[32,40,128]{2,1,0:T(8,128)S(1)}, u32[]{:S(2)}, u32[]{:S(2)}) async-start(f32[32,40,128]{2,1,0:T(8,128)} %block.1.after), calls=%async_computation | async-start | bytes 1310720 | tf_op jit(solution)/shard_map/all_to_all | solution.py:601
  17.0 7.5 %collective-permute-start.6 = (f32[7,32,512]{2,1,0:T(8,128)S(1)}, f32[7,32,512]{2,1,0:T(8,128)S(1)}, u32[]{:S(2)}, u32[]{:S(2)}) collective-permute-start(f32[7,32,512]{2,1,0:T(8,128)S(1)} %get-tuple-element.42), channel_id=1, source_target_pairs={{0,32},{32,64},{64,96},{96,128},{128,160},{160,192},{192,224},{224... | collective-permute-start | bytes 1376264 | tf_op jit(solution)/shard_map/ppermute | solution.py:602
  19.0 8.2 %collective-permute-start.7 = (f32[7,32,512]{2,1,0:T(8,128)S(1)}, f32[7,32,512]{2,1,0:T(8,128)S(1)}, u32[]{:S(2)}, u32[]{:S(2)}) collective-permute-start(f32[7,32,512]{2,1,0:T(8,128)S(1)} %get-tuple-element.43), channel_id=1, source_target_pairs={{0,224},{32,0},{64,32},{96,64},{128,96},{160,128},{192,160},{224,1... | collective-permute-start | bytes 1376264 | tf_op jit(solution)/shard_map/ppermute | solution.py:603
  27.7 21.8 %collective-permute-start.8 = (f32[24,8,512]{2,1,0:T(8,128)S(1)}, f32[24,8,512]{2,1,0:T(8,128)S(1)}, u32[]{:S(2)}, u32[]{:S(2)}) collective-permute-start(f32[24,8,512]{2,1,0:T(8,128)S(1)} %get-tuple-element.46), channel_id=1, source_target_pairs={{0,1},{1,2},{2,3},{3,4},{4,5},{5,6},{6,7},{7,8},{8,9},{9,10},{10,1... | collective-permute-start | bytes 1179656 | tf_op jit(solution)/shard_map/ppermute | solution.py:623
  29.3 20.2 %collective-permute-start.9 = (f32[24,8,512]{2,1,0:T(8,128)S(1)}, f32[24,8,512]{2,1,0:T(8,128)S(1)}, u32[]{:S(2)}, u32[]{:S(2)}) collective-permute-start(f32[24,8,512]{2,1,0:T(8,128)S(1)} %get-tuple-element.47), channel_id=1, source_target_pairs={{0,31},{1,0},{2,1},{3,2},{4,3},{5,4},{6,5},{7,6},{8,7},{9,8},{10,9... | collective-permute-start | bytes 1179656 | tf_op jit(solution)/shard_map/ppermute | solution.py:624
  32.9 6.8 %collective-permute-start = (f32[19,1024]{1,0:T(8,128)S(1)}, f32[19,1024]{1,0:T(8,128)S(1)}, u32[]{:S(2)}, u32[]{:S(2)}) collective-permute-start(f32[19,1024]{1,0:T(8,128)S(1)} %get-tuple-element.29), channel_id=1, source_target_pairs={{0,32},{32,64},{64,96},{96,128},{128,160},{160,192},{192,224},{224... | collective-permute-start | bytes 233480 | tf_op jit(solution)/shard_map/ppermute | solution.py:612
  38.1 4.3 %collective-permute-start.1 = (f32[19,1024]{1,0:T(8,128)S(1)}, f32[19,1024]{1,0:T(8,128)S(1)}, u32[]{:S(2)}, u32[]{:S(2)}) collective-permute-start(f32[19,1024]{1,0:T(8,128)S(1)} %get-tuple-element.30.after), channel_id=1, source_target_pairs={{0,224},{32,0},{64,32},{96,64},{128,96},{160,128},{192,160},{224,1... | collective-permute-start | bytes 233480 | tf_op jit(solution)/shard_map/ppermute | solution.py:613
  39.6 2.8 %copy-start = (s32[1024]{0:T(1024)S(1)}, s32[1024]{0:T(1024)}, u32[]{:S(2)}) copy-start(s32[1024]{0:T(1024)} %param.11) | copy-start | bytes 12292
  45.0 1.1 %collective-permute-start.2 = (f32[1,128]{1,0:T(1,128)S(1)}, f32[1,128]{1,0:T(1,128)S(1)}, u32[]{:S(2)}, u32[]{:S(2)}) collective-permute-start(f32[1,128]{1,0:T(1,128)S(1)} %get-tuple-element.32), channel_id=1, source_target_pairs={{0,32},{32,0},{64,96},{96,64},{128,160},{160,128},{192,224},{224,1... | collective-permute-start | bytes 1544 | tf_op jit(solution)/shard_map/ppermute | solution.py:662
  46.2 9.7 %collective-permute-start.5 = (f32[1,128]{1,0:T(1,128)S(1)}, f32[1,128]{1,0:T(1,128)S(1)}, u32[]{:S(2)}, u32[]{:S(2)}) collective-permute-start(f32[1,128]{1,0:T(1,128)S(1)} %add.3.share0), channel_id=1, source_target_pairs={{0,192},{32,224},{64,0},{96,32},{128,64},{160,96},{192,128},{224,1... | collective-permute-start | bytes 1544 | tf_op jit(solution)/shard_map/ppermute | solution.py:663
  48.9 7.0 %collective-permute-start.4 = (f32[1,128]{1,0:T(1,128)S(1)}, f32[1,128]{1,0:T(1,128)S(1)}, u32[]{:S(2)}, u32[]{:S(2)}) collective-permute-start(f32[1,128]{1,0:T(1,128)S(1)} %add.3.share0), channel_id=1, source_target_pairs={{0,128},{32,160},{64,192},{96,224},{128,0},{160,32},{192,64},{224,... | collective-permute-start | bytes 1544 | tf_op jit(solution)/shard_map/ppermute | solution.py:663
  49.2 6.7 %collective-permute-start.3 = (f32[1,128]{1,0:T(1,128)S(1)}, f32[1,128]{1,0:T(1,128)S(1)}, u32[]{:S(2)}, u32[]{:S(2)}) collective-permute-start(f32[1,128]{1,0:T(1,128)S(1)} %add.3.share0), channel_id=1, source_target_pairs={{0,64},{32,96},{64,128},{96,160},{128,192},{160,224},{192,0},{224,... | collective-permute-start | bytes 1544 | tf_op jit(solution)/shard_map/ppermute | solution.py:663

commit v8 on v7

--- a/solution.py
+++ b/solution.py
@@ -93,23 +93,25 @@
         block[i] = folded
 
 
-def pack_kernel(p, q, after, xlow, xhigh, ylow, yhigh, edges, sems):
-    pairs = [(x.at[:, at : at + 8], edges.at[i]) for i, (x, at) in enumerate(((p, 0), (q, 0), (p, 24), (q, 24)))]
-    pairs += [
+def tips_kernel(p, q, after, xlow, xhigh, sems):
+    pairs = [
         (p.at[0:4], xlow.at[0:4]),
         (q.at[0:3], xlow.at[4:7]),
         (p.at[12:16], xhigh.at[0:4]),
         (q.at[13:16], xhigh.at[4:7]),
     ]
-    copies = started(pairs, sems)
+    for copy in started(pairs, sems):
+        copy.wait()
+
+
+def sides_kernel(p, q, after, ylow, yhigh, edges, sems):
+    pairs = [(x.at[:, at : at + 8], edges.at[i]) for i, (x, at) in enumerate(((p, 0), (q, 0), (p, 24), (q, 24)))]
+    for copy in started(pairs, sems):
+        copy.wait()
     lower = sublanes((8, NZ)) < 4
-    for copy in copies[0:4]:
-        copy.wait()
     for r in range(BX):
         ylow[r] = jnp.where(lower, edges[0, r], pltpu.roll(edges[1, r], 4, 0))
         yhigh[r] = jnp.where(lower, pltpu.roll(edges[3, r], 4, 0), edges[2, r])
-    for copy in copies[4:]:
-        copy.wait()
 
 
 def corner_kernel(xlow, xhigh, own_low, own_high, out_ylow, out_yhigh, corners, sems):
@@ -589,15 +591,25 @@
         compiler_params=granted(6),
         name="block",
     )(air_now, air_prev, membrane_now, membrane_prev, inv_mass)
-    to_xlow, to_xhigh, to_ylow, to_yhigh = pl.pallas_call(
-        pack_kernel,
-        out_shape=(halo_x, halo_x, own_y, own_y),
+    to_xlow, to_xhigh = pl.pallas_call(
+        tips_kernel,
+        out_shape=(halo_x, halo_x),
         in_specs=[HBM] * 2 + [ANY],
-        out_specs=(WHOLE,) * 4,
-        scratch_shapes=[VMEM((4, BX, 8, NZ), jnp.float32), sems(8)],
-        compiler_params=granted(4),
-        name="pack",
+        out_specs=(WHOLE,) * 2,
+        scratch_shapes=[sems(4)],
+        compiler_params=granted(3),
+        name="tips",
     )(air_now, air_prev, block)
+    to_ylow, to_yhigh = pl.pallas_call(
+        sides_kernel,
+        out_shape=(own_y, own_y),
+        in_specs=[HBM] * 2 + [ANY],
+        out_specs=(WHOLE,) * 2,
+        scratch_shapes=[VMEM((4, BX, 8, NZ), jnp.float32), sems(4)],
+        compiler_params=granted(3),
+        cost_estimate=pl.CostEstimate(flops=0, bytes_accessed=8_000_000, transcendentals=0),
+        name="sides",
+    )(air_now, air_prev, to_xlow)
     blocks = lax.all_to_all(block, "gy", 0, 0)
     xlow = lax.ppermute(to_xhigh, "gx", ring(GX, 1))
     xhigh = lax.ppermute(to_xlow, "gx", ring(GX, -1))

time: 58.8 us -> 58.9 us (level)
  waiting for transfers between devices: 12.1 us -> 10.8 us
  Pallas kernels: 17.5 us -> 18.5 us
    ppermute x1, waiting for transfers between devices: 5.42 us -> 4.14 us  [per_device(): xlow = lax.ppermute(to_xhigh, 'gx', ring(GX, 1))]
    pallas_call x1 -> x2, Pallas kernels: 1.54 us -> 2.49 us  [the longest x1 1.28 us: per_device(): pl.pallas_call(sides_kernel, out_shape=(own_y, own_y), in_specs=[HBM] * 2...]
  transfers between devices with their start and end apart: 11 -> 11, of which waited for: 5 -> 5; matrix products, arithmetic and copies ran while one was open for 0% -> 0% of each run, Pallas kernels for 22% -> 23%
where the time goes in v8:
time: 58.9 us; the launch traced here: 58.2 us
  starting transfers between devices  28 us (48%)
  Pallas kernels  18.5 us (31%)
  waiting for transfers between devices  10.8 us (18%)
  between operations  0.9 us (2%)
    all_to_all x1, starting transfers between devices, per_device(): blocks = lax.all_to_all(block, 'gy', 0, 0)  12 us
    pallas_call x1, Pallas kernels, per_device(): pl.pallas_call(air_kernel, out_shape=(air, air), in_specs=[ANY] * 6, out_...  6.37 us
    ppermute x1, starting transfers between devices, per_device(): hlow = lax.ppermute(to_high, 'gx', ring(GX, 1))  5.52 us
    ppermute x1, waiting for transfers between devices, per_device(): xlow = lax.ppermute(to_xhigh, 'gx', ring(GX, 1))  4.14 us
    ppermute x1, starting transfers between devices, per_device(): yhigh = lax.ppermute(to_ylow, 'gy', ring(GY, -1))  3.5 us
    ppermute x3, starting transfers between devices, per_device(): lax.ppermute(sums, 'gx', across(GX, by))  3.26 us
    ppermute x1, waiting for transfers between devices, per_device(): xhigh = lax.ppermute(to_xlow, 'gx', ring(GX, -1))  2.77 us
    pallas_call x1, Pallas kernels, per_device(): pl.pallas_call(block_kernel, out_shape=f32(GY, FOLD, 128), in_specs=[HBM]...  2.72 us
  transfers between devices with their start and end apart: 11, of which 5 were waited for; matrix products, arithmetic and copies ran while one was open for 0% of the time, Pallas kernels for 23%

profile of v8, /device:TPU:1, one launch (start us, length us, event | category | flops | bytes accessed | tf_op | source)
XLA Modules:
  0.0 58.2 jit_solution(16038538918373348763)
XLA Ops:
  0.6 2.7 %block.1.after = f32[32,40,128]{2,1,0:T(8,128)} custom-call(f32[16,32,512]{2,1,0:T(8,128)} %p.7, f32[16,32,512]{2,1,0:T(8,128)} %q.7, f32[16,32]{1,0:T(8,128)} %u.1, f32[16,32]{1,0:T(8,128)} %w.1, f32[16,32]{1,0:T(8,128)} %m.1), custom_call_target="tpu_custom_call" | custom-call | tf_op jit(solution)/shard_map/block/pallas_call | solution.py:579
  3.4 12.0 %all-to-all-start = ((f32[32,40,128]{2,1,0:T(8,128)}), f32[32,40,128]{2,1,0:T(8,128)S(1)}, u32[]{:S(2)}, u32[]{:S(2)}) async-start(f32[32,40,128]{2,1,0:T(8,128)} %block.1.after), calls=%async_computation | async-start | bytes 1310720 | tf_op jit(solution)/shard_map/all_to_all | solution.py:613
  15.4 1.2 %tips.1 = (f32[7,32,512]{2,1,0:T(8,128)S(1)}, f32[7,32,512]{2,1,0:T(8,128)S(1)}) custom-call(f32[16,32,512]{2,1,0:T(8,128)} %p.7, f32[16,32,512]{2,1,0:T(8,128)} %q.7, f32[32,40,128]{2,1,0:T(8,128)} %block.1.after), custom_call_target="tpu_custom_call" | custom-call | tf_op jit(solution)/shard_map/tips/pallas_call | solution.py:594
  16.6 2.1 %collective-permute-start.6 = (f32[7,32,512]{2,1,0:T(8,128)S(1)}, f32[7,32,512]{2,1,0:T(8,128)S(1)}, u32[]{:S(2)}, u32[]{:S(2)}) collective-permute-start(f32[7,32,512]{2,1,0:T(8,128)S(1)} %get-tuple-element.42), channel_id=1, source_target_pairs={{0,32},{32,64},{64,96},{96,128},{128,160},{160,192},{192,224},{224... | collective-permute-start | bytes 1376264 | tf_op jit(solution)/shard_map/ppermute | solution.py:614
  18.7 0.0 collective-permute-start.7
  18.7 1.3 %sides.1 = (f32[16,8,512]{2,1,0:T(8,128)S(1)}, f32[16,8,512]{2,1,0:T(8,128)S(1)}) custom-call(f32[16,32,512]{2,1,0:T(8,128)} %p.7, f32[16,32,512]{2,1,0:T(8,128)} %q.7, f32[7,32,512]{2,1,0:T(8,128)S(1)} %get-tuple-element.43.after), custom_call_target="tpu_custom_call" | custom-call | bytes 8000000 | tf_op jit(solution)/shard_map/sides/pallas_call | solution.py:603
  20.0 4.1 %collective-permute-done.6.xlow = f32[7,32,512]{2,1,0:T(8,128)S(1)} collective-permute-done((f32[7,32,512]{2,1,0:T(8,128)S(1)}, f32[7,32,512]{2,1,0:T(8,128)S(1)}, u32[]{:S(2)}, u32[]{:S(2)}) %collective-permute-start.6) | collective-permute-done | bytes 458784 | tf_op jit(solution)/shard_map/ppermute | solution.py:614
  24.1 2.8 %collective-permute-done.7.xhigh = f32[7,32,512]{2,1,0:T(8,128)S(1)} collective-permute-done((f32[7,32,512]{2,1,0:T(8,128)S(1)}, f32[7,32,512]{2,1,0:T(8,128)S(1)}, u32[]{:S(2)}, u32[]{:S(2)}) %collective-permute-start.7) | collective-permute-done | bytes 458784 | tf_op jit(solution)/shard_map/ppermute | solution.py:615
  26.9 0.5 corners.1
  27.4 1.6 %collective-permute-start.8 = (f32[24,8,512]{2,1,0:T(8,128)S(1)}, f32[24,8,512]{2,1,0:T(8,128)S(1)}, u32[]{:S(2)}, u32[]{:S(2)}) collective-permute-start(f32[24,8,512]{2,1,0:T(8,128)S(1)} %get-tuple-element.46), channel_id=1, source_target_pairs={{0,1},{1,2},{2,3},{3,4},{4,5},{5,6},{6,7},{7,8},{8,9},{9,10},{10,1... | collective-permute-start | bytes 1179656 | tf_op jit(solution)/shard_map/ppermute | solution.py:635
  29.0 3.5 %collective-permute-start.9 = (f32[24,8,512]{2,1,0:T(8,128)S(1)}, f32[24,8,512]{2,1,0:T(8,128)S(1)}, u32[]{:S(2)}, u32[]{:S(2)}) collective-permute-start(f32[24,8,512]{2,1,0:T(8,128)S(1)} %get-tuple-element.47), channel_id=1, source_target_pairs={{0,31},{1,0},{2,1},{3,2},{4,3},{5,4},{6,5},{7,6},{8,7},{9,8},{10,9... | collective-permute-start | bytes 1179656 | tf_op jit(solution)/shard_map/ppermute | solution.py:636
  32.5 0.0 all-to-all-done.blocks
  32.5 0.1 unfold.1
  32.6 5.5 %collective-permute-start = (f32[19,1024]{1,0:T(8,128)S(1)}, f32[19,1024]{1,0:T(8,128)S(1)}, u32[]{:S(2)}, u32[]{:S(2)}) collective-permute-start(f32[19,1024]{1,0:T(8,128)S(1)} %get-tuple-element.29), channel_id=1, source_target_pairs={{0,32},{32,64},{64,96},{96,128},{128,160},{160,192},{192,224},{224... | collective-permute-start | bytes 233480 | tf_op jit(solution)/shard_map/ppermute | solution.py:624
  38.1 0.0 collective-permute-start.1
  38.1 1.6 %stage.1 = (f32[16,32,512]{2,1,0:T(8,128)S(1)}, f32[16,32,512]{2,1,0:T(8,128)S(1)}, f32[8,128]{1,0:T(8,128)S(1)}) custom-call(f32[16,32,512]{2,1,0:T(8,128)} %p.7, f32[16,32,512]{2,1,0:T(8,128)} %q.7, f32[19,1024]{1,0:T(8,128)S(1)} %get-tuple-element.30.after), custom_call_target="tpu_custom_call" | custom-call | bytes 8000000 | tf_op jit(solution)/shard_map/stage/pallas_call | solution.py:638
  39.7 0.0 copy-start
  39.7 0.1 collective-permute-done.hlow
  39.8 2.7 %collective-permute-done.1.hhigh = f32[19,1024]{1,0:T(8,128)S(1)} collective-permute-done((f32[19,1024]{1,0:T(8,128)S(1)}, f32[19,1024]{1,0:T(8,128)S(1)}, u32[]{:S(2)}, u32[]{:S(2)}) %collective-permute-start.1) | collective-permute-done | bytes 77856 | tf_op jit(solution)/shard_map/ppermute | solution.py:625
  42.5 0.0 copy-done
  42.5 2.6 %membrane.1 = (f32[1,128]{1,0:T(1,128)S(1)}, f32[48,1024]{1,0:T(8,128)S(1)}, f32[48,1024]{1,0:T(8,128)S(1)}, f32[96,1024]{1,0:T(8,128)S(1)}, f32[96,1024]{1,0:T(...) custom-call(f32[48,1024]{1,0:T(8,128)S(1)} %get-tuple-element.27.members, ...), custom_call_target="tpu_custom_call" | custom-call | tf_op jit(solution)/shard_map/membrane/pallas_call | solution.py:659
  45.1 0.0 collective-permute-start.2
  45.1 1.1 %collective-permute-done.2 = f32[1,128]{1,0:T(1,128)S(1)} collective-permute-done((f32[1,128]{1,0:T(1,128)S(1)}, f32[1,128]{1,0:T(1,128)S(1)}, u32[]{:S(2)}, u32[]{:S(2)}) %collective-permute-start.2) | collective-permute-done | bytes 544 | tf_op jit(solution)/shard_map/ppermute | solution.py:674
  46.2 2.7 %collective-permute-start.5 = (f32[1,128]{1,0:T(1,128)S(1)}, f32[1,128]{1,0:T(1,128)S(1)}, u32[]{:S(2)}, u32[]{:S(2)}) collective-permute-start(f32[1,128]{1,0:T(1,128)S(1)} %add.3.share0), channel_id=1, source_target_pairs={{0,192},{32,224},{64,0},{96,32},{128,64},{160,96},{192,128},{224,1... | collective-permute-start | bytes 1544 | tf_op jit(solution)/shard_map/ppermute | solution.py:675
  48.9 0.3 collective-permute-start.4
  49.2 0.3 collective-permute-start.3
  49.5 0.0 collective-permute-done.8.ylow
  49.5 0.0 collective-permute-done.9.yhigh
  49.5 6.4 %air_free.1 = (f32[16,32,512]{2,1,0:T(8,128)}, f32[16,32,512]{2,1,0:T(8,128)}) custom-call(f32[16,32,512]{2,1,0:T(8,128)S(1)} %get-tuple-element.40.p, f32[16,32,512]{2,1,0:T(8,128)S(1)} %get-tuple-element.41.q, f32[7,32,512]{2,1,0:T(8,128)S(1)} %collective-permute-done.6.xlow, f32[7,32,512]{2,1,0:T(8,128)S(1)} %collective-permute-done.7.xhigh, ...), custom_call_target="tpu_custom_call" | custom-call | flops 40000000 | bytes 8000000 | tf_op jit(solution)/shard_map/air_free/pallas_call | solution.py:649
  55.9 0.0 collective-permute-done.5.share3
  55.9 0.0 collective-permute-done.4.share2
  55.9 0.0 collective-permute-done.3.share1
  55.9 2.1 %finish.1 = (f32[16,32,512]{2,1,0:T(8,128)}, f32[16,32,512]{2,1,0:T(8,128)}, f32[16,32]{1,0:T(8,128)}, f32[16,32]{1,0:T(8,128)}) custom-call(f32[1,128]{1,0:T(1,128)S(1)} %add.3.share0, f32[1,128]{1,0:T(1,128)S(1)} %collective-permute-done.3.share1, f32[1,128]{1,0:T(1,128)S(1)} %collective-permute-done.4.share2, ...), custom_call_target="tpu_custom_call", output_to_operand_aliasing={{0}: (12, {}), {1}: (13, {})} | custom-call | tf_op jit(solution)/shard_map/finish/pallas_call | solution.py:676
  (1 shorter events, 0.0 us)
Async XLA Ops:
  3.4 29.1 %all-to-all-start = ((f32[32,40,128]{2,1,0:T(8,128)}), f32[32,40,128]{2,1,0:T(8,128)S(1)}, u32[]{:S(2)}, u32[]{:S(2)}) async-start(f32[32,40,128]{2,1,0:T(8,128)} %block.1.after), calls=%async_computation | async-start | bytes 1310720 | tf_op jit(solution)/shard_map/all_to_all | solution.py:613
  16.6 7.5 %collective-permute-start.6 = (f32[7,32,512]{2,1,0:T(8,128)S(1)}, f32[7,32,512]{2,1,0:T(8,128)S(1)}, u32[]{:S(2)}, u32[]{:S(2)}) collective-permute-start(f32[7,32,512]{2,1,0:T(8,128)S(1)} %get-tuple-element.42), channel_id=1, source_target_pairs={{0,32},{32,64},{64,96},{96,128},{128,160},{160,192},{192,224},{224... | collective-permute-start | bytes 1376264 | tf_op jit(solution)/shard_map/ppermute | solution.py:614
  18.7 8.2 %collective-permute-start.7 = (f32[7,32,512]{2,1,0:T(8,128)S(1)}, f32[7,32,512]{2,1,0:T(8,128)S(1)}, u32[]{:S(2)}, u32[]{:S(2)}) collective-permute-start(f32[7,32,512]{2,1,0:T(8,128)S(1)} %get-tuple-element.43.after), channel_id=1, source_target_pairs={{0,224},{32,0},{64,32},{96,64},{128,96},{160,128},{192,160},{224,1... | collective-permute-start | bytes 1376264 | tf_op jit(solution)/shard_map/ppermute | solution.py:615
  27.4 22.1 %collective-permute-start.8 = (f32[24,8,512]{2,1,0:T(8,128)S(1)}, f32[24,8,512]{2,1,0:T(8,128)S(1)}, u32[]{:S(2)}, u32[]{:S(2)}) collective-permute-start(f32[24,8,512]{2,1,0:T(8,128)S(1)} %get-tuple-element.46), channel_id=1, source_target_pairs={{0,1},{1,2},{2,3},{3,4},{4,5},{5,6},{6,7},{7,8},{8,9},{9,10},{10,1... | collective-permute-start | bytes 1179656 | tf_op jit(solution)/shard_map/ppermute | solution.py:635
  29.0 20.5 %collective-permute-start.9 = (f32[24,8,512]{2,1,0:T(8,128)S(1)}, f32[24,8,512]{2,1,0:T(8,128)S(1)}, u32[]{:S(2)}, u32[]{:S(2)}) collective-permute-start(f32[24,8,512]{2,1,0:T(8,128)S(1)} %get-tuple-element.47), channel_id=1, source_target_pairs={{0,31},{1,0},{2,1},{3,2},{4,3},{5,4},{6,5},{7,6},{8,7},{9,8},{10,9... | collective-permute-start | bytes 1179656 | tf_op jit(solution)/shard_map/ppermute | solution.py:636
  32.6 7.2 %collective-permute-start = (f32[19,1024]{1,0:T(8,128)S(1)}, f32[19,1024]{1,0:T(8,128)S(1)}, u32[]{:S(2)}, u32[]{:S(2)}) collective-permute-start(f32[19,1024]{1,0:T(8,128)S(1)} %get-tuple-element.29), channel_id=1, source_target_pairs={{0,32},{32,64},{64,96},{96,128},{128,160},{160,192},{192,224},{224... | collective-permute-start | bytes 233480 | tf_op jit(solution)/shard_map/ppermute | solution.py:624
  38.1 4.3 %collective-permute-start.1 = (f32[19,1024]{1,0:T(8,128)S(1)}, f32[19,1024]{1,0:T(8,128)S(1)}, u32[]{:S(2)}, u32[]{:S(2)}) collective-permute-start(f32[19,1024]{1,0:T(8,128)S(1)} %get-tuple-element.30.after), channel_id=1, source_target_pairs={{0,224},{32,0},{64,32},{96,64},{128,96},{160,128},{192,160},{224,1... | collective-permute-start | bytes 233480 | tf_op jit(solution)/shard_map/ppermute | solution.py:625
  39.7 2.8 %copy-start = (s32[1024]{0:T(1024)S(1)}, s32[1024]{0:T(1024)}, u32[]{:S(2)}) copy-start(s32[1024]{0:T(1024)} %param.11) | copy-start | bytes 12292
  45.1 1.1 %collective-permute-start.2 = (f32[1,128]{1,0:T(1,128)S(1)}, f32[1,128]{1,0:T(1,128)S(1)}, u32[]{:S(2)}, u32[]{:S(2)}) collective-permute-start(f32[1,128]{1,0:T(1,128)S(1)} %get-tuple-element.32), channel_id=1, source_target_pairs={{0,32},{32,0},{64,96},{96,64},{128,160},{160,128},{192,224},{224,1... | collective-permute-start | bytes 1544 | tf_op jit(solution)/shard_map/ppermute | solution.py:674
  46.2 9.7 %collective-permute-start.5 = (f32[1,128]{1,0:T(1,128)S(1)}, f32[1,128]{1,0:T(1,128)S(1)}, u32[]{:S(2)}, u32[]{:S(2)}) collective-permute-start(f32[1,128]{1,0:T(1,128)S(1)} %add.3.share0), channel_id=1, source_target_pairs={{0,192},{32,224},{64,0},{96,32},{128,64},{160,96},{192,128},{224,1... | collective-permute-start | bytes 1544 | tf_op jit(solution)/shard_map/ppermute | solution.py:675
  48.9 7.0 %collective-permute-start.4 = (f32[1,128]{1,0:T(1,128)S(1)}, f32[1,128]{1,0:T(1,128)S(1)}, u32[]{:S(2)}, u32[]{:S(2)}) collective-permute-start(f32[1,128]{1,0:T(1,128)S(1)} %add.3.share0), channel_id=1, source_target_pairs={{0,128},{32,160},{64,192},{96,224},{128,0},{160,32},{192,64},{224,... | collective-permute-start | bytes 1544 | tf_op jit(solution)/shard_map/ppermute | solution.py:675
  49.2 6.7 %collective-permute-start.3 = (f32[1,128]{1,0:T(1,128)S(1)}, f32[1,128]{1,0:T(1,128)S(1)}, u32[]{:S(2)}, u32[]{:S(2)}) collective-permute-start(f32[1,128]{1,0:T(1,128)S(1)} %add.3.share0), channel_id=1, source_target_pairs={{0,64},{32,96},{64,128},{96,160},{128,192},{160,224},{192,0},{224,... | collective-permute-start | bytes 1544 | tf_op jit(solution)/shard_map/ppermute | solution.py:675
